TPU v7x, 32 devices: a whole 2x2x4 slice. The times are simulated.
32 devices in a mesh: rep: 16 (over z, x, core), shard: 2 (over y).
Axes of the slice: x: 2, y: 2, z: 4, core: 2. Of those that a mesh axis runs over, the one named last changes fastest.
Arguments:
- latents: bfloat16 [128, 32, 32, 640], P(('rep', 'shard'))
- cotangent: bfloat16 [128, 32, 32, 640], P(('rep', 'shard')), may hold values from -6 to 6
- gn_gain: float32 [640], replicated, may hold values from 0.1 to 1.9
- gn_bias: float32 [640], replicated, may hold values from -3 to 3
- conv_weight: bfloat16 [5760, 640], P('shard'), may hold values from -0.078125 to 0.078125
- master: float32 [640, 5760], P('rep', 'shard'), may hold values from -6 to 6
- moment_one: float32 [640, 5760], P('rep', 'shard'), may hold values from -6 to 6
- moment_two: float32 [640, 5760], P('rep', 'shard'), may hold values from 0.1 to 10
- departing: int32 [16], replicated, may hold values from 0 to 1, as said below
- partner: int32 [16], replicated, may hold values from 0 to 15, as said below
Outputs:
- conv_out: bfloat16 [128, 32, 32, 640], P(('rep', 'shard'))
- new_master: float32 [16, 2, 40, 5760], P('rep', None, None, 'shard')
- new_first: float32 [16, 2, 40, 5760], P('rep', None, None, 'shard')
- new_second: float32 [16, 2, 40, 5760], P('rep', None, None, 'shard')
Inputs may be any that keep to these rules, and one draw needn't show every extreme that they name: Exactly 8 replicas have departing = 1. partner pairs each departing replica with one staying replica and back: partner[partner[r]] = r and departing[partner[r]] = 1 - departing[r]; at least one replica r has partner[r] = (r + 8) mod 16.
All inputs are finite; a program needn't handle non-finite values.
Results may differ from a plain program's by a relative error of at most 0.007.
Values may be sent and summed in bfloat16 or wider, within the bound.
No kernel may reach another device: no remote copies, remote signals or barrier semaphores. Data moves between devices by JAX's collectives and lax.ppermute only.
A program may use at most 192 MiB of HBM per device.

v0:
```python
import jax
import jax.numpy as jnp
from jax import lax
from jax.sharding import PartitionSpec as P

GROUPS = 32


beta_one = 0.9
beta_two = 0.999
step_count = 100.0
learn_rate = 0.01
weight_decay = 0.01
adam_eps = 1e-08
norm_eps = 1e-05


def gather_taps(padded, row_count, col_count):
    taps = [
        padded[:, row_off : row_off + row_count, col_off : col_off + col_count, :]
        for row_off in range(3)
        for col_off in range(3)
    ]
    return jnp.concatenate(taps, axis=3)


def adam(master, first_moment, second_moment, gradient):
    first_moment = beta_one * first_moment + (1.0 - beta_one) * gradient
    second_moment = beta_two * second_moment + (1.0 - beta_two) * gradient * gradient
    first_hat = first_moment / (1.0 - beta_one**step_count)
    second_hat = second_moment / (1.0 - beta_two**step_count)
    master = master - learn_rate * (
        first_hat / (jnp.sqrt(second_hat) + adam_eps) + weight_decay * master
    )
    return (master, first_moment, second_moment)


def group_totals(values, image_count, group_width):
    return jnp.sum(values, axis=(1, 2)).reshape(image_count, GROUPS, group_width).sum(-1)


def fold_states(stacked, partner_index):
    running = jnp.zeros_like(stacked)
    pieces_in = lax.all_gather(stacked.astype(jnp.bfloat16), "rep", axis=1, tiled=True).astype(
        jnp.float32
    )
    block_cols = running.shape[1]
    row_ids = lax.iota(jnp.int32, pieces_in.shape[1])
    slot_ids = lax.iota(jnp.int32, block_cols)
    select = (
        (row_ids[None, :] // block_cols == partner_index)
        & (row_ids[None, :] % block_cols == slot_ids[:, None])
    ).astype(jnp.float32)
    return running + jnp.einsum("br,srk->sbk", select, pieces_in, precision=lax.Precision.HIGHEST)


def per_device(
    latents,
    cotangent,
    gn_gain,
    gn_bias,
    conv_weight,
    master,
    moment_one,
    moment_two,
    departing,
    partner,
):
    image_count, row_count, col_count, channels = latents.shape
    group_width = channels // GROUPS
    pixel_count = row_count * col_count * group_width
    float_in = latents.astype(jnp.float32)
    group_mean = group_totals(float_in, image_count, group_width) / pixel_count
    centred = float_in - jnp.repeat(group_mean, group_width, axis=1)[:, None, None, :]
    variance = group_totals(centred * centred, image_count, group_width) / pixel_count
    inverse = jnp.repeat(lax.rsqrt(variance + norm_eps), group_width, axis=1)[:, None, None, :]
    activated = jax.nn.silu(centred * inverse * gn_gain + gn_bias).astype(jnp.bfloat16)
    padded = jnp.pad(activated, ((0, 0), (1, 1), (1, 1), (0, 0)))
    patches = gather_taps(padded, row_count, col_count).reshape(-1, 9 * channels)
    out_cols = conv_weight.shape[1]
    columns = patches
    forward = jnp.dot(
        columns,
        lax.all_gather(conv_weight, "shard", axis=0, tiled=True),
        preferred_element_type=jnp.float32,
    )
    conv_out = forward.astype(jnp.bfloat16).reshape(image_count, row_count, col_count, out_cols)
    cot_flat = cotangent.reshape(-1, cotangent.shape[3])
    columns = patches
    grad_rows = lax.psum_scatter(
        lax.dot_general(
            columns, cot_flat, (((0,), (0,)), ((), ())), preferred_element_type=jnp.float32
        ).astype(jnp.bfloat16),
        "shard",
        scatter_dimension=0,
        tiled=True,
    ).astype(jnp.float32)
    my_index = lax.axis_index("rep")
    staying = (1 - departing[my_index]).astype(jnp.float32)
    partner_index = partner[my_index]
    images = image_count * lax.axis_size("shard") * (lax.axis_size("rep") // 2)
    owned = (
        lax.psum_scatter(
            (grad_rows * staying).astype(jnp.bfloat16), "rep", scatter_dimension=1, tiled=True
        ).astype(jnp.float32)
        / images
    )
    own_state = adam(master, moment_one, moment_two, owned.T)
    received = fold_states(jnp.stack(own_state), partner_index)
    mate_state = (received[0], received[1], received[2])

    def arrange(own_part, mate_part):
        return (jnp.stack([own_part, mate_part]) * staying)[None]

    return (
        conv_out,
        arrange(own_state[0], mate_state[0]),
        arrange(own_state[1], mate_state[1]),
        arrange(own_state[2], mate_state[2]),
    )


def solution(mesh):
    return jax.shard_map(
        per_device,
        mesh=mesh,
        in_specs=(
            P(("rep", "shard"), None, None, None),
            P(("rep", "shard"), None, None, None),
            P(),
            P(),
            P("shard", None),
            P("rep", "shard"),
            P("rep", "shard"),
            P("rep", "shard"),
            P(),
            P(),
        ),
        out_specs=(
            P(("rep", "shard"), None, None, None),
            P("rep", None, None, "shard"),
            P("rep", None, None, "shard"),
            P("rep", None, None, "shard"),
        ),
        check_vma=False,
    )
```

profile of v0, /device:TPU:0, one launch (start us, length us, event | category | flops | bytes accessed | tf_op | source)
XLA Modules:
  0.0 515.0 jit_solution(16802415914537754507)
XLA Ops:
  7.2 3.2 convert_reduce_fusion
  10.8 3.9 fusion.2
  15.0 0.1 mul.100
  15.2 6.0 %fusion.10 = bf16[4,32,32,640]{3,2,1,0:T(8,128)(2,1)S(1)} fusion(bf16[4,32,32,640]{3,2,1,0:T(8,128)(2,1)} %param.10, f32[640]{0:T(1024)S(1)} %copy-done.3, f32[640]{0:T(1024)S(1)} %copy-done.4, f32[4,640]{1,0:T(4,128)S(1)} %mul.100, f32[4,640]{1,0:T(4,128)S(1)} %sub.23), kind=kLoop, calls=%fused_computation.13 | loop fusion | flops 26214400 | bytes 10511360 | tf_op jit(solution)/shard_map/convert_element_type | solution.py:77
  21.2 4.1 fusion.11
  25.3 3.1 fusion.12
  28.3 5.4 %fusion.13 = bf16[4,32,32,5760]{3,2,1,0:T(8,128)(2,1)} fusion(bf16[4,32,32,5760]{3,2,1,0:T(8,128)(2,1)} %fusion.12, bf16[4,32,32,640]{3,2,1,0:T(8,128)(2,1)S(1)} %fusion.10), kind=kLoop, calls=%fused_computation.26 | loop fusion | bytes 10485760
  33.7 5.6 %fusion.14 = bf16[4,32,32,5760]{3,2,1,0:T(8,128)(2,1)} fusion(bf16[4,32,32,5760]{3,2,1,0:T(8,128)(2,1)} %fusion.13, bf16[4,32,32,640]{3,2,1,0:T(8,128)(2,1)S(1)} %fusion.10), kind=kLoop, calls=%fused_computation.27 | loop fusion | bytes 10485760
  39.3 5.3 %constant_dynamic-update-slice_fusion = bf16[4,32,32,5760]{3,2,1,0:T(8,128)(2,1)} fusion(bf16[4,32,32,5760]{3,2,1,0:T(8,128)(2,1)} %fusion.14, f32[640]{0:T(1024)S(1)} %copy-done.3, f32[640]{0:T(1024)S(1)} %copy-done.4, f32[4,640]{1,0:T(4,128)S(1)} %mul.100, f32[4,640]{1,0:T(4,128)S(1)} %sub.23, bf16[4,32,32,640]{3,2,1,0:T(8,128)(2,1)S(1)} %bitcast.57), kind=kLoop, calls=%fused_computation.54 | loop fusion | flops 26214400 | bytes 10511360
  44.5 5.4 %fusion.15 = bf16[4,32,32,5760]{3,2,1,0:T(8,128)(2,1)} fusion(bf16[4,32,32,5760]{3,2,1,0:T(8,128)(2,1)} %constant_dynamic-update-slice_fusion, bf16[4,32,32,640]{3,2,1,0:T(8,128)(2,1)S(1)} %fusion.10), kind=kLoop, calls=%fused_computation.28 | loop fusion | bytes 10485760
  49.9 5.2 %fusion.16 = bf16[4,32,32,5760]{3,2,1,0:T(8,128)(2,1)} fusion(bf16[4,32,32,5760]{3,2,1,0:T(8,128)(2,1)} %fusion.15, bf16[4,32,32,640]{3,2,1,0:T(8,128)(2,1)S(1)} %fusion.10), kind=kLoop, calls=%fused_computation.29 | loop fusion | bytes 10485760
  55.1 3.1 fusion.17
  58.3 5.3 %fusion.18 = bf16[4,32,32,5760]{3,2,1,0:T(8,128)(2,1)} fusion(bf16[4,32,32,5760]{3,2,1,0:T(8,128)(2,1)} %fusion.17, bf16[4,32,32,640]{3,2,1,0:T(8,128)(2,1)S(1)} %fusion.10), kind=kLoop, calls=%fused_computation.31 | loop fusion | bytes 10485760 | tf_op jit(solution)/shard_map/concatenate | solution.py:24
  63.6 43.8 %bitcast_convert_fusion = bf16[5760,640]{1,0:T(8,128)(2,1)} fusion(bf16[4,32,32,5760]{3,2,1,0:T(8,128)(2,1)} %fusion.18, bf16[4,32,32,640]{3,2,1,0:T(8,128)(2,1)S(1)} %bitcast.61), kind=kOutput, calls=%fused_computation | convolution fusion | flops 30202675200 | bytes 59801600 | tf_op jit(solution)/shard_map/dot_general | solution.py:91
  107.5 0.6 dynamic_slice.6
  108.8 90.3 %reduce-scatter.3.cloned.1.call-done = bf16[2880,640]{1,0:T(8,128)(2,1)} async-done(((bf16[5760,640]{1,0:T(8,128)(2,1)}), bf16[2880,640]{1,0:T(8,128)(2,1)}) %reduce-scatter.3.cloned.1.call-update) | async-done | bytes 3686416 | tf_op jit(solution)/shard_map/reduce_scatter | solution.py:90
  199.1 4.6 multiply_convert_fusion
  203.8 0.7 all-gather.3.cloned.1.call-update
  204.5 0.6 dynamic-slice
  205.8 105.3 %all-reduce.4.cloned.1.call-done = bf16[2880,640]{1,0:T(8,128)(2,1)} async-done(((bf16[2880,640]{1,0:T(8,128)(2,1)}), bf16[2880,640]{1,0:T(8,128)(2,1)}) %all-reduce.4.cloned.1.call-update) | async-done | bytes 3686416
  311.1 1.7 constant_dynamic-slice_fusion
  312.7 0.3 copy.42
  313.1 0.4 fusion.35
  313.5 0.9 pad_maximum_fusion
  314.5 0.6 dynamic_slice.7
  315.1 0.7 fusion.33
  315.7 88.4 %all-gather.3.cloned.1.call-done = bf16[5760,640]{1,0:T(8,128)(2,1)} async-done(((bf16[2880,640]{1,0:T(8,128)(2,1)}), bf16[5760,640]{1,0:T(8,128)(2,1)}) %all-gather.3.cloned.1.call-update) | async-done | bytes 7372816 | tf_op jit(solution)/shard_map/all_gather | solution.py:84
  404.2 45.6 %convolution_convert_fusion = bf16[4096,640]{1,0:T(8,128)(2,1)} fusion(bf16[4096,5760]{1,0:T(8,128)(2,1)} %bitcast.59, bf16[5760,640]{1,0:T(8,128)(2,1)} %all-gather.3.cloned.1.call-done), kind=kOutput, calls=%fused_computation.23 | convolution fusion | flops 30201610240 | bytes 59801600 | tf_op jit(solution)/shard_map/dot_general | solution.py:82
  449.8 50.0 %all-gather.5.cloned.1.call-done = bf16[3,640,2880]{2,1,0:T(8,128)(2,1)} async-done(((bf16[3,40,2880]{2,1,0:T(8,128)(2,1)}), bf16[3,640,2880]{2,1,0:T(8,128)(2,1)}) %all-gather.5.cloned.1.call-update) | async-done | bytes 11059216 | tf_op jit(solution)/shard_map/all_gather | solution.py:44
  499.7 5.9 %convolution_bitcast_fusion = f32[3,40,2880]{2,1,0:T(8,128)S(1)} fusion(bf16[3,640,2880]{2,1,0:T(8,128)(2,1)} %all-gather.5.cloned.1.call-done, s32[640]{0:T(1024)S(1)} %fusion.27, pred[640]{0:T(1024)(128)(4,1)S(1)} %fusion.33), kind=kOutput, calls=%fused_computation.32 | convolution fusion | flops 442419200 | bytes 12444800 | tf_op jit(solution)/shard_map/br,srk->sbk/dot_general | solution.py:54
  505.8 1.0 maximum_multiply_fusion.2
  506.8 1.4 maximum_multiply_fusion
  (44 shorter events, 1.0 us)
Async XLA Ops:
  7.2 8.0 %copy-start.4 = (f32[640]{0:T(1024)S(1)}, f32[640]{0:T(1024)}, u32[]{:S(2)}) copy-start(f32[640]{0:T(1024)} %param.12) | copy-start | bytes 7684
  7.2 8.0 %copy-start.3 = (f32[640]{0:T(1024)S(1)}, f32[640]{0:T(1024)}, u32[]{:S(2)}) copy-start(f32[640]{0:T(1024)} %param.13) | copy-start | bytes 7684
  7.2 191.9 %reduce-scatter.3.cloned.1.call-start = ((), (), s32[]{:S(2)}) async-start(), calls=%async_computation.2 | async-start | bytes 11059200 | tf_op jit(solution)/shard_map/reduce_scatter | solution.py:90
  28.3 10.9 %slice-start = ((s8[5242880]{0:T(1024)(128)(4,1)}), s8[4194304]{0:T(1024)(128)(4,1)S(1)}, s32[]{:S(2)}) async-start(s8[5242880]{0:T(1024)(128)(4,1)} %bitcast.56), calls=%async_computation.5 | async-start | bytes 8388608
  33.7 5.6 %slice-start.1 = ((s8[5242880]{0:T(1024)(128)(4,1)}), s8[1048576]{0:T(1024)(128)(4,1)S(1)}, s32[]{:S(2)}) async-start(s8[5242880]{0:T(1024)(128)(4,1)} %bitcast.56), calls=%async_computation.6 | async-start | bytes 2097152
  55.1 8.4 %slice-start.2 = ((s8[5242880]{0:T(1024)(128)(4,1)}), s8[4194304]{0:T(1024)(128)(4,1)S(1)}, s32[]{:S(2)}) async-start(s8[5242880]{0:T(1024)(128)(4,1)} %bitcast.60), calls=%async_computation.7 | async-start | bytes 8388608
  58.3 5.3 %slice-start.3 = ((s8[5242880]{0:T(1024)(128)(4,1)}), s8[1048576]{0:T(1024)(128)(4,1)S(1)}, s32[]{:S(2)}) async-start(s8[5242880]{0:T(1024)(128)(4,1)} %bitcast.60), calls=%async_computation.8 | async-start | bytes 2097152
  63.6 43.9 %copy-start.5 = (s32[16]{0:T(128)S(1)}, s32[16]{0:T(128)}, u32[]{:S(2)}) copy-start(s32[16]{0:T(128)} %param.18) | copy-start | bytes 196
  107.4 97.1 %copy-start.7 = (u32[32]{0:T(128)S(1)}, u32[32]{0:T(128)}, u32[]{:S(2)}) copy-start(u32[32]{0:T(128)} %constant.75) | copy-start | bytes 388
  107.4 205.6 %copy-start = (f32[40,2880]{1,0:T(8,128)S(1)}, f32[40,2880]{1,0:T(8,128)}, u32[]{:S(2)}) copy-start(f32[40,2880]{1,0:T(8,128)} %param.17) | copy-start | bytes 1382404
  107.4 205.6 %copy-start.1 = (f32[40,2880]{1,0:T(8,128)S(1)}, f32[40,2880]{1,0:T(8,128)}, u32[]{:S(2)}) copy-start(f32[40,2880]{1,0:T(8,128)} %param.15) | copy-start | bytes 1382404
  107.4 205.6 %copy-start.2 = (f32[40,2880]{1,0:T(8,128)S(1)}, f32[40,2880]{1,0:T(8,128)}, u32[]{:S(2)}) copy-start(f32[40,2880]{1,0:T(8,128)} %param.16) | copy-start | bytes 1382404
  107.5 203.6 %all-reduce.4.cloned.1.call-start = ((), (), s32[]{:S(2)}) async-start(), calls=%async_computation.4 | async-start | bytes 7372800
  199.1 115.4 %copy-start.6 = (s32[16]{0:T(128)S(1)}, s32[16]{0:T(128)}, u32[]{:S(2)}) copy-start(s32[16]{0:T(128)} %param.19) | copy-start | bytes 196
  203.7 200.4 %all-gather.3.cloned.1.call-start = ((), (), s32[]{:S(2)}) async-start(), calls=%async_computation.1 | async-start | bytes 11059200 | tf_op jit(solution)/shard_map/all_gather | solution.py:84
  204.5 295.3 %all-gather.5.cloned.1.call-start = ((), (), s32[]{:S(2)}) async-start(), calls=%async_computation.3 | async-start | bytes 12011520 | tf_op jit(solution)/shard_map/all_gather | solution.py:44
Sparse Core Ops, SparseCore 0:
  107.6 91.4 reduce-scatter.2
  203.9 107.1 all-reduce.3
  312.6 91.4 all-gather.2
  406.8 92.9 all-gather.4
where the time goes:
time: 518 us; the launch traced here: 515 us
  waiting for transfers between devices  335 us (65%)
  matrix products  95.4 us (18%)
  local copies, waits for them, and re-layouts  41.5 us (8%)
  other arithmetic  27.6 us (5%)
  between operations  15.5 us (3%)
    unnamed x5, waiting for transfers between devices  106 us
    reduce_scatter x1, waiting for transfers between devices, per_device(): lax.psum_scatter(lax.dot_general(columns, cot_flat, (((0,), (0,)), ((), (...  90.3 us
    all_gather x1, waiting for transfers between devices, per_device(): lax.all_gather(conv_weight, 'shard', axis=0, tiled=True)  88.4 us
    all_gather x1, waiting for transfers between devices, fold_states(): lax.all_gather(stacked.astype(jnp.bfloat16), 'rep', axis=1, tiled=True)  50 us
    dot_general x1, matrix products, per_device(): jnp.dot(columns, lax.all_gather(conv_weight, 'shard', axis=0, tiled=True)...  45.6 us
    dot_general x1, matrix products, per_device(): lax.dot_general(columns, cot_flat, (((0,), (0,)), ((), ())), preferred_el...  43.8 us
    unnamed x33, local copies, waits for them, and re-layouts  34.1 us
  transfers between devices with their start and end apart: 4, of which 4 were waited for; matrix products, arithmetic and copies ran while one was open for 10% of the time, Pallas kernels for 0%

commit v1 on v0

--- a/solution.py
+++ b/solution.py
@@ -1,10 +1,17 @@
+import functools
+
 import jax
 import jax.numpy as jnp
+import numpy as np
 from jax import lax
+from jax.experimental import pallas as pl
+from jax.experimental.pallas import tpu as pltpu
 from jax.sharding import PartitionSpec as P
 
 GROUPS = 32
-
+LANES = 128
+MIB = 1024 * 1024
+VMEM_LIMIT = 58 * MIB
 
 beta_one = 0.9
 beta_two = 0.999
@@ -13,15 +20,10 @@
 weight_decay = 0.01
 adam_eps = 1e-08
 norm_eps = 1e-05
-
-
-def gather_taps(padded, row_count, col_count):
-    taps = [
-        padded[:, row_off : row_off + row_count, col_off : col_off + col_count, :]
-        for row_off in range(3)
-        for col_off in range(3)
-    ]
-    return jnp.concatenate(taps, axis=3)
+CHUNKS = (16, 8)
+
+BF16 = jnp.bfloat16
+F32 = jnp.float32
 
 
 def adam(master, first_moment, second_moment, gradient):
@@ -33,6 +35,437 @@
         first_hat / (jnp.sqrt(second_hat) + adam_eps) + weight_decay * master
     )
     return (master, first_moment, second_moment)
+
+
+def norm_kernel(lat_ref, gain_ref, bias_ref, member_ref, out_ref, mean_ref, scale_ref):
+    images, rows, width, ch = lat_ref.shape
+    tiles = ch // LANES
+    count = rows * width * (ch // GROUPS)
+    image = pl.program_id(0)
+
+    def group_means(totals):
+        by_group = jnp.dot(
+            jnp.concatenate(totals, axis=0),
+            member_ref[...],
+            precision=lax.Precision.HIGHEST,
+            preferred_element_type=F32,
+        )
+        back = lax.dot_general(
+            by_group,
+            member_ref[...],
+            (((1,), (1,)), ((), ())),
+            precision=lax.Precision.HIGHEST,
+            preferred_element_type=F32,
+        )
+        sums = jnp.sum(back.reshape(images, 8, ch), axis=1)
+        return sums * (1.0 / count)
+
+    def fold(value):
+        return jnp.sum(value.reshape(width // 8, 8, ch), axis=0)
+
+    @pl.when(image == 0)
+    def _():
+        zero = jnp.zeros((8, ch), F32)
+        totals = []
+        for k in range(images):
+            def add_row(row, total, k=k):
+                return total + fold(lat_ref[k, row].astype(F32))
+
+            totals.append(lax.fori_loop(0, rows, add_row, zero, unroll=8))
+        means = group_means(totals)
+        mean_ref[0:images, :] = means
+        totals = []
+        for k in range(images):
+            mean = means[k : k + 1]
+
+            def add_square(row, total, k=k, mean=mean):
+                centred = lat_ref[k, row].astype(F32) - mean
+                return total + fold(centred * centred)
+
+            totals.append(lax.fori_loop(0, rows, add_square, zero, unroll=8))
+        scale_ref[0:images, :] = lax.rsqrt(group_means(totals) + norm_eps) * gain_ref[...]
+
+    mean = mean_ref[pl.ds(image, 1), :]
+    scale = scale_ref[pl.ds(image, 1), :]
+    bias = bias_ref[...]
+    column = lax.broadcasted_iota(jnp.int32, (width, ch), 0)
+
+    def write_row(row, carry):
+        half = 0.5 * ((lat_ref[image, row].astype(F32) - mean) * scale + bias)
+        act = half + half * jnp.tanh(half)
+        before = jnp.where(column == 0, 0.0, pltpu.roll(act, 1, 0))
+        after = jnp.where(column == width - 1, 0.0, pltpu.roll(act, width - 1, 0))
+        start = pl.multiple_of((row + 1) * width, width)
+        for shift, value in enumerate((before, act, after)):
+            value = value.astype(BF16)
+            for tile in range(tiles):
+                out_ref[shift * tiles + tile, 0, pl.ds(start, width), :] = value[
+                    :, tile * LANES : (tile + 1) * LANES
+                ]
+        return carry
+
+    lax.fori_loop(0, rows, write_row, 0, unroll=2)
+    edge = jnp.zeros((width, LANES), BF16)
+    for slab in range(3 * tiles):
+        out_ref[slab, 0, 0:width, :] = edge
+        out_ref[slab, 0, (rows + 1) * width : (rows + 2) * width, :] = edge
+
+
+def norm_slabs(latents, gain, bias):
+    images, rows, width, ch = latents.shape
+    member = np.zeros((ch, LANES), np.float32)
+    member[np.arange(ch), np.arange(ch) // (ch // GROUPS)] = 1.0
+    slabs, cells = 3 * ch // LANES, (rows + 2) * width
+    return pl.pallas_call(
+        norm_kernel,
+        grid=(images,),
+        in_specs=[
+            pl.BlockSpec((images, rows, width, ch), lambda i: (0, 0, 0, 0)),
+            pl.BlockSpec((1, ch), lambda i: (0, 0)),
+            pl.BlockSpec((1, ch), lambda i: (0, 0)),
+            pl.BlockSpec((ch, LANES), lambda i: (0, 0)),
+        ],
+        out_specs=pl.BlockSpec((slabs, 1, cells, LANES), lambda i: (0, i, 0, 0)),
+        out_shape=jax.ShapeDtypeStruct((slabs, images, cells, LANES), BF16),
+        scratch_shapes=[pltpu.VMEM((-(-images // 8) * 8, ch), F32)] * 2,
+        compiler_params=pltpu.CompilerParams(vmem_limit_bytes=VMEM_LIMIT),
+        cost_estimate=pl.CostEstimate(
+            flops=20 * latents.size, bytes_accessed=8 * latents.size, transcendentals=latents.size
+        ),
+        name="norm",
+    )(latents, gain.reshape(1, ch), bias.reshape(1, ch), jnp.asarray(member))
+
+
+def weight_grad_kernel(pairs, table, info, cot_ref, *refs):
+    slab_refs, out_ref = refs[:-1], refs[-1]
+    images, cells, _ = cot_ref.shape
+    inner = len(slab_refs) // 2
+    quarter = pl.program_id(0) ^ info[0]
+    staying = info[1].astype(F32)
+    for k in range(inner):
+        total = None
+        for image in range(images):
+            sides = []
+            for side in range(2):
+                row = table[(2 * side + 1) * pairs + quarter * inner + k]
+                start = pl.multiple_of(row, 32)
+                sides.append(slab_refs[2 * k + side][0, image, pl.ds(start, cells), :])
+            term = lax.dot_general(
+                cot_ref[image],
+                jnp.concatenate(sides, axis=1),
+                (((0,), (0,)), ((), ())),
+                preferred_element_type=F32,
+            )
+            total = term if total is None else total + term
+        value = (total * staying).astype(BF16)
+        out_ref[k, 0] = value[:, :LANES]
+        out_ref[k, 1] = value[:, LANES:]
+
+
+def weight_grad(slabs, cot, table, info):
+    images, cells, out_ch = cot.shape
+    pairs = table.shape[0] // 4
+    inner = pairs // 8
+    padded = slabs.shape[2]
+
+    def slab_of(k, side):
+        def index(step, table_ref, info_ref):
+            pair = (step ^ info_ref[0]) * inner + k
+            return (table_ref[2 * side * pairs + pair], 0, 0, 0)
+
+        return pl.BlockSpec((1, images, padded, LANES), index)
+
+    return pl.pallas_call(
+        functools.partial(weight_grad_kernel, pairs),
+        grid_spec=pltpu.PrefetchScalarGridSpec(
+            num_scalar_prefetch=2,
+            grid=(4,),
+            in_specs=[pl.BlockSpec((images, cells, out_ch), lambda p, *_: (0, 0, 0))]
+            + [slab_of(k, side) for k in range(inner) for side in range(2)],
+            out_specs=pl.BlockSpec((inner, 2, out_ch, LANES), lambda p, *_: (p, 0, 0, 0)),
+        ),
+        out_shape=jax.ShapeDtypeStruct((4 * inner, 2, out_ch, LANES), BF16),
+        compiler_params=pltpu.CompilerParams(vmem_limit_bytes=VMEM_LIMIT),
+        cost_estimate=pl.CostEstimate(
+            flops=2 * 4 * inner * 2 * LANES * images * cells * out_ch,
+            bytes_accessed=4 * 4 * inner * images * padded * LANES,
+            transcendentals=0,
+        ),
+        name="weight_grad",
+    )(table, info, cot, *([slabs] * (2 * inner)))
+
+
+def tile_table(first, tiles, shards, cols, ch, width):
+    inner_pairs = tiles // 8
+    index = np.arange(8 * inner_pairs)
+    bits, inner = index // inner_pairs, index % inner_pairs
+    p_core, p_shard, p_x = bits >> 2, (bits >> 1) & 1, bits & 1
+    per_tap = ch // LANES
+    table = []
+    for side in range(2):
+        tile = first + p_core * (tiles // 2) + p_x * (tiles // 4) + 2 * inner + side
+        tile = np.minimum((p_shard * cols) // LANES + tile, 9 * per_tap - 1)
+        tap = tile // per_tap
+        table += [(tap % 3) * per_tap + tile % per_tap, (tap // 3) * width]
+    return jnp.asarray(np.concatenate(table), jnp.int32)
+
+
+def forward_kernel(place, slab_ref, own_ref, near_ref, far_ref, *refs):
+    out_ref, weight, sems = refs[-3:]
+    _, _, padded, _ = slab_ref.shape
+    _, cells, out_ch = out_ref.shape
+    slabs = slab_ref.shape[0]
+    width = (padded - cells) // 2
+    own_rows, part_rows = own_ref.shape[0], near_ref.shape[0]
+
+    @pl.when(pl.program_id(0) == 0)
+    def _():
+        copies = [
+            pltpu.make_async_copy(
+                ref,
+                weight.at[pl.ds(pl.multiple_of(place[index], 16), rows)],
+                sems.at[index],
+            )
+            for index, (ref, rows) in enumerate(
+                ((own_ref, own_rows), (near_ref, part_rows), (far_ref, part_rows))
+            )
+        ]
+        for copy in copies:
+            copy.start()
+        for copy in copies:
+            copy.wait()
+
+    block = 512
+    for start in range(0, cells, block):
+        cols = jnp.concatenate(
+            [
+                slab_ref[slab, 0, start + width * down : start + width * down + block, :]
+                for down in range(3)
+                for slab in range(slabs)
+            ],
+            axis=1,
+        )
+        total = lax.dot_general(
+            weight[...], cols, (((0,), (1,)), ((), ())), preferred_element_type=F32
+        )
+        out_ref[0, start : start + block, :] = total.astype(BF16).T
+
+
+def forward(slabs, own, near, far, place, width, first, count, earlier=None):
+    slab_count, images, padded, _ = slabs.shape
+    cells = padded - 2 * width
+    out_ch = own.shape[1]
+    rows = own.shape[0] + near.shape[0] + far.shape[0]
+    extra = () if earlier is None else (earlier,)
+    return pl.pallas_call(
+        forward_kernel,
+        grid_spec=pltpu.PrefetchScalarGridSpec(
+            num_scalar_prefetch=1,
+            grid=(count,),
+            in_specs=[
+                pl.BlockSpec((slab_count, 1, padded, LANES), lambda i, *_: (0, i + first, 0, 0)),
+                pl.BlockSpec(memory_space=pl.ANY),
+                pl.BlockSpec(memory_space=pl.ANY),
+                pl.BlockSpec(memory_space=pl.ANY),
+            ]
+            + [pl.BlockSpec(memory_space=pl.ANY) for _ in extra],
+            out_specs=pl.BlockSpec((1, cells, out_ch), lambda i, *_: (i + first, 0, 0)),
+            scratch_shapes=[
+                pltpu.VMEM((rows, out_ch), BF16),
+                pltpu.SemaphoreType.DMA((3,)),
+            ],
+        ),
+        out_shape=jax.ShapeDtypeStruct((images, cells, out_ch), BF16),
+        input_output_aliases={5: 0} if extra else {},
+        compiler_params=pltpu.CompilerParams(vmem_limit_bytes=VMEM_LIMIT),
+        cost_estimate=pl.CostEstimate(
+            flops=2 * count * cells * rows * out_ch,
+            bytes_accessed=2 * (rows * out_ch + slab_count * count * padded * LANES),
+            transcendentals=0,
+        ),
+        name="forward",
+    )(place, slabs, own, near, far, *extra)
+
+
+def choose_kernel(partner, *refs):
+    out_ref = refs[-1]
+    reps = out_ref.shape[0]
+    at = 0
+    for group in range(0, len(refs) - 1, 4):
+        total = refs[group][...].astype(F32)
+        for ref in refs[group + 1 : group + 4]:
+            total = total + ref[...].astype(F32)
+        total = total.astype(BF16)
+        tiles = total.shape[0]
+        for rep in range(reps):
+            out_ref[rep, 0, at : at + tiles] = total[:, rep]
+        at += tiles
+    for rep in range(reps):
+        out_ref[rep, 1] = out_ref[partner[rep], 0]
+
+
+def choose(parts, partner):
+    _, reps, rows, lanes = parts[0].shape
+    tiles = sum(part.shape[0] for part in parts) // 4
+    return pl.pallas_call(
+        choose_kernel,
+        in_specs=[pl.BlockSpec(memory_space=pltpu.SMEM)]
+        + [pl.BlockSpec(memory_space=pltpu.VMEM)] * len(parts),
+        out_specs=pl.BlockSpec(memory_space=pltpu.VMEM),
+        out_shape=jax.ShapeDtypeStruct((reps, 2, tiles, rows, lanes), BF16),
+        compiler_params=pltpu.CompilerParams(vmem_limit_bytes=VMEM_LIMIT),
+        name="choose",
+    )(partner, *parts)
+
+
+def update_kernel(source, images, info, grad_ref, master_ref, one_ref, two_ref, mate_ref, *refs):
+    outs, grad = refs[:3], refs[3]
+    block_rows, cols = master_ref.shape
+    high = grad_ref.shape[3]
+    staying = info[1].astype(F32)
+    odd = info[2] != 0
+    skew = info[3]
+    for block in range(2):
+        for tile, (upper, lower, inner) in enumerate(source):
+            span = slice(tile * LANES, (tile + 1) * LANES)
+            top = grad_ref[upper, block, inner].astype(F32)
+            low = grad_ref[lower, block, inner].astype(F32)
+            grad[0:high, span] = top
+            grad[high:block_rows, span] = low[2 * high - block_rows : high]
+        gradient = jnp.where(odd, grad[:, LANES // 2 : LANES // 2 + cols], grad[:, 0:cols])
+        gradient = gradient / images
+        if block == 0:
+            state = (master_ref[...], one_ref[...], two_ref[...])
+        else:
+            state = tuple(mate_ref[0, k].astype(F32) for k in range(3))
+        for out, value in zip(outs, adam(*state, gradient)):
+            out[0, block] = value * staying
+
+
+def update(received, source, images, master, one, two, mates, info):
+    block_rows, cols = master.shape
+    out = jax.ShapeDtypeStruct((1, 2, block_rows, cols), F32)
+    whole = [pl.BlockSpec(received.shape, lambda i, *_: (0,) * received.ndim)]
+    state = [pl.BlockSpec((block_rows, cols), lambda i, *_: (0, 0))] * 3
+    return pl.pallas_call(
+        functools.partial(lambda info_ref, *refs: update_kernel(source, images, info_ref, *refs)),
+        grid_spec=pltpu.PrefetchScalarGridSpec(
+            num_scalar_prefetch=1,
+            grid=(1,),
+            in_specs=whole
+            + state
+            + [pl.BlockSpec((1, 3, block_rows, cols), lambda i, info_ref: (info_ref[0], 0, 0, 0))],
+            out_specs=[pl.BlockSpec((1, 2, block_rows, cols), lambda i, *_: (0, 0, 0, 0))] * 3,
+            scratch_shapes=[pltpu.VMEM((block_rows, len(source) * LANES), F32)],
+        ),
+        out_shape=[out] * 3,
+        compiler_params=pltpu.CompilerParams(vmem_limit_bytes=VMEM_LIMIT),
+        name="update",
+    )(info, received, master, one, two, mates)
+
+
+def per_device(
+    latents,
+    cotangent,
+    gn_gain,
+    gn_bias,
+    conv_weight,
+    master,
+    moment_one,
+    moment_two,
+    departing,
+    partner,
+):
+    images, rows, width, ch = latents.shape
+    reps, shards = lax.axis_size("rep"), lax.axis_size("shard")
+    out_ch = conv_weight.shape[1]
+    block_rows, cols = master.shape
+    rep, shard = lax.axis_index("rep"), lax.axis_index("shard")
+    core, col_x, low_z, high_z = rep & 1, (rep >> 1) & 1, (rep >> 2) & 1, rep >> 3
+    staying = 1 - departing[rep]
+
+    def swap_rep(value, bits):
+        return lax.ppermute(value, "rep", [(i, i ^ bits) for i in range(reps)])
+
+    def swap_shard(value):
+        return lax.ppermute(value, "shard", [(0, 1), (1, 0)])
+
+    def swap_both(value, bits):
+        pairs = [(i, i ^ (2 * bits + 1)) for i in range(2 * reps)]
+        return lax.ppermute(value, ("rep", "shard"), pairs)
+
+    state = jnp.stack([master, moment_one, moment_two]).astype(BF16)
+    mates = lax.all_gather(state, "rep", axis=0, tiled=False)
+
+    own_rows = conv_weight.shape[0]
+    part_rows = own_rows // 2
+    near = swap_shard(lax.dynamic_slice_in_dim(conv_weight, core * part_rows, part_rows, 0))
+    far = swap_rep(near, 1)
+    missing = (1 - shard) * own_rows
+    place = jnp.stack(
+        [shard * own_rows, missing + core * part_rows, missing + (1 - core) * part_rows]
+    ).astype(jnp.int32)
+
+    slabs = norm_slabs(latents, gn_gain, gn_bias)
+
+    def add(*terms):
+        total = terms[0].astype(F32)
+        for term in terms[1:]:
+            total = total + term.astype(F32)
+        return total.astype(BF16)
+
+    cot = cotangent.reshape(images, rows * width, out_ch)
+    here = 4 * core + 2 * shard + col_x
+    info_send = jnp.stack([here ^ 4, staying]).astype(jnp.int32)
+    info_keep = jnp.stack([here, staying]).astype(jnp.int32)
+    high = -(-block_rows // 16) * 8
+    pieces, source, first_tile, held_before = [], [], 0, 0
+    last_tile = -(-cols // LANES)
+    for tiles in CHUNKS:
+        inner = tiles // 8
+        table = tile_table(first_tile, tiles, shards, cols, ch, width)
+        other = swap_rep(weight_grad(slabs, cot, table, info_send), 1)
+        if first_tile == 0:
+            other, far = lax.optimization_barrier((other, far))
+        keep = weight_grad(slabs, cot, table, info_keep)
+        quarter = [add(keep[k * inner : (k + 1) * inner], other[k * inner : (k + 1) * inner]) for k in range(4)]
+        arrived = (swap_both(quarter[3], 2), swap_shard(quarter[2]), swap_rep(quarter[1], 2))
+        if first_tile + tiles >= last_tile:
+            conv = forward(slabs, conv_weight, near, far, place, width, 0, images // 2)
+            arrived, conv = lax.optimization_barrier((arrived, conv))
+        plane = add(quarter[0], *arrived)
+        plane = plane.reshape(tiles // 4, reps, block_rows, LANES)
+        held = tiles // 8
+
+        def part(d_high, d_low):
+            start = (held * (low_z ^ d_low), 0, (block_rows - high) * (high_z ^ d_high), 0)
+            return lax.dynamic_slice(plane, start, (held, reps, high, LANES))
+
+        pieces += [part(0, 0), swap_rep(part(1, 1), 12), swap_rep(part(1, 0), 8), swap_rep(part(0, 1), 4)]
+        for tile in range(tiles):
+            at = 4 * ((tile % (tiles // 4)) // held) + 2 * ((tile % (tiles // 2)) // (tiles // 4))
+            at += tile // (tiles // 2)
+            source.append((at, at + 8, held_before + tile % held))
+        first_tile += tiles
+        held_before += held
+    source = source[:last_tile]
+    conv = forward(slabs, conv_weight, near, far, place, width, images // 2, images - images // 2, conv)
+    pieces, conv = lax.optimization_barrier((pieces, conv))
+    received = lax.all_to_all(choose(pieces, partner), "rep", 0, 0, tiled=True)
+
+    info = jnp.stack([partner[rep], staying, shard, jnp.zeros_like(shard)]).astype(jnp.int32)
+    count = images * shards * (reps // 2)
+    new = update(received, source, count, master, moment_one, moment_two, mates, info)
+    return (conv.reshape(images, rows, width, out_ch), *new)
+
+
+def gather_taps(padded, row_count, col_count):
+    taps = [
+        padded[:, row_off : row_off + row_count, col_off : col_off + col_count, :]
+        for row_off in range(3)
+        for col_off in range(3)
+    ]
+    return jnp.concatenate(taps, axis=3)
 
 
 def group_totals(values, image_count, group_width):
@@ -54,7 +487,7 @@
     return running + jnp.einsum("br,srk->sbk", select, pieces_in, precision=lax.Precision.HIGHEST)
 
 
-def per_device(
+def per_device_any(
     latents,
     cotangent,
     gn_gain,
@@ -121,8 +554,9 @@
 
 
 def solution(mesh):
+    paired = mesh.shape["shard"] == 2 and mesh.shape["rep"] == 16
     return jax.shard_map(
-        per_device,
+        per_device if paired else per_device_any,
         mesh=mesh,
         in_specs=(
             P(("rep", "shard"), None, None, None),

time: 518 us -> 212 us (0.41)
  waiting for transfers between devices: 335 us -> 18.8 us
  Pallas kernels: 0 us -> 130 us
  matrix products: 95.4 us -> 0 us
  local copies, waits for them, and re-layouts: 41.5 us -> 8.44 us
  starting transfers between devices: 0.16 us -> 24.4 us
  other arithmetic: 27.6 us -> 14.7 us
    all_gather x2 -> x1, waiting for transfers between devices: 138 us -> 0.01 us  [per_device(): mates = lax.all_gather(state, 'rep', axis=0, tiled=False)]
    pallas_call x0 -> x9, Pallas kernels: none -> 130 us  [the longest x4 59.3 us: weight_grad(): pl.pallas_call(functools.partial(weight_grad_kernel, pairs), grid_spec=pl...]
    unnamed x5 -> x1, waiting for transfers between devices: 106 us -> 0.02 us
    dot_general x3 -> x0, matrix products: 95.4 us -> none  [the longest x1 45.6 us: per_device(): jnp.dot(columns, lax.all_gather(conv_weight, 'shard', axis=0, tiled=True)...]
    reduce_scatter x1 -> x0, waiting for transfers between devices: 90.3 us -> none  [per_device(): lax.psum_scatter(lax.dot_general(columns, cot_flat, (((0,), (0,)), ((), (...]
    unnamed x33 -> x24, local copies, waits for them, and re-layouts: 34.1 us -> 2.96 us
    ppermute x0 -> x16, starting transfers between devices: none -> 18.6 us  [the longest x11 11.5 us: swap_rep(): return lax.ppermute(value, 'rep', [(i, i ^ bits) for i in range(reps)])]
    all_to_all x0 -> x1, waiting for transfers between devices: none -> 13.7 us  [per_device(): received = lax.all_to_all(choose(pieces, partner), 'rep', 0, 0, tiled=True)]
  transfers between devices with their start and end apart: 4 -> 18, of which waited for: 4 -> 3; matrix products, arithmetic and copies ran while one was open for 10% -> 8% of each run, Pallas kernels for 0% -> 59%
where the time goes in v1:
time: 212 us; the launch traced here: 211 us
  Pallas kernels  130 us (61%)
  starting transfers between devices  24.4 us (12%)
  waiting for transfers between devices  18.8 us (9%)
  between operations  14.9 us (7%)
  other arithmetic  14.7 us (7%)
  local copies, waits for them, and re-layouts  8.44 us (4%)
    pallas_call x4, Pallas kernels, weight_grad(): pl.pallas_call(functools.partial(weight_grad_kernel, pairs), grid_spec=pl...  59.3 us
    pallas_call x2, Pallas kernels, forward(): pl.pallas_call(forward_kernel, grid_spec=pltpu.PrefetchScalarGridSpec(num...  47.6 us
    pallas_call x1, Pallas kernels, norm_slabs(): pl.pallas_call(norm_kernel, grid=(images,), in_specs=[pl.BlockSpec((image...  15.6 us
    all_to_all x1, waiting for transfers between devices, per_device(): received = lax.all_to_all(choose(pieces, partner), 'rep', 0, 0, tiled=True)  13.7 us
    ppermute x11, starting transfers between devices, swap_rep(): return lax.ppermute(value, 'rep', [(i, i ^ bits) for i in range(reps)])  11.5 us
    convert_element_type x4, other arithmetic, add(): return total.astype(BF16)  8.45 us
    all_to_all x1, starting transfers between devices, per_device(): received = lax.all_to_all(choose(pieces, partner), 'rep', 0, 0, tiled=True)  5.73 us
    ppermute x2, waiting for transfers between devices, swap_both(): return lax.ppermute(value, ('rep', 'shard'), pairs)  5.01 us
  transfers between devices with their start and end apart: 18, of which 3 were waited for; matrix products, arithmetic and copies ran while one was open for 8% of the time, Pallas kernels for 59%

profile of v1, /device:TPU:0, one launch (start us, length us, event | category | flops | bytes accessed | tf_op | source)
XLA Modules:
  0.0 211.0 jit_solution(1844648686239628373)
XLA Ops:
  7.2 1.1 convert_bitcast_fusion.2
  8.3 1.2 convert_bitcast_fusion
  9.5 0.9 pad_maximum_fusion
  10.5 1.7 constant_dynamic-slice_fusion.8
  12.2 3.0 %collective-permute-start.1 = (bf16[1440,640]{1,0:T(8,128)(2,1)S(1)}, bf16[1440,640]{1,0:T(8,128)(2,1)}, u32[]{:S(2)}, u32[]{:S(2)}) collective-permute-start(bf16[1440,640]{1,0:T(8,128)(2,1)S(1)} %constant_dynamic-slice_fusion.8), channel_id=1, source_target_pairs={{0,1},{1,0},{2,3},{3,2},{4,5},{5,4},{6,7},{7,6},{8,9},{9,8},{10,11... | collective-permute-start | bytes 5529608 | tf_op jit(solution)/shard_map/ppermute | solution.py:391
  17.6 15.6 %norm.1.refs_0_.refs_1_.refs_2_.refs_3_.slab_ref = bf16[15,4,1088,128]{3,2,1,0:T(8,128)(2,1)} custom-call(bf16[4,32,32,640]{3,2,1,0:T(8,128)(2,1)} %lat_ref.1, f32[1,640]{1,0:T(1,128)} %reshape.78.gain_ref, f32[1,640]{1,0:T(1,128)} %reshape.79.bias_ref, f32[640,128]{1,0:T(8,128)} %constant.36.clone.member_ref), custom_call_target="tpu_custom_call" | custom-call | flops 52428800 | bytes 20971520 | tf_op jit(solution)/shard_map/norm/pallas_call | solution.py:119
  33.8 17.7 %weight_grad.5 = bf16[8,2,640,128]{3,2,1,0:T(8,128)(2,1)} custom-call(s32[64]{0:T(128)} %constant.37.clone.table, s32[2]{0:T(128)} %pad_add_fusion.1.info, bf16[4,1024,640]{2,1,0:T(8,128)(2,1)} %bitcast.16, bf16[15,4,1088,128]{3,2,1,0:T(8,128)(2,1)} %norm.1.refs_0_.refs_1_.refs_2_.refs_3_.slab_ref, ...), custom_call_target="tpu_custom_call" | custom-call | flops 10737418240 | bytes 17825792 | tf_op jit(solution)/shard_map/weight_grad/pallas_call | solution.py:178
  51.5 12.5 %weight_grad.7 = bf16[4,2,640,128]{3,2,1,0:T(8,128)(2,1)} custom-call(s32[32]{0:T(128)} %constant.38.clone.table, s32[2]{0:T(128)} %pad_add_fusion.1.info, bf16[4,1024,640]{2,1,0:T(8,128)(2,1)} %bitcast.17, bf16[15,4,1088,128]{3,2,1,0:T(8,128)(2,1)} %norm.1.refs_0_.refs_1_.refs_2_.refs_3_.slab_ref, ...), custom_call_target="tpu_custom_call" | custom-call | flops 5368709120 | bytes 8912896 | tf_op jit(solution)/shard_map/weight_grad/pallas_call | solution.py:178
  65.1 11.2 %weight_grad.6 = bf16[4,2,640,128]{3,2,1,0:T(8,128)(2,1)} custom-call(s32[32]{0:T(128)} %constant.38.clone.table, s32[2]{0:T(128)} %pad_add_fusion.info, bf16[4,1024,640]{2,1,0:T(8,128)(2,1)} %bitcast.18, bf16[15,4,1088,128]{3,2,1,0:T(8,128)(2,1)} %norm.1.refs_0_.refs_1_.refs_2_.refs_3_.slab_ref, ...), custom_call_target="tpu_custom_call" | custom-call | flops 5368709120 | bytes 8912896 | tf_op jit(solution)/shard_map/weight_grad/pallas_call | solution.py:178
  76.3 17.9 %weight_grad.4 = bf16[8,2,640,128]{3,2,1,0:T(8,128)(2,1)} custom-call(s32[64]{0:T(128)} %constant.37.clone.table, s32[2]{0:T(128)} %pad_add_fusion.info, bf16[4,1024,640]{2,1,0:T(8,128)(2,1)} %bitcast.19, bf16[15,4,1088,128]{3,2,1,0:T(8,128)(2,1)} %norm.1.refs_0_.refs_1_.refs_2_.refs_3_.slab_ref, ...), custom_call_target="tpu_custom_call" | custom-call | flops 10737418240 | bytes 17825792 | tf_op jit(solution)/shard_map/weight_grad/pallas_call | solution.py:178
  94.3 2.5 %add_convert_fusion.6 = (bf16[1,2,640,128]{3,2,1,0:T(8,128)(2,1)}, bf16[1,2,640,128]{3,2,1,0:T(8,128)(2,1)}, bf16[1,2,640,128]{3,2,1,0:T(8,128)(2,1)S(1)}) fusion(bf16[4,2,640,128]{3,2,1,0:T(8,128)(2,1)} %collective-permute-done.9, bf16[4,2,640,128]{3,2,1,0:T(8,128)(2,1)S(1)} %copy-done.1), kind=kLoop, calls=%fused_computation.7 | loop fusion | flops 1966080 | bytes 2949120 | tf_op jit(solution)/shard_map/convert_element_type | solution.py:415
  96.8 1.1 collective-permute-start.10
  98.5 1.7 collective-permute-start.11
  100.9 2.8 %add_convert_fusion.3 = (bf16[2,2,640,128]{3,2,1,0:T(8,128)(2,1)S(1)}, bf16[2,2,640,128]{3,2,1,0:T(8,128)(2,1)}, bf16[2,2,640,128]{3,2,1,0:T(8,128)(2,1)S(1)}) fusion(bf16[8,2,640,128]{3,2,1,0:T(8,128)(2,1)S(1)} %copy-done, bf16[8,2,640,128]{3,2,1,0:T(8,128)(2,1)} %collective-permute-done), kind=kLoop, calls=%fused_computation.3 | loop fusion | flops 3932160 | bytes 5898240 | tf_op jit(solution)/shard_map/convert_element_type | solution.py:415
  103.7 1.5 collective-permute-start.5
  105.4 2.9 %collective-permute-done.10 = bf16[1,2,640,128]{3,2,1,0:T(8,128)(2,1)S(1)} collective-permute-done((bf16[1,2,640,128]{3,2,1,0:T(8,128)(2,1)S(1)}, bf16[1,2,640,128]{3,2,1,0:T(8,128)(2,1)S(1)}, u32[]{:S(2)}, u32[]{:S(2)}) %collective-permute-start.10) | collective-permute-done | bytes 327712 | tf_op jit(solution)/shard_map/ppermute | solution.py:395
  109.0 1.1 collective-permute-start.3
  110.1 23.8 %forward.2.refs_0_ = bf16[4,1024,640]{2,1,0:T(8,128)(2,1)} custom-call(s32[3]{0:T(128)} %pad_add_fusion.2.place, bf16[15,4,1088,128]{3,2,1,0:T(8,128)(2,1)} %norm.1.refs_0_.refs_1_.refs_2_.refs_3_.slab_ref, bf16[2880,640]{1,0:T(8,128)(2,1)} %own_ref.3, bf16[1440,640]{1,0:T(8,128)(2,1)} %collective-permute-done.1.near_ref, ...), custom_call_target="tpu_custom_call" | custom-call | flops 15099494400 | bytes 15728640 | tf_op jit(solution)/shard_map/forward/pallas_call | solution.py:260
  133.9 1.6 add_convert_fusion.5
  136.2 3.8 %collective-permute-start.13 = (bf16[1,16,24,128]{3,2,1,0:T(8,128)(2,1)S(1)}, bf16[1,16,24,128]{3,2,1,0:T(8,128)(2,1)S(1)}, u32[]{:S(2)}, u32[]{:S(2)}) collective-permute-start(bf16[1,16,24,128]{3,2,1,0:T(8,128)(2,1)S(1)} %get-tuple-element.52), channel_id=1, source_target_pairs={{0,24},{2,26},{4,28},{6,30},{8,16},{10,18},{12,20},{14,22},{16,8},... | collective-permute-start | bytes 294920 | tf_op jit(solution)/shard_map/ppermute | solution.py:388
  140.6 2.1 %collective-permute-done.3 = bf16[2,2,640,128]{3,2,1,0:T(8,128)(2,1)S(1)} collective-permute-done((bf16[2,2,640,128]{3,2,1,0:T(8,128)(2,1)S(1)}, bf16[2,2,640,128]{3,2,1,0:T(8,128)(2,1)S(1)}, u32[]{:S(2)}, u32[]{:S(2)}) %collective-permute-start.3) | collective-permute-done | bytes 655392 | tf_op jit(solution)/shard_map/ppermute | solution.py:395
  142.7 1.5 add_convert_fusion
  144.3 0.8 constant_dynamic-slice_fusion.4
  145.0 3.5 %collective-permute-start.6 = (bf16[2,16,24,128]{3,2,1,0:T(8,128)(2,1)S(1)}, bf16[2,16,24,128]{3,2,1,0:T(8,128)(2,1)S(1)}, u32[]{:S(2)}, u32[]{:S(2)}) collective-permute-start(bf16[2,16,24,128]{3,2,1,0:T(8,128)(2,1)S(1)} %get-tuple-element.48), channel_id=1, source_target_pairs={{0,24},{2,26},{4,28},{6,30},{8,16},{10,18},{12,20},{14,22},{16,8},... | collective-permute-start | bytes 589832 | tf_op jit(solution)/shard_map/ppermute | solution.py:388
  149.3 0.8 collective-permute-start.8
  150.1 23.8 %forward.3 = bf16[4,1024,640]{2,1,0:T(8,128)(2,1)} custom-call(s32[3]{0:T(128)} %pad_add_fusion.2.place, bf16[15,4,1088,128]{3,2,1,0:T(8,128)(2,1)} %norm.1.refs_0_.refs_1_.refs_2_.refs_3_.slab_ref, bf16[2880,640]{1,0:T(8,128)(2,1)} %own_ref.3, bf16[1440,640]{1,0:T(8,128)(2,1)} %collective-permute-done.1.near_ref, ...), custom_call_target="tpu_custom_call", output_to_operand_aliasing={{}: (5, {})} | custom-call | flops 15099494400 | bytes 15728640 | tf_op jit(solution)/shard_map/forward/pallas_call | solution.py:260
  174.8 2.5 %choose.1 = bf16[16,2,3,24,128]{4,3,2,1,0:T(8,128)(2,1)} custom-call(s32[16]{0:T(128)} %partner.1, bf16[2,16,24,128]{3,2,1,0:T(8,128)(2,1)} %get-tuple-element.29.refs_0_, bf16[2,16,24,128]{3,2,1,0:T(8,128)(2,1)} %copy-done.4, bf16[2,16,24,128]{3,2,1,0:T(8,128)(2,1)} %copy-done.5, bf16[2,16,24,128]{3,2,1,0:T(8,128)(2,1)} %copy-done.6, ...), custom_call_target="tpu_custom_call" | custom-call | tf_op jit(solution)/shard_map/choose/pallas_call | solution.py:310
  177.2 5.7 %all-to-all-start = ((bf16[16,2,3,24,128]{4,3,2,1,0:T(8,128)(2,1)}), bf16[16,2,3,24,128]{4,3,2,1,0:T(8,128)(2,1)S(1)}, u32[]{:S(2)}, u32[]{:S(2)}) async-start(bf16[16,2,3,24,128]{4,3,2,1,0:T(8,128)(2,1)} %choose.1), calls=%async_computation | async-start | bytes 1179648 | tf_op jit(solution)/shard_map/all_to_all | solution.py:454
  183.6 1.3 pad_add_fusion.3.info_ref
  184.8 13.7 %all-to-all-done.refs_0_ = bf16[16,2,3,24,128]{4,3,2,1,0:T(8,128)(2,1)S(1)} async-done(((bf16[16,2,3,24,128]{4,3,2,1,0:T(8,128)(2,1)}), bf16[16,2,3,24,128]{4,3,2,1,0:T(8,128)(2,1)S(1)}, u32[]{:S(2)}, u32[]{:S(2)}) %all-to-all-start) | async-done | bytes 589856 | tf_op jit(solution)/shard_map/all_to_all | solution.py:454
  198.5 0.8 copy-done.2
  199.3 4.9 %update.1 = (f32[1,2,40,2880]{3,2,1,0:T(8,128)}, f32[1,2,40,2880]{3,2,1,0:T(8,128)}, f32[1,2,40,2880]{3,2,1,0:T(8,128)}) custom-call(s32[4]{0:T(128)} %pad_add_fusion.3.info_ref, bf16[16,2,3,24,128]{4,3,2,1,0:T(8,128)(2,1)} %copy-done.2, f32[40,2880]{1,0:T(8,128)} %refs_1_.1, f32[40,2880]{1,0:T(8,128)} %refs_2_.1, f32[40,2880]{1,0:T(8,128)} %refs_3_.1, ...), custom_call_target="tpu_custom_call" | custom-call | tf_op jit(solution)/shard_map/update/pallas_call | solution.py:350
  (56 shorter events, 8.9 us)
Async XLA Ops:
  7.2 191.3 %all-gather.2.cloned.1.call-start = ((), (), s32[]{:S(2)}) async-start(), calls=%async_computation.1 | async-start | bytes 12011520 | tf_op jit(solution)/shard_map/all_gather | solution.py:398
  10.5 4.7 %copy-start.8 = (f32[640]{0:T(1024)S(1)}, f32[640]{0:T(1024)}, u32[]{:S(2)}) copy-start(f32[640]{0:T(1024)} %param.15) | copy-start | bytes 7684
  10.5 5.3 %copy-start.9 = (f32[640]{0:T(1024)S(1)}, f32[640]{0:T(1024)}, u32[]{:S(2)}) copy-start(f32[640]{0:T(1024)} %param.16) | copy-start | bytes 7684
  10.5 5.9 %copy-start.11 = (s32[16]{0:T(128)S(1)}, s32[16]{0:T(128)}, u32[]{:S(2)}) copy-start(s32[16]{0:T(128)} %param.21) | copy-start | bytes 196
  12.2 52.9 %collective-permute-start.1 = (bf16[1440,640]{1,0:T(8,128)(2,1)S(1)}, bf16[1440,640]{1,0:T(8,128)(2,1)}, u32[]{:S(2)}, u32[]{:S(2)}) collective-permute-start(bf16[1440,640]{1,0:T(8,128)(2,1)S(1)} %constant_dynamic-slice_fusion.8), channel_id=1, source_target_pairs={{0,1},{1,0},{2,3},{3,2},{4,5},{5,4},{6,7},{7,6},{8,9},{9,8},{10,11... | collective-permute-start | bytes 5529608 | tf_op jit(solution)/shard_map/ppermute | solution.py:391
  51.5 49.4 %collective-permute-start = (bf16[8,2,640,128]{3,2,1,0:T(8,128)(2,1)}, bf16[8,2,640,128]{3,2,1,0:T(8,128)(2,1)}, u32[]{:S(2)}, u32[]{:S(2)}) collective-permute-start(bf16[8,2,640,128]{3,2,1,0:T(8,128)(2,1)} %weight_grad.5), channel_id=1, source_target_pairs={{0,2},{2,0},{4,6},{6,4},{8,10},{10,8},{12,14},{14,12},{16,18},{18,... | collective-permute-start | bytes 7864328 | tf_op jit(solution)/shard_map/ppermute | solution.py:388
  64.0 30.2 %collective-permute-start.9 = (bf16[4,2,640,128]{3,2,1,0:T(8,128)(2,1)}, bf16[4,2,640,128]{3,2,1,0:T(8,128)(2,1)}, u32[]{:S(2)}, u32[]{:S(2)}) collective-permute-start(bf16[4,2,640,128]{3,2,1,0:T(8,128)(2,1)} %weight_grad.7), channel_id=1, source_target_pairs={{0,2},{2,0},{4,6},{6,4},{8,10},{10,8},{12,14},{14,12},{16,18},{18,... | collective-permute-start | bytes 3932168 | tf_op jit(solution)/shard_map/ppermute | solution.py:388
  65.1 35.8 %collective-permute-start.2 = (bf16[1440,640]{1,0:T(8,128)(2,1)}, bf16[1440,640]{1,0:T(8,128)(2,1)}, u32[]{:S(2)}, u32[]{:S(2)}) collective-permute-start(bf16[1440,640]{1,0:T(8,128)(2,1)} %collective-permute-done.1.near_ref), channel_id=1, source_target_pairs={{0,2},{2,0},{4,6},{6,4},{8,10},{10,8},{12,14},{14,12},{16,18},{18,... | collective-permute-start | bytes 5529608 | tf_op jit(solution)/shard_map/ppermute | solution.py:388
  76.3 17.9 %copy-start.1 = (bf16[4,2,640,128]{3,2,1,0:T(8,128)(2,1)S(1)}, bf16[4,2,640,128]{3,2,1,0:T(8,128)(2,1)}, u32[]{:S(2)}) copy-start(bf16[4,2,640,128]{3,2,1,0:T(8,128)(2,1)} %weight_grad.6) | copy-start | bytes 3932164
  94.3 6.6 %copy-start = (bf16[8,2,640,128]{3,2,1,0:T(8,128)(2,1)S(1)}, bf16[8,2,640,128]{3,2,1,0:T(8,128)(2,1)}, u32[]{:S(2)}) copy-start(bf16[8,2,640,128]{3,2,1,0:T(8,128)(2,1)} %weight_grad.4) | copy-start | bytes 7864324
  96.8 11.5 %collective-permute-start.10 = (bf16[1,2,640,128]{3,2,1,0:T(8,128)(2,1)S(1)}, bf16[1,2,640,128]{3,2,1,0:T(8,128)(2,1)S(1)}, u32[]{:S(2)}, u32[]{:S(2)}) collective-permute-start(bf16[1,2,640,128]{3,2,1,0:T(8,128)(2,1)S(1)} %get-tuple-element.45), channel_id=1, source_target_pairs={{0,5},{1,4},{2,7},{3,6},{4,1},{5,0},{6,3},{7,2},{8,13},{9,12},{10,... | collective-permute-start | bytes 983048 | tf_op jit(solution)/shard_map/ppermute | solution.py:395
  98.5 35.4 %collective-permute-start.11 = (bf16[1,2,640,128]{3,2,1,0:T(8,128)(2,1)}, bf16[1,2,640,128]{3,2,1,0:T(8,128)(2,1)}, u32[]{:S(2)}, u32[]{:S(2)}) collective-permute-start(bf16[1,2,640,128]{3,2,1,0:T(8,128)(2,1)} %get-tuple-element.44), channel_id=1, source_target_pairs={{0,1},{1,0},{2,3},{3,2},{4,5},{5,4},{6,7},{7,6},{8,9},{9,8},{10,11... | collective-permute-start | bytes 983048 | tf_op jit(solution)/shard_map/ppermute | solution.py:391
  100.2 33.7 %collective-permute-start.12 = (bf16[1,2,640,128]{3,2,1,0:T(8,128)(2,1)}, bf16[1,2,640,128]{3,2,1,0:T(8,128)(2,1)}, u32[]{:S(2)}, u32[]{:S(2)}) collective-permute-start(bf16[1,2,640,128]{3,2,1,0:T(8,128)(2,1)} %get-tuple-element.43), channel_id=1, source_target_pairs={{0,4},{2,6},{4,0},{6,2},{8,12},{10,14},{12,8},{14,10},{16,20},{18,... | collective-permute-start | bytes 983048 | tf_op jit(solution)/shard_map/ppermute | solution.py:388
  103.7 36.3 %collective-permute-start.5 = (bf16[2,2,640,128]{3,2,1,0:T(8,128)(2,1)}, bf16[2,2,640,128]{3,2,1,0:T(8,128)(2,1)S(1)}, u32[]{:S(2)}, u32[]{:S(2)}) collective-permute-start(bf16[2,2,640,128]{3,2,1,0:T(8,128)(2,1)} %get-tuple-element.41), channel_id=1, source_target_pairs={{0,4},{2,6},{4,0},{6,2},{8,12},{10,14},{12,8},{14,10},{16,20},{18,... | collective-permute-start | bytes 1966088 | tf_op jit(solution)/shard_map/ppermute | solution.py:388
  105.2 35.4 %collective-permute-start.4 = (bf16[2,2,640,128]{3,2,1,0:T(8,128)(2,1)S(1)}, bf16[2,2,640,128]{3,2,1,0:T(8,128)(2,1)S(1)}, u32[]{:S(2)}, u32[]{:S(2)}) collective-permute-start(bf16[2,2,640,128]{3,2,1,0:T(8,128)(2,1)S(1)} %get-tuple-element.42), channel_id=1, source_target_pairs={{0,1},{1,0},{2,3},{3,2},{4,5},{5,4},{6,7},{7,6},{8,9},{9,8},{10,11... | collective-permute-start | bytes 1966088 | tf_op jit(solution)/shard_map/ppermute | solution.py:391
  108.3 0.7 copy-start.3
  109.0 33.8 %collective-permute-start.3 = (bf16[2,2,640,128]{3,2,1,0:T(8,128)(2,1)S(1)}, bf16[2,2,640,128]{3,2,1,0:T(8,128)(2,1)S(1)}, u32[]{:S(2)}, u32[]{:S(2)}) collective-permute-start(bf16[2,2,640,128]{3,2,1,0:T(8,128)(2,1)S(1)} %get-tuple-element.40), channel_id=1, source_target_pairs={{0,5},{1,4},{2,7},{3,6},{4,1},{5,0},{6,3},{7,2},{8,13},{9,12},{10,... | collective-permute-start | bytes 1966088 | tf_op jit(solution)/shard_map/ppermute | solution.py:395
  136.2 12.4 %collective-permute-start.13 = (bf16[1,16,24,128]{3,2,1,0:T(8,128)(2,1)S(1)}, bf16[1,16,24,128]{3,2,1,0:T(8,128)(2,1)S(1)}, u32[]{:S(2)}, u32[]{:S(2)}) collective-permute-start(bf16[1,16,24,128]{3,2,1,0:T(8,128)(2,1)S(1)} %get-tuple-element.52), channel_id=1, source_target_pairs={{0,24},{2,26},{4,28},{6,30},{8,16},{10,18},{12,20},{14,22},{16,8},... | collective-permute-start | bytes 294920 | tf_op jit(solution)/shard_map/ppermute | solution.py:388
  140.0 33.9 %collective-permute-start.14 = (bf16[1,16,24,128]{3,2,1,0:T(8,128)(2,1)S(1)}, bf16[1,16,24,128]{3,2,1,0:T(8,128)(2,1)}, u32[]{:S(2)}, u32[]{:S(2)}) collective-permute-start(bf16[1,16,24,128]{3,2,1,0:T(8,128)(2,1)S(1)} %get-tuple-element.51), channel_id=1, source_target_pairs={{0,16},{2,18},{4,20},{6,22},{8,24},{10,26},{12,28},{14,30},{16,0},... | collective-permute-start | bytes 294920 | tf_op jit(solution)/shard_map/ppermute | solution.py:388
  140.0 33.9 %collective-permute-start.15 = (bf16[1,16,24,128]{3,2,1,0:T(8,128)(2,1)S(1)}, bf16[1,16,24,128]{3,2,1,0:T(8,128)(2,1)}, u32[]{:S(2)}, u32[]{:S(2)}) collective-permute-start(bf16[1,16,24,128]{3,2,1,0:T(8,128)(2,1)S(1)} %get-tuple-element.50), channel_id=1, source_target_pairs={{0,8},{2,10},{4,12},{6,14},{8,0},{10,2},{12,4},{14,6},{16,24},{18,... | collective-permute-start | bytes 294920 | tf_op jit(solution)/shard_map/ppermute | solution.py:388
  145.0 28.9 %collective-permute-start.6 = (bf16[2,16,24,128]{3,2,1,0:T(8,128)(2,1)S(1)}, bf16[2,16,24,128]{3,2,1,0:T(8,128)(2,1)S(1)}, u32[]{:S(2)}, u32[]{:S(2)}) collective-permute-start(bf16[2,16,24,128]{3,2,1,0:T(8,128)(2,1)S(1)} %get-tuple-element.48), channel_id=1, source_target_pairs={{0,24},{2,26},{4,28},{6,30},{8,16},{10,18},{12,20},{14,22},{16,8},... | collective-permute-start | bytes 589832 | tf_op jit(solution)/shard_map/ppermute | solution.py:388
  148.6 25.4 %collective-permute-start.7 = (bf16[2,16,24,128]{3,2,1,0:T(8,128)(2,1)S(1)}, bf16[2,16,24,128]{3,2,1,0:T(8,128)(2,1)S(1)}, u32[]{:S(2)}, u32[]{:S(2)}) collective-permute-start(bf16[2,16,24,128]{3,2,1,0:T(8,128)(2,1)S(1)} %get-tuple-element.47), channel_id=1, source_target_pairs={{0,16},{2,18},{4,20},{6,22},{8,24},{10,26},{12,28},{14,30},{16,0},... | collective-permute-start | bytes 589832 | tf_op jit(solution)/shard_map/ppermute | solution.py:388
  148.6 0.7 copy-start.7
  149.3 24.7 %collective-permute-start.8 = (bf16[2,16,24,128]{3,2,1,0:T(8,128)(2,1)S(1)}, bf16[2,16,24,128]{3,2,1,0:T(8,128)(2,1)S(1)}, u32[]{:S(2)}, u32[]{:S(2)}) collective-permute-start(bf16[2,16,24,128]{3,2,1,0:T(8,128)(2,1)S(1)} %get-tuple-element.46), channel_id=1, source_target_pairs={{0,8},{2,10},{4,12},{6,14},{8,0},{10,2},{12,4},{14,6},{16,24},{18,... | collective-permute-start | bytes 589832 | tf_op jit(solution)/shard_map/ppermute | solution.py:388
  173.9 0.7 copy-start.4
  174.0 0.7 copy-start.5
  174.0 0.8 copy-start.6
  174.8 8.2 %copy-start.10 = (s32[16]{0:T(128)S(1)}, s32[16]{0:T(128)}, u32[]{:S(2)}) copy-start(s32[16]{0:T(128)} %partner.1) | copy-start | bytes 196
  177.2 21.3 %all-to-all-start = ((bf16[16,2,3,24,128]{4,3,2,1,0:T(8,128)(2,1)}), bf16[16,2,3,24,128]{4,3,2,1,0:T(8,128)(2,1)S(1)}, u32[]{:S(2)}, u32[]{:S(2)}) async-start(bf16[16,2,3,24,128]{4,3,2,1,0:T(8,128)(2,1)} %choose.1), calls=%async_computation | async-start | bytes 1179648 | tf_op jit(solution)/shard_map/all_to_all | solution.py:454
  198.5 0.8 copy-start.2
Sparse Core Ops, SparseCore 0:
  10.7 95.6 all-gather.1

commit v2 on v1

v2 whole, which is shorter than its diff:
```python
import functools

import jax
import jax.numpy as jnp
import numpy as np
from jax import lax
from jax.experimental import pallas as pl
from jax.experimental.pallas import tpu as pltpu
from jax.sharding import PartitionSpec as P

GROUPS = 32
LANES = 128
MIB = 1024 * 1024
VMEM_LIMIT = 58 * MIB
PARTS = 3

beta_one = 0.9
beta_two = 0.999
step_count = 100.0
learn_rate = 0.01
weight_decay = 0.01
adam_eps = 1e-08
norm_eps = 1e-05
CHUNKS = (16, 8)
FORWARD = (2, 0, 1)

BF16 = jnp.bfloat16
F32 = jnp.float32


def adam(master, first_moment, second_moment, gradient):
    first_moment = beta_one * first_moment + (1.0 - beta_one) * gradient
    second_moment = beta_two * second_moment + (1.0 - beta_two) * gradient * gradient
    first_hat = first_moment / (1.0 - beta_one**step_count)
    second_hat = second_moment / (1.0 - beta_two**step_count)
    master = master - learn_rate * (
        first_hat / (jnp.sqrt(second_hat) + adam_eps) + weight_decay * master
    )
    return (master, first_moment, second_moment)


def norm_grad_kernel(
    inners, table, info, departing, lat_ref, gain_ref, bias_ref, member_ref, cot_hbm, slab_hbm, *refs
):
    images, rows, width, ch = lat_ref.shape
    tiles = ch // LANES
    cells = rows * width
    count = cells * (ch // GROUPS)
    halves, (slabs, cot, stage, cot_sem, slab_sems, stage_sems) = refs[:-6], refs[-6:]
    load = pltpu.make_async_copy(cot_hbm, cot, cot_sem)
    load.start()

    def group_means(totals):
        by_group = jnp.dot(
            jnp.concatenate(totals, axis=0),
            member_ref[...],
            precision=lax.Precision.HIGHEST,
            preferred_element_type=F32,
        )
        back = lax.dot_general(
            by_group,
            member_ref[...],
            (((1,), (1,)), ((), ())),
            precision=lax.Precision.HIGHEST,
            preferred_element_type=F32,
        )
        return jnp.sum(back.reshape(images, 8, ch), axis=1) * (1.0 / count)

    def fold(value):
        return jnp.sum(value.reshape(width // 8, 8, ch), axis=0)

    zero = jnp.zeros((8, ch), F32)

    def image_sum(image):
        def add_row(row, total):
            return total + fold(lat_ref[image, row].astype(F32))

        return lax.fori_loop(0, rows, add_row, zero, unroll=8)

    def image_square(image, mean):
        def add_row(row, total):
            centred = lat_ref[image, row].astype(F32) - mean
            return total + fold(centred * centred)

        return lax.fori_loop(0, rows, add_row, zero, unroll=8)

    means = group_means([image_sum(image) for image in range(images)])
    squares = [image_square(image, means[image : image + 1]) for image in range(images)]
    scales = lax.rsqrt(group_means(squares) + norm_eps) * gain_ref[...].reshape(1, ch)
    bias = bias_ref[...].reshape(1, ch)
    column = lax.broadcasted_iota(jnp.int32, (width, ch), 0)
    edge = jnp.zeros((width, LANES), BF16)
    stores = []
    for image in range(images):
        mean, scale = means[image : image + 1], scales[image : image + 1]

        def write_row(row, carry, image=image, mean=mean, scale=scale):
            half = 0.5 * ((lat_ref[image, row].astype(F32) - mean) * scale + bias)
            act = half + half * jnp.tanh(half)
            before = jnp.where(column == 0, 0.0, pltpu.roll(act, 1, 0))
            after = jnp.where(column == width - 1, 0.0, pltpu.roll(act, width - 1, 0))
            start = pl.multiple_of((row + 1) * width, width)
            for shift, value in enumerate((before, act, after)):
                value = value.astype(BF16)
                for tile in range(tiles):
                    slabs[shift * tiles + tile, image, pl.ds(start, width), :] = value[
                        :, tile * LANES : (tile + 1) * LANES
                    ]
            return carry

        for slab in range(3 * tiles):
            slabs[slab, image, 0:width, :] = edge
            slabs[slab, image, cells + width : cells + 2 * width, :] = edge
        lax.fori_loop(0, rows, write_row, 0, unroll=2)
        stores.append(pltpu.make_async_copy(slabs.at[:, image], slab_hbm.at[:, image], slab_sems.at[image]))
        stores[-1].start()

    load.wait()
    here = info[0]
    staying = (1 - departing[info[1]]).astype(F32)
    first = 0
    all_pairs = table.shape[0] // 4
    for chunk, inner in enumerate(inners):
        send_hbm, keep_hbm = halves[2 * chunk : 2 * chunk + 2]

        def finish(slot, keep_hbm=keep_hbm):
            pltpu.make_async_copy(stage.at[slot], keep_hbm.at[0], stage_sems.at[slot]).wait()

        def step(index, carry, first=first, inner=inner, send_hbm=send_hbm, keep_hbm=keep_hbm, finish=finish):
            slot = index % 2

            @pl.when(index >= 2)
            def _():
                finish(slot)

            total = None
            for image in range(images):
                sides = []
                for side in range(2):
                    at = 2 * side * all_pairs + first + index
                    row = pl.multiple_of(table[at + all_pairs], 32)
                    sides.append(slabs[table[at], image, pl.ds(row, cells), :])
                term = lax.dot_general(
                    cot[image],
                    jnp.concatenate(sides, axis=1),
                    (((0,), (0,)), ((), ())),
                    preferred_element_type=F32,
                )
                total = term if total is None else total + term
            value = (total * staying).astype(BF16)
            stage[slot, 0] = value[:, :LANES]
            stage[slot, 1] = value[:, LANES:]
            place = (index // inner) ^ here
            at = (place & 3) * inner + index % inner

            @pl.when(place >= 4)
            def _():
                pltpu.make_async_copy(stage.at[slot], send_hbm.at[at], stage_sems.at[slot]).start()

            @pl.when(place < 4)
            def _():
                pltpu.make_async_copy(stage.at[slot], keep_hbm.at[at], stage_sems.at[slot]).start()

            return carry

        lax.fori_loop(0, 8 * inner, step, 0)
        finish(0)
        finish(1)
        first += 8 * inner
    for store in stores:
        store.wait()


def norm_grad(latents, gain, bias, cot, table, info, departing, inners):
    images, rows, width, ch = latents.shape
    _, cells, out_ch = cot.shape
    member = np.zeros((ch, LANES), np.float32)
    member[np.arange(ch), np.arange(ch) // (ch // GROUPS)] = 1.0
    slabs = (3 * ch // LANES, images, (rows + 2) * width, LANES)
    halves = [
        jax.ShapeDtypeStruct((4 * inner, 2, out_ch, LANES), BF16) for inner in inners for _ in range(2)
    ]
    smem, vmem = pl.BlockSpec(memory_space=pltpu.SMEM), pl.BlockSpec(memory_space=pltpu.VMEM)
    anywhere = pl.BlockSpec(memory_space=pl.ANY)
    return pl.pallas_call(
        functools.partial(norm_grad_kernel, inners),
        in_specs=[smem, smem, smem, vmem, vmem, vmem, vmem, anywhere],
        out_specs=[anywhere] * (1 + len(halves)),
        out_shape=[jax.ShapeDtypeStruct(slabs, BF16)] + halves,
        scratch_shapes=[
            pltpu.VMEM(slabs, BF16),
            pltpu.VMEM(cot.shape, BF16),
            pltpu.VMEM((2, 2, out_ch, LANES), BF16),
            pltpu.SemaphoreType.DMA,
            pltpu.SemaphoreType.DMA((images,)),
            pltpu.SemaphoreType.DMA((2,)),
        ],
        compiler_params=pltpu.CompilerParams(vmem_limit_bytes=VMEM_LIMIT),
        cost_estimate=pl.CostEstimate(
            flops=32 * sum(inners) * LANES * images * cells * out_ch,
            bytes_accessed=10 * latents.size,
            transcendentals=latents.size,
        ),
        name="norm_grad",
    )(table, info, departing, latents, gain, bias, jnp.asarray(member), cot)


def tile_table(chunks, shards, cols, ch, width):
    per_tap = ch // LANES
    first, table = 0, [[], [], [], []]
    for tiles in chunks:
        inner_pairs = tiles // 8
        index = np.arange(8 * inner_pairs)
        bits, inner = index // inner_pairs, index % inner_pairs
        p_core, p_shard, p_x = bits >> 2, (bits >> 1) & 1, bits & 1
        for side in range(2):
            tile = first + p_core * (tiles // 2) + p_x * (tiles // 4) + 2 * inner + side
            tile = np.minimum((p_shard * cols) // LANES + tile, 9 * per_tap - 1)
            tap = tile // per_tap
            table[2 * side].append((tap % 3) * per_tap + tile % per_tap)
            table[2 * side + 1].append((tap // 3) * width)
        first += tiles
    return jnp.asarray(np.concatenate([np.concatenate(row) for row in table]), jnp.int32)


def forward_kernel(first, count, info, slab_hbm, own_ref, near_ref, far_ref, *refs):
    out_ref, weight, cols_ref, weight_sems, cols_sems = refs[-5:]
    slabs, _, padded, _ = slab_hbm.shape
    _, cells, out_ch = out_ref.shape
    width = (padded - cells) // 2
    step = pl.program_id(0)
    slot = step % 2

    def cols_copy(image, at):
        return pltpu.make_async_copy(slab_hbm.at[:, first + image], cols_ref.at[at], cols_sems.at[at])

    @pl.when(step == 0)
    def _():
        cols_copy(0, 0).start()
        copies = []
        for source, ref in enumerate((own_ref, near_ref, far_ref)):
            rows = ref.shape[0] // PARTS
            for part in range(PARTS):
                place = pl.multiple_of(info[2 + source] + part * rows, 16)
                copies.append(
                    pltpu.make_async_copy(
                        ref.at[pl.ds(part * rows, rows)],
                        weight.at[pl.ds(place, rows)],
                        weight_sems.at[source * PARTS + part],
                    )
                )
        for copy in copies:
            copy.start()
        if count > 1:
            cols_copy(1, 1).start()
        for copy in copies:
            copy.wait()

    cols_copy(0, slot).wait()
    block = 512
    for start in range(0, cells, block):
        cols = jnp.concatenate(
            [
                cols_ref[slot, slab, start + width * down : start + width * down + block, :]
                for down in range(3)
                for slab in range(slabs)
            ],
            axis=1,
        )
        total = lax.dot_general(
            weight[...], cols, (((0,), (1,)), ((), ())), preferred_element_type=F32
        )
        out_ref[0, start : start + block, :] = total.astype(BF16).T
    if count > 2:

        @pl.when(step + 2 < count)
        def _():
            cols_copy(step + 2, slot).start()


def forward(slabs, own, near, far, info, width, first, count, earlier=None):
    slab_count, images, padded, _ = slabs.shape
    cells = padded - 2 * width
    out_ch = own.shape[1]
    rows = own.shape[0] + near.shape[0] + far.shape[0]
    extra = () if earlier is None else (earlier,)
    return pl.pallas_call(
        functools.partial(forward_kernel, first, count),
        grid_spec=pltpu.PrefetchScalarGridSpec(
            num_scalar_prefetch=1,
            grid=(count,),
            in_specs=[pl.BlockSpec(memory_space=pl.ANY)] * (4 + len(extra)),
            out_specs=pl.BlockSpec((1, cells, out_ch), lambda i, *_: (i + first, 0, 0)),
            scratch_shapes=[
                pltpu.VMEM((rows, out_ch), BF16),
                pltpu.VMEM((2, slab_count, padded, LANES), BF16),
                pltpu.SemaphoreType.DMA((3 * PARTS,)),
                pltpu.SemaphoreType.DMA((2,)),
            ],
        ),
        out_shape=jax.ShapeDtypeStruct((images, cells, out_ch), BF16),
        input_output_aliases={5: 0} if extra else {},
        compiler_params=pltpu.CompilerParams(vmem_limit_bytes=VMEM_LIMIT),
        cost_estimate=pl.CostEstimate(
            flops=2 * count * cells * rows * out_ch,
            bytes_accessed=2 * (rows * out_ch + slab_count * count * padded * LANES),
            transcendentals=0,
        ),
        name="forward",
    )(info, slabs, own, near, far, *extra)


def pack_kernel(master_ref, one_ref, two_ref, out_ref):
    parts = [master_ref[...], one_ref[...], two_ref[...]]
    spare = out_ref.shape[0] - 3 * master_ref.shape[0]
    if spare:
        parts.append(jnp.zeros((spare, master_ref.shape[1]), F32))
    out_ref[...] = jnp.concatenate(parts, axis=0).astype(BF16)


def pack(master, one, two, reps):
    rows, cols = master.shape
    padded = -(-3 * rows // (8 * reps)) * 8 * reps
    return pl.pallas_call(
        pack_kernel,
        out_shape=jax.ShapeDtypeStruct((padded, cols), BF16),
        compiler_params=pltpu.CompilerParams(vmem_limit_bytes=VMEM_LIMIT),
        name="pack",
    )(master, one, two)


def route_kernel(partner, in_ref, out_ref):
    for rep in range(out_ref.shape[0]):
        out_ref[rep] = in_ref[partner[rep]]


def route(pieces, partner):
    return pl.pallas_call(
        route_kernel,
        in_specs=[pl.BlockSpec(memory_space=pltpu.SMEM), pl.BlockSpec(memory_space=pltpu.VMEM)],
        out_specs=pl.BlockSpec(memory_space=pltpu.VMEM),
        out_shape=jax.ShapeDtypeStruct(pieces.shape, BF16),
        compiler_params=pltpu.CompilerParams(vmem_limit_bytes=VMEM_LIMIT),
        name="route",
    )(partner, pieces)


def choose_kernel(partner, *refs):
    out_ref = refs[-1]
    reps = out_ref.shape[0]
    at = 0
    for group in range(0, len(refs) - 1, 4):
        total = refs[group][...].astype(F32)
        for ref in refs[group + 1 : group + 4]:
            total = total + ref[...].astype(F32)
        total = total.astype(BF16)
        tiles = total.shape[0]
        for rep in range(reps):
            out_ref[rep, 0, at : at + tiles] = total[:, rep]
        at += tiles
    for rep in range(reps):
        out_ref[rep, 1] = out_ref[partner[rep], 0]


def choose(parts, partner):
    _, reps, rows, lanes = parts[0].shape
    tiles = sum(part.shape[0] for part in parts) // 4
    return pl.pallas_call(
        choose_kernel,
        in_specs=[pl.BlockSpec(memory_space=pltpu.SMEM)]
        + [pl.BlockSpec(memory_space=pltpu.VMEM)] * len(parts),
        out_specs=pl.BlockSpec(memory_space=pltpu.VMEM),
        out_shape=jax.ShapeDtypeStruct((reps, 2, tiles, rows, lanes), BF16),
        compiler_params=pltpu.CompilerParams(vmem_limit_bytes=VMEM_LIMIT),
        name="choose",
    )(partner, *parts)


def update_kernel(source, images, info, departing, grad_ref, master_ref, one_ref, two_ref, mate_ref, *refs):
    outs, grad = refs[:3], refs[3]
    block_rows, cols = master_ref.shape
    high = grad_ref.shape[3]
    staying = (1 - departing[info[1]]).astype(F32)
    odd = info[5] != 0
    mates = mate_ref[...].astype(F32)
    for block in range(2):
        for tile, (upper, lower, inner) in enumerate(source):
            span = slice(tile * LANES, (tile + 1) * LANES)
            top = grad_ref[upper, block, inner].astype(F32)
            low = grad_ref[lower, block, inner].astype(F32)
            grad[0:high, span] = top
            grad[high:block_rows, span] = low[2 * high - block_rows : high]
        gradient = jnp.where(odd, grad[:, LANES // 2 : LANES // 2 + cols], grad[:, 0:cols])
        gradient = gradient / images
        if block == 0:
            state = (master_ref[...], one_ref[...], two_ref[...])
        else:
            state = tuple(mates[k * block_rows : (k + 1) * block_rows] for k in range(3))
        for out, value in zip(outs, adam(*state, gradient)):
            out[0, block] = value * staying


def update(received, source, images, master, one, two, mates, info, departing):
    block_rows, cols = master.shape
    out = jax.ShapeDtypeStruct((1, 2, block_rows, cols), F32)
    whole = [pl.BlockSpec(received.shape, lambda i, *_: (0,) * received.ndim)]
    state = [pl.BlockSpec((block_rows, cols), lambda i, *_: (0, 0))] * 3
    return pl.pallas_call(
        functools.partial(update_kernel, source, images),
        grid_spec=pltpu.PrefetchScalarGridSpec(
            num_scalar_prefetch=2,
            grid=(1,),
            in_specs=whole
            + state
            + [pl.BlockSpec(mates.shape, lambda i, *_: (0, 0))],
            out_specs=[pl.BlockSpec((1, 2, block_rows, cols), lambda i, *_: (0, 0, 0, 0))] * 3,
            scratch_shapes=[pltpu.VMEM((block_rows, len(source) * LANES), F32)],
        ),
        out_shape=[out] * 3,
        compiler_params=pltpu.CompilerParams(vmem_limit_bytes=VMEM_LIMIT),
        name="update",
    )(info, departing, received, master, one, two, mates)


def per_device(
    latents,
    cotangent,
    gn_gain,
    gn_bias,
    conv_weight,
    master,
    moment_one,
    moment_two,
    departing,
    partner,
):
    images, rows, width, ch = latents.shape
    reps, shards = lax.axis_size("rep"), lax.axis_size("shard")
    out_ch = conv_weight.shape[1]
    block_rows, cols = master.shape
    rep, shard = lax.axis_index("rep"), lax.axis_index("shard")
    core, col_x, low_z, high_z = rep & 1, (rep >> 1) & 1, (rep >> 2) & 1, rep >> 3

    def swap_rep(value, bits):
        return lax.ppermute(value, "rep", [(i, i ^ bits) for i in range(reps)])

    def swap_shard(value):
        return lax.ppermute(value, "shard", [(0, 1), (1, 0)])

    def swap_both(value, bits):
        pairs = [(i, i ^ (2 * bits + 1)) for i in range(2 * reps)]
        return lax.ppermute(value, ("rep", "shard"), pairs)

    own_rows = conv_weight.shape[0]
    part_rows = own_rows // 2
    near = swap_shard(lax.dynamic_slice_in_dim(conv_weight, core * part_rows, part_rows, 0))

    here = 4 * core + 2 * shard + col_x
    missing = (1 - shard) * own_rows
    info = jnp.stack(
        [
            here,
            rep,
            shard * own_rows,
            missing + core * part_rows,
            missing + (1 - core) * part_rows,
            shard,
        ]
    ).astype(jnp.int32)

    def add(*terms):
        total = terms[0].astype(F32)
        for term in terms[1:]:
            total = total + term.astype(F32)
        return total.astype(BF16)

    conv, done = None, 0

    def convolve(count):
        nonlocal conv, done
        if count:
            conv = forward(slabs, conv_weight, near, far, info, width, done, count, conv)
            done += count

    state = pack(master, moment_one, moment_two, reps)
    spread = lax.all_to_all(state, "rep", 0, 0, tiled=True)

    cot = cotangent.reshape(images, rows * width, out_ch)
    inners = [tiles // 8 for tiles in CHUNKS]
    table = tile_table(CHUNKS, shards, cols, ch, width)
    slabs, *halves = norm_grad(latents, gn_gain, gn_bias, cot, table, info, departing, inners)
    sends, keeps = halves[0::2], halves[1::2]
    sends, near, spread = lax.optimization_barrier((sends, near, spread))
    far = swap_rep(near, 1)

    others = [swap_rep(send, 1) for send in sends]
    routed = route(spread.reshape(reps, -1, cols), partner)
    mates = lax.all_to_all(routed.reshape(-1, cols), "rep", 0, 0, tiled=True)
    mine, arriving = [], []
    for inner, keep, other in zip(inners, keeps, others):
        if mine:
            other, quarter = lax.optimization_barrier((other, quarter))
            mine[-1] = quarter[0]
        quarter = [add(keep[k * inner : (k + 1) * inner], other[k * inner : (k + 1) * inner]) for k in range(4)]
        mine.append(quarter[0])
        arriving.append((swap_both(quarter[3], 2), swap_shard(quarter[2]), swap_rep(quarter[1], 2)))

    near, far, mine[-1] = lax.optimization_barrier((near, far, mine[-1]))

    high = -(-block_rows // 16) * 8
    pieces, source, held_before = [], [], 0
    for chunk, tiles in enumerate(CHUNKS):
        arrived = arriving[chunk]
        if FORWARD[chunk]:
            convolve(FORWARD[chunk])
            arrived, conv = lax.optimization_barrier((arrived, conv))
        if chunk == 0:
            arrived, mates = lax.optimization_barrier((arrived, mates))
        else:
            arrived, pieces[-1] = lax.optimization_barrier((arrived, pieces[-1]))
        plane = add(mine[chunk], *arrived).reshape(tiles // 4, reps, block_rows, LANES)
        held = tiles // 8

        def part(d_high, d_low):
            start = (held * (low_z ^ d_low), 0, (block_rows - high) * (high_z ^ d_high), 0)
            return lax.dynamic_slice(plane, start, (held, reps, high, LANES))

        pieces += [part(0, 0), swap_rep(part(1, 1), 12), swap_rep(part(1, 0), 8), swap_rep(part(0, 1), 4)]
        for tile in range(tiles):
            at = 4 * ((tile % (tiles // 4)) // held) + 2 * ((tile % (tiles // 2)) // (tiles // 4))
            at += tile // (tiles // 2)
            source.append((at, at + 8, held_before + tile % held))
        held_before += held
    source = source[: -(-cols // LANES)]
    if FORWARD[-1]:
        convolve(FORWARD[-1])
        pieces, conv = lax.optimization_barrier((pieces, conv))
    received = lax.all_to_all(choose(pieces, partner), "rep", 0, 0, tiled=True)
    if done < images:
        convolve(images - done)
        received, conv = lax.optimization_barrier((received, conv))
    count = images * shards * (reps // 2)
    new = update(received, source, count, master, moment_one, moment_two, mates, info, departing)
    return (conv.reshape(images, rows, width, out_ch), *new)


def gather_taps(padded, row_count, col_count):
    taps = [
        padded[:, row_off : row_off + row_count, col_off : col_off + col_count, :]
        for row_off in range(3)
        for col_off in range(3)
    ]
    return jnp.concatenate(taps, axis=3)


def group_totals(values, image_count, group_width):
    return jnp.sum(values, axis=(1, 2)).reshape(image_count, GROUPS, group_width).sum(-1)


def fold_states(stacked, partner_index):
    running = jnp.zeros_like(stacked)
    pieces_in = lax.all_gather(stacked.astype(jnp.bfloat16), "rep", axis=1, tiled=True).astype(
        jnp.float32
    )
    block_cols = running.shape[1]
    row_ids = lax.iota(jnp.int32, pieces_in.shape[1])
    slot_ids = lax.iota(jnp.int32, block_cols)
    select = (
        (row_ids[None, :] // block_cols == partner_index)
        & (row_ids[None, :] % block_cols == slot_ids[:, None])
    ).astype(jnp.float32)
    return running + jnp.einsum("br,srk->sbk", select, pieces_in, precision=lax.Precision.HIGHEST)


def per_device_any(
    latents,
    cotangent,
    gn_gain,
    gn_bias,
    conv_weight,
    master,
    moment_one,
    moment_two,
    departing,
    partner,
):
    image_count, row_count, col_count, channels = latents.shape
    group_width = channels // GROUPS
    pixel_count = row_count * col_count * group_width
    float_in = latents.astype(jnp.float32)
    group_mean = group_totals(float_in, image_count, group_width) / pixel_count
    centred = float_in - jnp.repeat(group_mean, group_width, axis=1)[:, None, None, :]
    variance = group_totals(centred * centred, image_count, group_width) / pixel_count
    inverse = jnp.repeat(lax.rsqrt(variance + norm_eps), group_width, axis=1)[:, None, None, :]
    activated = jax.nn.silu(centred * inverse * gn_gain + gn_bias).astype(jnp.bfloat16)
    padded = jnp.pad(activated, ((0, 0), (1, 1), (1, 1), (0, 0)))
    patches = gather_taps(padded, row_count, col_count).reshape(-1, 9 * channels)
    out_cols = conv_weight.shape[1]
    columns = patches
    forward = jnp.dot(
        columns,
        lax.all_gather(conv_weight, "shard", axis=0, tiled=True),
        preferred_element_type=jnp.float32,
    )
    conv_out = forward.astype(jnp.bfloat16).reshape(image_count, row_count, col_count, out_cols)
    cot_flat = cotangent.reshape(-1, cotangent.shape[3])
    columns = patches
    grad_rows = lax.psum_scatter(
        lax.dot_general(
            columns, cot_flat, (((0,), (0,)), ((), ())), preferred_element_type=jnp.float32
        ).astype(jnp.bfloat16),
        "shard",
        scatter_dimension=0,
        tiled=True,
    ).astype(jnp.float32)
    my_index = lax.axis_index("rep")
    staying = (1 - departing[my_index]).astype(jnp.float32)
    partner_index = partner[my_index]
    images = image_count * lax.axis_size("shard") * (lax.axis_size("rep") // 2)
    owned = (
        lax.psum_scatter(
            (grad_rows * staying).astype(jnp.bfloat16), "rep", scatter_dimension=1, tiled=True
        ).astype(jnp.float32)
        / images
    )
    own_state = adam(master, moment_one, moment_two, owned.T)
    received = fold_states(jnp.stack(own_state), partner_index)
    mate_state = (received[0], received[1], received[2])

    def arrange(own_part, mate_part):
        return (jnp.stack([own_part, mate_part]) * staying)[None]

    return (
        conv_out,
        arrange(own_state[0], mate_state[0]),
        arrange(own_state[1], mate_state[1]),
        arrange(own_state[2], mate_state[2]),
    )


def solution(mesh):
    paired = mesh.shape["shard"] == 2 and mesh.shape["rep"] == 16
    return jax.shard_map(
        per_device if paired else per_device_any,
        mesh=mesh,
        in_specs=(
            P(("rep", "shard"), None, None, None),
            P(("rep", "shard"), None, None, None),
            P(),
            P(),
            P("shard", None),
            P("rep", "shard"),
            P("rep", "shard"),
            P("rep", "shard"),
            P(),
            P(),
        ),
        out_specs=(
            P(("rep", "shard"), None, None, None),
            P("rep", None, None, "shard"),
            P("rep", None, None, "shard"),
            P("rep", None, None, "shard"),
        ),
        check_vma=False,
    )
```

time: 212 us -> 181 us (0.85)
  starting transfers between devices: 24.4 us -> 40.2 us
  Pallas kernels: 130 us -> 115 us
  between operations: 14.9 us -> 0.93 us
  waiting for transfers between devices: 18.8 us -> 7.8 us
  other arithmetic: 14.7 us -> 8.97 us
    pallas_call x8 -> x7, Pallas kernels: 127 us -> 112 us  [the longest x1 52.6 us: norm_grad(): pl.pallas_call(functools.partial(norm_grad_kernel, inners), in_specs=[sme...]
    all_to_all x1, waiting for transfers between devices: 13.7 us -> 1.41 us  [per_device(): received = lax.all_to_all(choose(pieces, partner), 'rep', 0, 0, tiled=True)]
    all_to_all x0 -> x2, starting transfers between devices: none -> 11.8 us  [the longest x1 5.91 us: per_device(): spread = lax.all_to_all(state, 'rep', 0, 0, tiled=True)]
    another operation x7 -> x0, other arithmetic: 6.23 us -> none  [the longest x3 3.21 us: per_device(): state = jnp.stack([master, moment_one, moment_two]).astype(BF16)]
    ppermute x11, waiting for transfers between devices: 0.03 us -> 5.39 us  [swap_rep(): return lax.ppermute(value, 'rep', [(i, i ^ bits) for i in range(reps)])]
    ppermute x2, waiting for transfers between devices: 5.01 us -> 0.12 us  [swap_both(): return lax.ppermute(value, ('rep', 'shard'), pairs)]
  transfers between devices with their start and end apart: 18 -> 19, of which waited for: 3 -> 5; matrix products, arithmetic and copies ran while one was open for 8% -> 6% of each run, Pallas kernels for 59% -> 60%
where the time goes in v2:
time: 181 us; the launch traced here: 180 us
  Pallas kernels  115 us (64%)
  starting transfers between devices  40.2 us (22%)
  other arithmetic  8.97 us (5%)
  waiting for transfers between devices  7.8 us (4%)
  local copies, waits for them, and re-layouts  7.52 us (4%)
    pallas_call x1, Pallas kernels, norm_grad(): pl.pallas_call(functools.partial(norm_grad_kernel, inners), in_specs=[sme...  52.6 us
    pallas_call x3, Pallas kernels, forward(): pl.pallas_call(functools.partial(forward_kernel, first, count), grid_spec...  50.6 us
    ppermute x11, starting transfers between devices, swap_rep(): return lax.ppermute(value, 'rep', [(i, i ^ bits) for i in range(reps)])  13.3 us
    convert_element_type x4, other arithmetic, add(): return total.astype(BF16)  8.97 us
    ppermute x3, starting transfers between devices, swap_shard(): return lax.ppermute(value, 'shard', [(0, 1), (1, 0)])  6 us
    all_to_all x1, starting transfers between devices, per_device(): spread = lax.all_to_all(state, 'rep', 0, 0, tiled=True)  5.91 us
    all_to_all x1, starting transfers between devices, per_device(): mates = lax.all_to_all(routed.reshape(-1, cols), 'rep', 0, 0, tiled=True)  5.84 us
    all_to_all x1, starting transfers between devices, per_device(): received = lax.all_to_all(choose(pieces, partner), 'rep', 0, 0, tiled=True)  5.42 us
  transfers between devices with their start and end apart: 19, of which 5 were waited for; matrix products, arithmetic and copies ran while one was open for 6% of the time, Pallas kernels for 60%

profile of v2, /device:TPU:0, one launch (start us, length us, event | category | flops | bytes accessed | tf_op | source)
XLA Modules:
  0.0 180.3 jit_solution(13613512701370339228)
XLA Ops:
  0.6 2.9 %constant_dynamic-slice_fusion.8 = bf16[1440,640]{1,0:T(8,128)(2,1)} fusion(bf16[2880,640]{1,0:T(8,128)(2,1)} %own_ref.5, s32[]{:T(128)S(6)} %select_n.14), kind=kLoop, calls=%fused_computation.18 | loop fusion | bytes 3686404 | tf_op jit(solution)/shard_map/dynamic_slice | solution.py:456
  3.5 3.0 %collective-permute-start = (bf16[1440,640]{1,0:T(8,128)(2,1)}, bf16[1440,640]{1,0:T(8,128)(2,1)S(1)}, u32[]{:S(2)}, u32[]{:S(2)}) collective-permute-start(bf16[1440,640]{1,0:T(8,128)(2,1)} %constant_dynamic-slice_fusion.8), channel_id=1, source_target_pairs={{0,1},{1,0},{2,3},{3,2},{4,5},{5,4},{6,7},{7,6},{8,9},{9,8},{10,11... | collective-permute-start | bytes 5529608 | tf_op jit(solution)/shard_map/ppermute | solution.py:448
  6.5 2.2 %pack.1 = bf16[128,2880]{1,0:T(8,128)(2,1)} custom-call(f32[40,2880]{1,0:T(8,128)} %master_ref.3, f32[40,2880]{1,0:T(8,128)} %one_ref.3, f32[40,2880]{1,0:T(8,128)} %two_ref.3), custom_call_target="tpu_custom_call" | custom-call | tf_op jit(solution)/shard_map/pack/pallas_call | solution.py:324
  8.8 5.9 %all-to-all-start = ((bf16[16,8,2880]{2,1,0:T(8,128)(2,1)}), bf16[16,8,2880]{2,1,0:T(8,128)(2,1)S(1)}, u32[]{:S(2)}, u32[]{:S(2)}) async-start(bf16[16,8,2880]{2,1,0:T(8,128)(2,1)} %bitcast.17), calls=%async_computation | async-start | bytes 1507328 | tf_op jit(solution)/shard_map/all_to_all | solution.py:486
  15.4 52.6 %norm_grad.1 = (bf16[15,4,1088,128]{3,2,1,0:T(8,128)(2,1)}, bf16[8,2,640,128]{3,2,1,0:T(8,128)(2,1)}, bf16[8,2,640,128]{3,2,1,0:T(8,128)(2,1)}, bf16[4,2,640,128]{3,2,1,0:T(8,128)(2,1)}, bf16[4,2,640,128]{3,2,1,0:T(8,128)(2,1)}) custom-call(s32[96]{0:T(128)} %constant.30.clone.table, s32[6]{0:T(128)} %stack.27.info, s32[16]{0:T(128)} %departing.3, ...), custom_call_target="tpu_custom_call" | custom-call | flops 32212254720 | bytes 26214400 | tf_op jit(solution)/shard_map/norm_grad/pallas_call | solution.py:185
  69.1 2.1 %route.1 = bf16[16,8,2880]{2,1,0:T(8,128)(2,1)} custom-call(s32[16]{0:T(128)} %partner.3, bf16[16,8,2880]{2,1,0:T(8,128)(2,1)} %copy-done.2), custom_call_target="tpu_custom_call" | custom-call | tf_op jit(solution)/shard_map/route/pallas_call | solution.py:338
  71.1 5.8 %all-to-all-start.1 = ((bf16[16,8,2880]{2,1,0:T(8,128)(2,1)}), bf16[16,8,2880]{2,1,0:T(8,128)(2,1)S(1)}, u32[]{:S(2)}, u32[]{:S(2)}) async-start(bf16[16,8,2880]{2,1,0:T(8,128)(2,1)} %route.1), calls=%async_computation.1 | async-start | bytes 1507328 | tf_op jit(solution)/shard_map/all_to_all | solution.py:498
  77.0 4.1 %add_convert_fusion.4 = (bf16[2,2,640,128]{3,2,1,0:T(8,128)(2,1)S(1)}, bf16[2,2,640,128]{3,2,1,0:T(8,128)(2,1)}, bf16[2,2,640,128]{3,2,1,0:T(8,128)(2,1)S(1)}, bf16[2,2,640,128]{3,2,1,0:T(8,128)(2,1)S(1)}) fusion(bf16[8,2,640,128]{3,2,1,0:T(8,128)(2,1)} %collective-permute-done.2, bf16[8,2,640,128]{3,2,1,0:T(8,128)(2,1)} %get-tuple-element.47), kind=kLoop, calls=%fused_computation.4 | loop fusion | flops 5242880 | bytes 7864320 | tf_op jit(solution)/shard_map/convert_element_type | solution.py:475
  81.1 1.9 %collective-permute-start.3 = (bf16[2,2,640,128]{3,2,1,0:T(8,128)(2,1)}, bf16[2,2,640,128]{3,2,1,0:T(8,128)(2,1)S(1)}, u32[]{:S(2)}, u32[]{:S(2)}) collective-permute-start(bf16[2,2,640,128]{3,2,1,0:T(8,128)(2,1)} %get-tuple-element.85), channel_id=1, source_target_pairs={{0,5},{1,4},{2,7},{3,6},{4,1},{5,0},{6,3},{7,2},{8,13},{9,12},{10,... | collective-permute-start | bytes 1966088 | tf_op jit(solution)/shard_map/ppermute | solution.py:452
  82.9 1.5 collective-permute-start.4
  84.6 2.6 %add_convert_fusion.6 = (bf16[1,2,640,128]{3,2,1,0:T(8,128)(2,1)}, bf16[1,2,640,128]{3,2,1,0:T(8,128)(2,1)}, bf16[1,2,640,128]{3,2,1,0:T(8,128)(2,1)}, bf16[1,2,640,128]{3,2,1,0:T(8,128)(2,1)}) fusion(bf16[4,2,640,128]{3,2,1,0:T(8,128)(2,1)} %collective-permute-done.1, bf16[4,2,640,128]{3,2,1,0:T(8,128)(2,1)S(1)} %copy-done.4), kind=kLoop, calls=%fused_computation.6 | loop fusion | flops 2621440 | bytes 3932160 | tf_op jit(solution)/shard_map/convert_element_type | solution.py:475
  87.2 1.9 %collective-permute-start.9 = (bf16[1,2,640,128]{3,2,1,0:T(8,128)(2,1)}, bf16[1,2,640,128]{3,2,1,0:T(8,128)(2,1)S(1)}, u32[]{:S(2)}, u32[]{:S(2)}) collective-permute-start(bf16[1,2,640,128]{3,2,1,0:T(8,128)(2,1)} %get-tuple-element.90), channel_id=1, source_target_pairs={{0,5},{1,4},{2,7},{3,6},{4,1},{5,0},{6,3},{7,2},{8,13},{9,12},{10,... | collective-permute-start | bytes 983048 | tf_op jit(solution)/shard_map/ppermute | solution.py:452
  89.0 1.5 collective-permute-start.10
  90.6 22.3 %forward.3.refs_0_ = bf16[4,1024,640]{2,1,0:T(8,128)(2,1)} custom-call(s32[6]{0:T(128)} %stack.27.info, bf16[15,4,1088,128]{3,2,1,0:T(8,128)(2,1)} %get-tuple-element.50.slab_hbm, bf16[2880,640]{1,0:T(8,128)(2,1)} %own_ref.5, bf16[1440,640]{1,0:T(8,128)(2,1)} %copy-done, bf16[1440,640]{1,0:T(8,128)(2,1)} %collective-permute-done.6.far_ref), custom_call_target="tpu_custom_call" | custom-call | flops 15099494400 | bytes 15728640 | tf_op jit(solution)/shard_map/forward/pallas_call | solution.py:287
  113.1 0.9 collective-permute-done.4
  114.0 0.8 copy-done.7
  114.8 2.4 %collective-permute-done.5 = bf16[2,2,640,128]{3,2,1,0:T(8,128)(2,1)} collective-permute-done((bf16[2,2,640,128]{3,2,1,0:T(8,128)(2,1)S(1)}, bf16[2,2,640,128]{3,2,1,0:T(8,128)(2,1)}, u32[]{:S(2)}, u32[]{:S(2)}) %collective-permute-start.5) | collective-permute-done | bytes 655392 | tf_op jit(solution)/shard_map/ppermute | solution.py:445
  117.2 2.1 %add_convert_fusion = bf16[2,2,640,128]{3,2,1,0:T(8,128)(2,1)S(1)} fusion(bf16[2,2,640,128]{3,2,1,0:T(8,128)(2,1)} %collective-permute-done.5, bf16[2,2,640,128]{3,2,1,0:T(8,128)(2,1)} %copy-done.7, bf16[2,2,640,128]{3,2,1,0:T(8,128)(2,1)} %copy-done.6, bf16[2,2,640,128]{3,2,1,0:T(8,128)(2,1)S(1)} %get-tuple-element.49), kind=kLoop, calls=%fused_computation | loop fusion | flops 2621440 | bytes 3276800 | tf_op jit(solution)/shard_map/convert_element_type | solution.py:475
  119.3 0.8 constant_dynamic-slice_fusion.4
  120.1 2.5 %collective-permute-start.12 = (bf16[2,16,24,128]{3,2,1,0:T(8,128)(2,1)S(1)}, bf16[2,16,24,128]{3,2,1,0:T(8,128)(2,1)S(1)}, u32[]{:S(2)}, u32[]{:S(2)}) collective-permute-start(bf16[2,16,24,128]{3,2,1,0:T(8,128)(2,1)S(1)} %get-tuple-element.92), channel_id=1, source_target_pairs={{0,8},{2,10},{4,12},{6,14},{8,0},{10,2},{12,4},{14,6},{16,24},{18,... | collective-permute-start | bytes 589832 | tf_op jit(solution)/shard_map/ppermute | solution.py:445
  122.6 1.9 %collective-permute-start.7 = (bf16[2,16,24,128]{3,2,1,0:T(8,128)(2,1)S(1)}, bf16[2,16,24,128]{3,2,1,0:T(8,128)(2,1)S(1)}, u32[]{:S(2)}, u32[]{:S(2)}) collective-permute-start(bf16[2,16,24,128]{3,2,1,0:T(8,128)(2,1)S(1)} %get-tuple-element.94), channel_id=1, source_target_pairs={{0,24},{2,26},{4,28},{6,30},{8,16},{10,18},{12,20},{14,22},{16,8},... | collective-permute-start | bytes 589832 | tf_op jit(solution)/shard_map/ppermute | solution.py:445
  124.6 3.3 %collective-permute-start.8 = (bf16[2,16,24,128]{3,2,1,0:T(8,128)(2,1)S(1)}, bf16[2,16,24,128]{3,2,1,0:T(8,128)(2,1)S(1)}, u32[]{:S(2)}, u32[]{:S(2)}) collective-permute-start(bf16[2,16,24,128]{3,2,1,0:T(8,128)(2,1)S(1)} %get-tuple-element.93), channel_id=1, source_target_pairs={{0,16},{2,18},{4,20},{6,22},{8,24},{10,26},{12,28},{14,30},{16,0},... | collective-permute-start | bytes 589832 | tf_op jit(solution)/shard_map/ppermute | solution.py:445
  127.8 3.0 %collective-permute-done.11 = bf16[1,2,640,128]{3,2,1,0:T(8,128)(2,1)S(1)} collective-permute-done((bf16[1,2,640,128]{3,2,1,0:T(8,128)(2,1)S(1)}, bf16[1,2,640,128]{3,2,1,0:T(8,128)(2,1)S(1)}, u32[]{:S(2)}, u32[]{:S(2)}) %collective-permute-start.11) | collective-permute-done | bytes 327712 | tf_op jit(solution)/shard_map/ppermute | solution.py:445
  131.7 2.8 %collective-permute-start.13 = (bf16[1,16,24,128]{3,2,1,0:T(8,128)(2,1)S(1)}, bf16[1,16,24,128]{3,2,1,0:T(8,128)(2,1)S(1)}, u32[]{:S(2)}, u32[]{:S(2)}) collective-permute-start(bf16[1,16,24,128]{3,2,1,0:T(8,128)(2,1)S(1)} %get-tuple-element.98), channel_id=1, source_target_pairs={{0,24},{2,26},{4,28},{6,30},{8,16},{10,18},{12,20},{14,22},{16,8},... | collective-permute-start | bytes 294920 | tf_op jit(solution)/shard_map/ppermute | solution.py:445
  134.5 1.0 collective-permute-start.14
  136.1 14.2 %forward.4.refs_0_ = bf16[4,1024,640]{2,1,0:T(8,128)(2,1)} custom-call(s32[6]{0:T(128)} %stack.27.info, bf16[15,4,1088,128]{3,2,1,0:T(8,128)(2,1)} %get-tuple-element.50.slab_hbm, bf16[2880,640]{1,0:T(8,128)(2,1)} %own_ref.5, bf16[1440,640]{1,0:T(8,128)(2,1)} %copy-done, ...), custom_call_target="tpu_custom_call", output_to_operand_aliasing={{}: (5, {})} | custom-call | flops 7549747200 | bytes 11550720 | tf_op jit(solution)/shard_map/forward/pallas_call | solution.py:287
  151.1 2.5 %choose.1 = bf16[16,2,3,24,128]{4,3,2,1,0:T(8,128)(2,1)} custom-call(s32[16]{0:T(128)} %partner.3, bf16[2,16,24,128]{3,2,1,0:T(8,128)(2,1)} %get-tuple-element.69.refs_0_, bf16[2,16,24,128]{3,2,1,0:T(8,128)(2,1)} %copy-done.10, bf16[2,16,24,128]{3,2,1,0:T(8,128)(2,1)} %copy-done.11, bf16[2,16,24,128]{3,2,1,0:T(8,128)(2,1)} %copy-done.9, ...), custom_call_target="tpu_custom_call" | custom-call | tf_op jit(solution)/shard_map/choose/pallas_call | solution.py:368
  153.6 5.4 %all-to-all-start.2 = ((bf16[16,2,3,24,128]{4,3,2,1,0:T(8,128)(2,1)}), bf16[16,2,3,24,128]{4,3,2,1,0:T(8,128)(2,1)S(1)}, u32[]{:S(2)}, u32[]{:S(2)}) async-start(bf16[16,2,3,24,128]{4,3,2,1,0:T(8,128)(2,1)} %choose.1), calls=%async_computation.2 | async-start | bytes 1179648 | tf_op jit(solution)/shard_map/all_to_all | solution.py:538
  159.0 14.1 %forward.5 = bf16[4,1024,640]{2,1,0:T(8,128)(2,1)} custom-call(s32[6]{0:T(128)} %stack.27.info, bf16[15,4,1088,128]{3,2,1,0:T(8,128)(2,1)} %get-tuple-element.50.slab_hbm, bf16[2880,640]{1,0:T(8,128)(2,1)} %own_ref.5, bf16[1440,640]{1,0:T(8,128)(2,1)} %copy-done, bf16[1440,640]{1,0:T(8,128)(2,1)} %collective-permute-done.6.far_ref, ...), custom_call_target="tpu_custom_call", output_to_operand_aliasing={{}: (5, {})} | custom-call | flops 7549747200 | bytes 11550720 | tf_op jit(solution)/shard_map/forward/pallas_call | solution.py:287
  173.2 1.4 all-to-all-done.2.grad_ref
  174.6 0.8 copy-done.3
  175.4 4.9 %update.1 = (f32[1,2,40,2880]{3,2,1,0:T(8,128)}, f32[1,2,40,2880]{3,2,1,0:T(8,128)}, f32[1,2,40,2880]{3,2,1,0:T(8,128)}) custom-call(s32[6]{0:T(128)} %stack.27.info, s32[16]{0:T(128)} %departing.3, bf16[16,2,3,24,128]{4,3,2,1,0:T(8,128)(2,1)} %copy-done.3, f32[40,2880]{1,0:T(8,128)} %master_ref.3, f32[40,2880]{1,0:T(8,128)} %one_ref.3, f32[40,2880]{1,0:T(8,128)} %two_ref.3, ...), custom_call_target="tpu_custom_call" | custom-call | tf_op jit(solution)/shard_map/update/pallas_call | solution.py:408
  (52 shorter events, 4.3 us)
Async XLA Ops:
  3.5 64.5 %collective-permute-start = (bf16[1440,640]{1,0:T(8,128)(2,1)}, bf16[1440,640]{1,0:T(8,128)(2,1)S(1)}, u32[]{:S(2)}, u32[]{:S(2)}) collective-permute-start(bf16[1440,640]{1,0:T(8,128)(2,1)} %constant_dynamic-slice_fusion.8), channel_id=1, source_target_pairs={{0,1},{1,0},{2,3},{3,2},{4,5},{5,4},{6,7},{7,6},{8,9},{9,8},{10,11... | collective-permute-start | bytes 5529608 | tf_op jit(solution)/shard_map/ppermute | solution.py:448
  8.8 59.3 %all-to-all-start = ((bf16[16,8,2880]{2,1,0:T(8,128)(2,1)}), bf16[16,8,2880]{2,1,0:T(8,128)(2,1)S(1)}, u32[]{:S(2)}, u32[]{:S(2)}) async-start(bf16[16,8,2880]{2,1,0:T(8,128)(2,1)} %bitcast.17), calls=%async_computation | async-start | bytes 1507328 | tf_op jit(solution)/shard_map/all_to_all | solution.py:486
  68.0 1.0 copy-start.2
  68.0 3.1 %copy-start = (bf16[1440,640]{1,0:T(8,128)(2,1)}, bf16[1440,640]{1,0:T(8,128)(2,1)S(1)}, u32[]{:S(2)}) copy-start(bf16[1440,640]{1,0:T(8,128)(2,1)S(1)} %collective-permute-done.near_ref) | copy-start | bytes 5529604
  68.1 8.9 %collective-permute-start.2 = (bf16[8,2,640,128]{3,2,1,0:T(8,128)(2,1)}, bf16[8,2,640,128]{3,2,1,0:T(8,128)(2,1)}, u32[]{:S(2)}, u32[]{:S(2)}) collective-permute-start(bf16[8,2,640,128]{3,2,1,0:T(8,128)(2,1)} %get-tuple-element.48), channel_id=1, source_target_pairs={{0,2},{2,0},{4,6},{6,4},{8,10},{10,8},{12,14},{14,12},{16,18},{18,... | collective-permute-start | bytes 7864328 | tf_op jit(solution)/shard_map/ppermute | solution.py:445
  68.5 18.6 %collective-permute-start.6 = (bf16[1440,640]{1,0:T(8,128)(2,1)S(1)}, bf16[1440,640]{1,0:T(8,128)(2,1)}, u32[]{:S(2)}, u32[]{:S(2)}) collective-permute-start(bf16[1440,640]{1,0:T(8,128)(2,1)S(1)} %collective-permute-done.near_ref), channel_id=1, source_target_pairs={{0,2},{2,0},{4,6},{6,4},{8,10},{10,8},{12,14},{14,12},{16,18},{18,... | collective-permute-start | bytes 5529608 | tf_op jit(solution)/shard_map/ppermute | solution.py:445
  68.6 15.9 %collective-permute-start.1 = (bf16[4,2,640,128]{3,2,1,0:T(8,128)(2,1)}, bf16[4,2,640,128]{3,2,1,0:T(8,128)(2,1)}, u32[]{:S(2)}, u32[]{:S(2)}) collective-permute-start(bf16[4,2,640,128]{3,2,1,0:T(8,128)(2,1)} %get-tuple-element.46), channel_id=1, source_target_pairs={{0,2},{2,0},{4,6},{6,4},{8,10},{10,8},{12,14},{14,12},{16,18},{18,... | collective-permute-start | bytes 3932168 | tf_op jit(solution)/shard_map/ppermute | solution.py:445
  71.1 46.1 %all-to-all-start.1 = ((bf16[16,8,2880]{2,1,0:T(8,128)(2,1)}), bf16[16,8,2880]{2,1,0:T(8,128)(2,1)S(1)}, u32[]{:S(2)}, u32[]{:S(2)}) async-start(bf16[16,8,2880]{2,1,0:T(8,128)(2,1)} %route.1), calls=%async_computation.1 | async-start | bytes 1507328 | tf_op jit(solution)/shard_map/all_to_all | solution.py:498
  77.0 7.6 %copy-start.4 = (bf16[4,2,640,128]{3,2,1,0:T(8,128)(2,1)S(1)}, bf16[4,2,640,128]{3,2,1,0:T(8,128)(2,1)}, u32[]{:S(2)}) copy-start(bf16[4,2,640,128]{3,2,1,0:T(8,128)(2,1)} %get-tuple-element.52) | copy-start | bytes 3932164
  81.1 31.8 %collective-permute-start.3 = (bf16[2,2,640,128]{3,2,1,0:T(8,128)(2,1)}, bf16[2,2,640,128]{3,2,1,0:T(8,128)(2,1)S(1)}, u32[]{:S(2)}, u32[]{:S(2)}) collective-permute-start(bf16[2,2,640,128]{3,2,1,0:T(8,128)(2,1)} %get-tuple-element.85), channel_id=1, source_target_pairs={{0,5},{1,4},{2,7},{3,6},{4,1},{5,0},{6,3},{7,2},{8,13},{9,12},{10,... | collective-permute-start | bytes 1966088 | tf_op jit(solution)/shard_map/ppermute | solution.py:452
  82.9 31.0 %collective-permute-start.4 = (bf16[2,2,640,128]{3,2,1,0:T(8,128)(2,1)S(1)}, bf16[2,2,640,128]{3,2,1,0:T(8,128)(2,1)S(1)}, u32[]{:S(2)}, u32[]{:S(2)}) collective-permute-start(bf16[2,2,640,128]{3,2,1,0:T(8,128)(2,1)S(1)} %get-tuple-element.86), channel_id=1, source_target_pairs={{0,1},{1,0},{2,3},{3,2},{4,5},{5,4},{6,7},{7,6},{8,9},{9,8},{10,11... | collective-permute-start | bytes 1966088 | tf_op jit(solution)/shard_map/ppermute | solution.py:448
  84.5 32.7 %collective-permute-start.5 = (bf16[2,2,640,128]{3,2,1,0:T(8,128)(2,1)S(1)}, bf16[2,2,640,128]{3,2,1,0:T(8,128)(2,1)}, u32[]{:S(2)}, u32[]{:S(2)}) collective-permute-start(bf16[2,2,640,128]{3,2,1,0:T(8,128)(2,1)S(1)} %get-tuple-element.87), channel_id=1, source_target_pairs={{0,4},{2,6},{4,0},{6,2},{8,12},{10,14},{12,8},{14,10},{16,20},{18,... | collective-permute-start | bytes 1966088 | tf_op jit(solution)/shard_map/ppermute | solution.py:445
  87.2 37.4 %collective-permute-start.9 = (bf16[1,2,640,128]{3,2,1,0:T(8,128)(2,1)}, bf16[1,2,640,128]{3,2,1,0:T(8,128)(2,1)S(1)}, u32[]{:S(2)}, u32[]{:S(2)}) collective-permute-start(bf16[1,2,640,128]{3,2,1,0:T(8,128)(2,1)} %get-tuple-element.90), channel_id=1, source_target_pairs={{0,5},{1,4},{2,7},{3,6},{4,1},{5,0},{6,3},{7,2},{8,13},{9,12},{10,... | collective-permute-start | bytes 983048 | tf_op jit(solution)/shard_map/ppermute | solution.py:452
  89.0 38.8 %collective-permute-start.10 = (bf16[1,2,640,128]{3,2,1,0:T(8,128)(2,1)}, bf16[1,2,640,128]{3,2,1,0:T(8,128)(2,1)S(1)}, u32[]{:S(2)}, u32[]{:S(2)}) collective-permute-start(bf16[1,2,640,128]{3,2,1,0:T(8,128)(2,1)} %get-tuple-element.89), channel_id=1, source_target_pairs={{0,1},{1,0},{2,3},{3,2},{4,5},{5,4},{6,7},{7,6},{8,9},{9,8},{10,11... | collective-permute-start | bytes 983048 | tf_op jit(solution)/shard_map/ppermute | solution.py:448
  90.5 22.4 %copy-start.8 = (bf16[1,2,640,128]{3,2,1,0:T(8,128)(2,1)S(1)}, bf16[1,2,640,128]{3,2,1,0:T(8,128)(2,1)}, u32[]{:S(2)}) copy-start(bf16[1,2,640,128]{3,2,1,0:T(8,128)(2,1)} %get-tuple-element.88) | copy-start | bytes 983044
  112.9 1.1 copy-start.6
  112.9 17.9 %collective-permute-start.11 = (bf16[1,2,640,128]{3,2,1,0:T(8,128)(2,1)S(1)}, bf16[1,2,640,128]{3,2,1,0:T(8,128)(2,1)S(1)}, u32[]{:S(2)}, u32[]{:S(2)}) collective-permute-start(bf16[1,2,640,128]{3,2,1,0:T(8,128)(2,1)S(1)} %copy-done.8), channel_id=1, source_target_pairs={{0,4},{2,6},{4,0},{6,2},{8,12},{10,14},{12,8},{14,10},{16,20},{18,... | collective-permute-start | bytes 983048 | tf_op jit(solution)/shard_map/ppermute | solution.py:445
  114.0 0.8 copy-start.7
  117.2 2.1 %copy-start.1 = (bf16[16,8,2880]{2,1,0:T(8,128)(2,1)}, bf16[16,8,2880]{2,1,0:T(8,128)(2,1)S(1)}, u32[]{:S(2)}) copy-start(bf16[16,8,2880]{2,1,0:T(8,128)(2,1)S(1)} %all-to-all-done.1) | copy-start | bytes 2211844
  119.3 11.5 %copy-start.5 = (bf16[1,2,640,128]{3,2,1,0:T(8,128)(2,1)S(1)}, bf16[1,2,640,128]{3,2,1,0:T(8,128)(2,1)}, u32[]{:S(2)}) copy-start(bf16[1,2,640,128]{3,2,1,0:T(8,128)(2,1)} %get-tuple-element.64) | copy-start | bytes 983044
  120.1 10.7 %collective-permute-start.12 = (bf16[2,16,24,128]{3,2,1,0:T(8,128)(2,1)S(1)}, bf16[2,16,24,128]{3,2,1,0:T(8,128)(2,1)S(1)}, u32[]{:S(2)}, u32[]{:S(2)}) collective-permute-start(bf16[2,16,24,128]{3,2,1,0:T(8,128)(2,1)S(1)} %get-tuple-element.92), channel_id=1, source_target_pairs={{0,8},{2,10},{4,12},{6,14},{8,0},{10,2},{12,4},{14,6},{16,24},{18,... | collective-permute-start | bytes 589832 | tf_op jit(solution)/shard_map/ppermute | solution.py:445
  122.6 27.7 %collective-permute-start.7 = (bf16[2,16,24,128]{3,2,1,0:T(8,128)(2,1)S(1)}, bf16[2,16,24,128]{3,2,1,0:T(8,128)(2,1)S(1)}, u32[]{:S(2)}, u32[]{:S(2)}) collective-permute-start(bf16[2,16,24,128]{3,2,1,0:T(8,128)(2,1)S(1)} %get-tuple-element.94), channel_id=1, source_target_pairs={{0,24},{2,26},{4,28},{6,30},{8,16},{10,18},{12,20},{14,22},{16,8},... | collective-permute-start | bytes 589832 | tf_op jit(solution)/shard_map/ppermute | solution.py:445
  124.6 25.8 %collective-permute-start.8 = (bf16[2,16,24,128]{3,2,1,0:T(8,128)(2,1)S(1)}, bf16[2,16,24,128]{3,2,1,0:T(8,128)(2,1)S(1)}, u32[]{:S(2)}, u32[]{:S(2)}) collective-permute-start(bf16[2,16,24,128]{3,2,1,0:T(8,128)(2,1)S(1)} %get-tuple-element.93), channel_id=1, source_target_pairs={{0,16},{2,18},{4,20},{6,22},{8,24},{10,26},{12,28},{14,30},{16,0},... | collective-permute-start | bytes 589832 | tf_op jit(solution)/shard_map/ppermute | solution.py:445
  130.8 19.4 %copy-start.9 = (bf16[2,16,24,128]{3,2,1,0:T(8,128)(2,1)}, bf16[2,16,24,128]{3,2,1,0:T(8,128)(2,1)S(1)}, u32[]{:S(2)}) copy-start(bf16[2,16,24,128]{3,2,1,0:T(8,128)(2,1)S(1)} %collective-permute-done.12.refs_3_) | copy-start | bytes 589828
  131.7 18.6 %collective-permute-start.13 = (bf16[1,16,24,128]{3,2,1,0:T(8,128)(2,1)S(1)}, bf16[1,16,24,128]{3,2,1,0:T(8,128)(2,1)S(1)}, u32[]{:S(2)}, u32[]{:S(2)}) collective-permute-start(bf16[1,16,24,128]{3,2,1,0:T(8,128)(2,1)S(1)} %get-tuple-element.98), channel_id=1, source_target_pairs={{0,24},{2,26},{4,28},{6,30},{8,16},{10,18},{12,20},{14,22},{16,8},... | collective-permute-start | bytes 294920 | tf_op jit(solution)/shard_map/ppermute | solution.py:445
  134.5 15.8 %collective-permute-start.14 = (bf16[1,16,24,128]{3,2,1,0:T(8,128)(2,1)S(1)}, bf16[1,16,24,128]{3,2,1,0:T(8,128)(2,1)S(1)}, u32[]{:S(2)}, u32[]{:S(2)}) collective-permute-start(bf16[1,16,24,128]{3,2,1,0:T(8,128)(2,1)S(1)} %get-tuple-element.97), channel_id=1, source_target_pairs={{0,16},{2,18},{4,20},{6,22},{8,24},{10,26},{12,28},{14,30},{16,0},... | collective-permute-start | bytes 294920 | tf_op jit(solution)/shard_map/ppermute | solution.py:445
  135.6 14.8 %collective-permute-start.15 = (bf16[1,16,24,128]{3,2,1,0:T(8,128)(2,1)S(1)}, bf16[1,16,24,128]{3,2,1,0:T(8,128)(2,1)S(1)}, u32[]{:S(2)}, u32[]{:S(2)}) collective-permute-start(bf16[1,16,24,128]{3,2,1,0:T(8,128)(2,1)S(1)} %get-tuple-element.96), channel_id=1, source_target_pairs={{0,8},{2,10},{4,12},{6,14},{8,0},{10,2},{12,4},{14,6},{16,24},{18,... | collective-permute-start | bytes 294920 | tf_op jit(solution)/shard_map/ppermute | solution.py:445
  150.3 0.7 copy-start.11
  150.4 0.7 copy-start.13
  150.4 0.8 copy-start.14
  153.6 21.0 %all-to-all-start.2 = ((bf16[16,2,3,24,128]{4,3,2,1,0:T(8,128)(2,1)}), bf16[16,2,3,24,128]{4,3,2,1,0:T(8,128)(2,1)S(1)}, u32[]{:S(2)}, u32[]{:S(2)}) async-start(bf16[16,2,3,24,128]{4,3,2,1,0:T(8,128)(2,1)} %choose.1), calls=%async_computation.2 | async-start | bytes 1179648 | tf_op jit(solution)/shard_map/all_to_all | solution.py:538
  174.6 0.8 copy-start.3
  (2 other events, 1.4 us)

commit v3 on v2

--- a/solution.py
+++ b/solution.py
@@ -12,6 +12,7 @@
 LANES = 128
 MIB = 1024 * 1024
 VMEM_LIMIT = 58 * MIB
+SMALL_LIMIT = 20 * MIB
 PARTS = 3
 
 beta_one = 0.9
@@ -40,13 +41,19 @@
 
 
 def norm_grad_kernel(
-    inners, table, info, departing, lat_ref, gain_ref, bias_ref, member_ref, cot_hbm, slab_hbm, *refs
+    inners, table, info, departing, lat_hbm, gain_ref, bias_ref, member_ref, cot_hbm, slab_hbm, *refs
 ):
-    images, rows, width, ch = lat_ref.shape
+    images, rows, width, ch = lat_hbm.shape
     tiles = ch // LANES
     cells = rows * width
     count = cells * (ch // GROUPS)
-    halves, (slabs, cot, stage, cot_sem, slab_sems, stage_sems) = refs[:-6], refs[-6:]
+    halves, (lat_ref, slabs, cot, stage, lat_sems, cot_sem, slab_sems, stage_sems) = refs[:-8], refs[-8:]
+    arrivals = [
+        pltpu.make_async_copy(lat_hbm.at[image], lat_ref.at[image], lat_sems.at[image])
+        for image in range(images)
+    ]
+    for arrival in arrivals:
+        arrival.start()
     load = pltpu.make_async_copy(cot_hbm, cot, cot_sem)
     load.start()
 
@@ -72,6 +79,8 @@
     zero = jnp.zeros((8, ch), F32)
 
     def image_sum(image):
+        arrivals[image].wait()
+
         def add_row(row, total):
             return total + fold(lat_ref[image, row].astype(F32))
 
@@ -184,13 +193,15 @@
     anywhere = pl.BlockSpec(memory_space=pl.ANY)
     return pl.pallas_call(
         functools.partial(norm_grad_kernel, inners),
-        in_specs=[smem, smem, smem, vmem, vmem, vmem, vmem, anywhere],
+        in_specs=[smem, smem, smem, anywhere, vmem, vmem, vmem, anywhere],
         out_specs=[anywhere] * (1 + len(halves)),
         out_shape=[jax.ShapeDtypeStruct(slabs, BF16)] + halves,
         scratch_shapes=[
+            pltpu.VMEM(latents.shape, BF16),
             pltpu.VMEM(slabs, BF16),
             pltpu.VMEM(cot.shape, BF16),
             pltpu.VMEM((2, 2, out_ch, LANES), BF16),
+            pltpu.SemaphoreType.DMA((images,)),
             pltpu.SemaphoreType.DMA,
             pltpu.SemaphoreType.DMA((images,)),
             pltpu.SemaphoreType.DMA((2,)),
@@ -231,8 +242,25 @@
     step = pl.program_id(0)
     slot = step % 2
 
-    def cols_copy(image, at):
-        return pltpu.make_async_copy(slab_hbm.at[:, first + image], cols_ref.at[at], cols_sems.at[at])
+    class cols_copy:
+        def __init__(self, image, at):
+            share = slabs // PARTS
+            self.copies = [
+                pltpu.make_async_copy(
+                    slab_hbm.at[part * share : (part + 1) * share, first + image],
+                    cols_ref.at[at, part * share : (part + 1) * share],
+                    cols_sems.at[at, part],
+                )
+                for part in range(PARTS)
+            ]
+
+        def start(self):
+            for copy in self.copies:
+                copy.start()
+
+        def wait(self):
+            for copy in self.copies:
+                copy.wait()
 
     @pl.when(step == 0)
     def _():
@@ -295,7 +323,7 @@
                 pltpu.VMEM((rows, out_ch), BF16),
                 pltpu.VMEM((2, slab_count, padded, LANES), BF16),
                 pltpu.SemaphoreType.DMA((3 * PARTS,)),
-                pltpu.SemaphoreType.DMA((2,)),
+                pltpu.SemaphoreType.DMA((2, PARTS)),
             ],
         ),
         out_shape=jax.ShapeDtypeStruct((images, cells, out_ch), BF16),
@@ -324,7 +352,7 @@
     return pl.pallas_call(
         pack_kernel,
         out_shape=jax.ShapeDtypeStruct((padded, cols), BF16),
-        compiler_params=pltpu.CompilerParams(vmem_limit_bytes=VMEM_LIMIT),
+        compiler_params=pltpu.CompilerParams(vmem_limit_bytes=SMALL_LIMIT),
         name="pack",
     )(master, one, two)
 
@@ -340,7 +368,7 @@
         in_specs=[pl.BlockSpec(memory_space=pltpu.SMEM), pl.BlockSpec(memory_space=pltpu.VMEM)],
         out_specs=pl.BlockSpec(memory_space=pltpu.VMEM),
         out_shape=jax.ShapeDtypeStruct(pieces.shape, BF16),
-        compiler_params=pltpu.CompilerParams(vmem_limit_bytes=VMEM_LIMIT),
+        compiler_params=pltpu.CompilerParams(vmem_limit_bytes=SMALL_LIMIT),
         name="route",
     )(partner, pieces)
 
@@ -371,7 +399,7 @@
         + [pl.BlockSpec(memory_space=pltpu.VMEM)] * len(parts),
         out_specs=pl.BlockSpec(memory_space=pltpu.VMEM),
         out_shape=jax.ShapeDtypeStruct((reps, 2, tiles, rows, lanes), BF16),
-        compiler_params=pltpu.CompilerParams(vmem_limit_bytes=VMEM_LIMIT),
+        compiler_params=pltpu.CompilerParams(vmem_limit_bytes=SMALL_LIMIT),
         name="choose",
     )(partner, *parts)
 
@@ -382,42 +410,47 @@
     high = grad_ref.shape[3]
     staying = (1 - departing[info[1]]).astype(F32)
     odd = info[5] != 0
-    mates = mate_ref[...].astype(F32)
-    for block in range(2):
-        for tile, (upper, lower, inner) in enumerate(source):
-            span = slice(tile * LANES, (tile + 1) * LANES)
-            top = grad_ref[upper, block, inner].astype(F32)
-            low = grad_ref[lower, block, inner].astype(F32)
-            grad[0:high, span] = top
-            grad[high:block_rows, span] = low[2 * high - block_rows : high]
-        gradient = jnp.where(odd, grad[:, LANES // 2 : LANES // 2 + cols], grad[:, 0:cols])
-        gradient = gradient / images
-        if block == 0:
-            state = (master_ref[...], one_ref[...], two_ref[...])
-        else:
-            state = tuple(mates[k * block_rows : (k + 1) * block_rows] for k in range(3))
+    for tile, (upper, lower, inner) in enumerate(source):
+        span = slice(tile * LANES, (tile + 1) * LANES)
+        grad[0:high, span] = grad_ref[upper, 0, inner].astype(F32)
+        low = grad_ref[lower, 0, inner].astype(F32)
+        grad[high:block_rows, span] = low[2 * high - block_rows : high]
+    gradient = jnp.where(odd, grad[:, LANES // 2 : LANES // 2 + cols], grad[:, 0:cols])
+    gradient = gradient / images
+
+    def write(state):
         for out, value in zip(outs, adam(*state, gradient)):
-            out[0, block] = value * staying
+            out[0, 0] = value * staying
+
+    @pl.when(pl.program_id(0) == 0)
+    def _():
+        write((master_ref[...], one_ref[...], two_ref[...]))
+
+    @pl.when(pl.program_id(0) == 1)
+    def _():
+        mates = mate_ref[...].astype(F32)
+        write(tuple(mates[k * block_rows : (k + 1) * block_rows] for k in range(3)))
 
 
 def update(received, source, images, master, one, two, mates, info, departing):
     block_rows, cols = master.shape
     out = jax.ShapeDtypeStruct((1, 2, block_rows, cols), F32)
-    whole = [pl.BlockSpec(received.shape, lambda i, *_: (0,) * received.ndim)]
+    part = (received.shape[0], 1, *received.shape[2:])
+    whole = [pl.BlockSpec(part, lambda i, *_: (0, i, 0, 0, 0))]
     state = [pl.BlockSpec((block_rows, cols), lambda i, *_: (0, 0))] * 3
     return pl.pallas_call(
         functools.partial(update_kernel, source, images),
         grid_spec=pltpu.PrefetchScalarGridSpec(
             num_scalar_prefetch=2,
-            grid=(1,),
+            grid=(2,),
             in_specs=whole
             + state
             + [pl.BlockSpec(mates.shape, lambda i, *_: (0, 0))],
-            out_specs=[pl.BlockSpec((1, 2, block_rows, cols), lambda i, *_: (0, 0, 0, 0))] * 3,
+            out_specs=[pl.BlockSpec((1, 1, block_rows, cols), lambda i, *_: (0, i, 0, 0))] * 3,
             scratch_shapes=[pltpu.VMEM((block_rows, len(source) * LANES), F32)],
         ),
         out_shape=[out] * 3,
-        compiler_params=pltpu.CompilerParams(vmem_limit_bytes=VMEM_LIMIT),
+        compiler_params=pltpu.CompilerParams(vmem_limit_bytes=SMALL_LIMIT),
         name="update",
     )(info, departing, received, master, one, two, mates)
 

time: 181 us -> 176 us (0.972)
  Pallas kernels: 115 us -> 112 us
  transfers between devices with their start and end apart: 19 -> 19, of which waited for: 5 -> 4; matrix products, arithmetic and copies ran while one was open for 6% -> 7% of each run, Pallas kernels for 60% -> 61%
where the time goes in v3:
time: 176 us; the launch traced here: 175 us
  Pallas kernels  112 us (64%)
  starting transfers between devices  40 us (23%)
  other arithmetic  10.2 us (6%)
  waiting for transfers between devices  6.37 us (4%)
  local copies, waits for them, and re-layouts  6 us (3%)
    pallas_call x1, Pallas kernels, norm_grad(): pl.pallas_call(functools.partial(norm_grad_kernel, inners), in_specs=[sme...  53.2 us
    pallas_call x3, Pallas kernels, forward(): pl.pallas_call(functools.partial(forward_kernel, first, count), grid_spec...  51.5 us
    ppermute x11, starting transfers between devices, swap_rep(): return lax.ppermute(value, 'rep', [(i, i ^ bits) for i in range(reps)])  13.4 us
    convert_element_type x4, other arithmetic, add(): return total.astype(BF16)  10.2 us
    ppermute x3, starting transfers between devices, swap_shard(): return lax.ppermute(value, 'shard', [(0, 1), (1, 0)])  6.01 us
    all_to_all x1, starting transfers between devices, per_device(): spread = lax.all_to_all(state, 'rep', 0, 0, tiled=True)  5.91 us
    all_to_all x1, starting transfers between devices, per_device(): mates = lax.all_to_all(routed.reshape(-1, cols), 'rep', 0, 0, tiled=True)  5.75 us
    all_to_all x1, starting transfers between devices, per_device(): received = lax.all_to_all(choose(pieces, partner), 'rep', 0, 0, tiled=True)  5.21 us
  transfers between devices with their start and end apart: 19, of which 4 were waited for; matrix products, arithmetic and copies ran while one was open for 7% of the time, Pallas kernels for 61%

profile of v3, /device:TPU:0, one launch (start us, length us, event | category | flops | bytes accessed | tf_op | source)
XLA Modules:
  0.0 175.4 jit_solution(16697506964957391356)
XLA Ops:
  0.7 3.0 %constant_dynamic-slice_fusion.8 = bf16[1440,640]{1,0:T(8,128)(2,1)} fusion(bf16[2880,640]{1,0:T(8,128)(2,1)} %own_ref.5, s32[]{:T(128)S(6)} %select_n.14), kind=kLoop, calls=%fused_computation.18 | loop fusion | bytes 3686404 | tf_op jit(solution)/shard_map/dynamic_slice | solution.py:489
  3.7 3.0 %collective-permute-start = (bf16[1440,640]{1,0:T(8,128)(2,1)}, bf16[1440,640]{1,0:T(8,128)(2,1)}, u32[]{:S(2)}, u32[]{:S(2)}) collective-permute-start(bf16[1440,640]{1,0:T(8,128)(2,1)} %constant_dynamic-slice_fusion.8), channel_id=1, source_target_pairs={{0,1},{1,0},{2,3},{3,2},{4,5},{5,4},{6,7},{7,6},{8,9},{9,8},{10,11... | collective-permute-start | bytes 5529608 | tf_op jit(solution)/shard_map/ppermute | solution.py:481
  6.7 0.9 pack.1
  7.6 5.9 %all-to-all-start = ((bf16[16,8,2880]{2,1,0:T(8,128)(2,1)}), bf16[16,8,2880]{2,1,0:T(8,128)(2,1)S(1)}, u32[]{:S(2)}, u32[]{:S(2)}) async-start(bf16[16,8,2880]{2,1,0:T(8,128)(2,1)} %bitcast.7), calls=%async_computation | async-start | bytes 1507328 | tf_op jit(solution)/shard_map/all_to_all | solution.py:519
  14.1 53.2 %norm_grad.1 = (bf16[15,4,1088,128]{3,2,1,0:T(8,128)(2,1)}, bf16[8,2,640,128]{3,2,1,0:T(8,128)(2,1)}, bf16[8,2,640,128]{3,2,1,0:T(8,128)(2,1)}, bf16[4,2,640,128]{3,2,1,0:T(8,128)(2,1)}, bf16[4,2,640,128]{3,2,1,0:T(8,128)(2,1)}) custom-call(s32[96]{0:T(128)} %constant.30.clone.table, s32[6]{0:T(128)} %stack.27.info, s32[16]{0:T(128)} %departing.3, ...), custom_call_target="tpu_custom_call" | custom-call | flops 32212254720 | bytes 26214400 | tf_op jit(solution)/shard_map/norm_grad/pallas_call | solution.py:194
  68.3 1.5 route.1
  69.8 5.8 %all-to-all-start.1 = ((bf16[16,8,2880]{2,1,0:T(8,128)(2,1)}), bf16[16,8,2880]{2,1,0:T(8,128)(2,1)S(1)}, u32[]{:S(2)}, u32[]{:S(2)}) async-start(bf16[16,8,2880]{2,1,0:T(8,128)(2,1)} %route.1), calls=%async_computation.1 | async-start | bytes 1507328 | tf_op jit(solution)/shard_map/all_to_all | solution.py:531
  75.6 4.4 %add_convert_fusion.4 = (bf16[2,2,640,128]{3,2,1,0:T(8,128)(2,1)S(1)}, bf16[2,2,640,128]{3,2,1,0:T(8,128)(2,1)}, bf16[2,2,640,128]{3,2,1,0:T(8,128)(2,1)}, bf16[2,2,640,128]{3,2,1,0:T(8,128)(2,1)}) fusion(bf16[8,2,640,128]{3,2,1,0:T(8,128)(2,1)} %collective-permute-done.2, bf16[8,2,640,128]{3,2,1,0:T(8,128)(2,1)} %get-tuple-element.47), kind=kLoop, calls=%fused_computation.4 | loop fusion | flops 5242880 | bytes 7864320 | tf_op jit(solution)/shard_map/convert_element_type | solution.py:508
  80.0 1.9 %collective-permute-start.3 = (bf16[2,2,640,128]{3,2,1,0:T(8,128)(2,1)}, bf16[2,2,640,128]{3,2,1,0:T(8,128)(2,1)S(1)}, u32[]{:S(2)}, u32[]{:S(2)}) collective-permute-start(bf16[2,2,640,128]{3,2,1,0:T(8,128)(2,1)} %get-tuple-element.85), channel_id=1, source_target_pairs={{0,5},{1,4},{2,7},{3,6},{4,1},{5,0},{6,3},{7,2},{8,13},{9,12},{10,... | collective-permute-start | bytes 1966088 | tf_op jit(solution)/shard_map/ppermute | solution.py:485
  81.8 1.5 collective-permute-start.4
  83.5 2.6 %add_convert_fusion.6 = (bf16[1,2,640,128]{3,2,1,0:T(8,128)(2,1)}, bf16[1,2,640,128]{3,2,1,0:T(8,128)(2,1)}, bf16[1,2,640,128]{3,2,1,0:T(8,128)(2,1)}, bf16[1,2,640,128]{3,2,1,0:T(8,128)(2,1)S(1)}) fusion(bf16[4,2,640,128]{3,2,1,0:T(8,128)(2,1)} %collective-permute-done.1, bf16[4,2,640,128]{3,2,1,0:T(8,128)(2,1)S(1)} %copy-done.6), kind=kLoop, calls=%fused_computation.6 | loop fusion | flops 2621440 | bytes 3932160 | tf_op jit(solution)/shard_map/convert_element_type | solution.py:508
  86.1 1.9 %collective-permute-start.9 = (bf16[1,2,640,128]{3,2,1,0:T(8,128)(2,1)}, bf16[1,2,640,128]{3,2,1,0:T(8,128)(2,1)S(1)}, u32[]{:S(2)}, u32[]{:S(2)}) collective-permute-start(bf16[1,2,640,128]{3,2,1,0:T(8,128)(2,1)} %get-tuple-element.90), channel_id=1, source_target_pairs={{0,5},{1,4},{2,7},{3,6},{4,1},{5,0},{6,3},{7,2},{8,13},{9,12},{10,... | collective-permute-start | bytes 983048 | tf_op jit(solution)/shard_map/ppermute | solution.py:485
  87.9 1.5 collective-permute-start.10
  89.5 23.1 %forward.3.refs_0_ = bf16[4,1024,640]{2,1,0:T(8,128)(2,1)} custom-call(s32[6]{0:T(128)} %stack.27.info, bf16[15,4,1088,128]{3,2,1,0:T(8,128)(2,1)} %get-tuple-element.50.slab_hbm, bf16[2880,640]{1,0:T(8,128)(2,1)} %own_ref.5, bf16[1440,640]{1,0:T(8,128)(2,1)} %collective-permute-done.near_ref, bf16[1440,640]{1,0:T(8,128)(2,1)} %collective-permute-done.6.far_ref), custom_call_target="tpu_custom_call" | custom-call | flops 15099494400 | bytes 15728640 | tf_op jit(solution)/shard_map/forward/pallas_call | solution.py:315
  112.8 0.6 copy-done.7
  113.4 0.8 copy-done.8
  114.2 1.7 collective-permute-done.5
  115.9 1.9 %add_convert_fusion = bf16[2,2,640,128]{3,2,1,0:T(8,128)(2,1)S(1)} fusion(bf16[2,2,640,128]{3,2,1,0:T(8,128)(2,1)} %collective-permute-done.5, bf16[2,2,640,128]{3,2,1,0:T(8,128)(2,1)} %copy-done.8, bf16[2,2,640,128]{3,2,1,0:T(8,128)(2,1)} %copy-done.7, bf16[2,2,640,128]{3,2,1,0:T(8,128)(2,1)S(1)} %get-tuple-element.49), kind=kLoop, calls=%fused_computation | loop fusion | flops 2621440 | bytes 3276800 | tf_op jit(solution)/shard_map/convert_element_type | solution.py:508
  117.8 0.8 constant_dynamic-slice_fusion.4
  118.7 2.5 %collective-permute-start.12 = (bf16[2,16,24,128]{3,2,1,0:T(8,128)(2,1)}, bf16[2,16,24,128]{3,2,1,0:T(8,128)(2,1)S(1)}, u32[]{:S(2)}, u32[]{:S(2)}) collective-permute-start(bf16[2,16,24,128]{3,2,1,0:T(8,128)(2,1)} %get-tuple-element.92), channel_id=1, source_target_pairs={{0,8},{2,10},{4,12},{6,14},{8,0},{10,2},{12,4},{14,6},{16,24},{18,... | collective-permute-start | bytes 589832 | tf_op jit(solution)/shard_map/ppermute | solution.py:478
  121.1 1.8 %collective-permute-start.7 = (bf16[2,16,24,128]{3,2,1,0:T(8,128)(2,1)}, bf16[2,16,24,128]{3,2,1,0:T(8,128)(2,1)S(1)}, u32[]{:S(2)}, u32[]{:S(2)}) collective-permute-start(bf16[2,16,24,128]{3,2,1,0:T(8,128)(2,1)} %get-tuple-element.94), channel_id=1, source_target_pairs={{0,24},{2,26},{4,28},{6,30},{8,16},{10,18},{12,20},{14,22},{16,8},... | collective-permute-start | bytes 589832 | tf_op jit(solution)/shard_map/ppermute | solution.py:478
  123.3 3.4 %collective-permute-start.8 = (bf16[2,16,24,128]{3,2,1,0:T(8,128)(2,1)S(1)}, bf16[2,16,24,128]{3,2,1,0:T(8,128)(2,1)S(1)}, u32[]{:S(2)}, u32[]{:S(2)}) collective-permute-start(bf16[2,16,24,128]{3,2,1,0:T(8,128)(2,1)S(1)} %get-tuple-element.93), channel_id=1, source_target_pairs={{0,16},{2,18},{4,20},{6,22},{8,24},{10,26},{12,28},{14,30},{16,0},... | collective-permute-start | bytes 589832 | tf_op jit(solution)/shard_map/ppermute | solution.py:478
  126.7 3.1 %collective-permute-done.11 = bf16[1,2,640,128]{3,2,1,0:T(8,128)(2,1)} collective-permute-done((bf16[1,2,640,128]{3,2,1,0:T(8,128)(2,1)}, bf16[1,2,640,128]{3,2,1,0:T(8,128)(2,1)}, u32[]{:S(2)}, u32[]{:S(2)}) %collective-permute-start.11) | collective-permute-done | bytes 327712 | tf_op jit(solution)/shard_map/ppermute | solution.py:478
  129.7 1.3 add_convert_fusion.5
  131.1 2.8 %collective-permute-start.13 = (bf16[1,16,24,128]{3,2,1,0:T(8,128)(2,1)S(1)}, bf16[1,16,24,128]{3,2,1,0:T(8,128)(2,1)S(1)}, u32[]{:S(2)}, u32[]{:S(2)}) collective-permute-start(bf16[1,16,24,128]{3,2,1,0:T(8,128)(2,1)S(1)} %get-tuple-element.98), channel_id=1, source_target_pairs={{0,24},{2,26},{4,28},{6,30},{8,16},{10,18},{12,20},{14,22},{16,8},... | collective-permute-start | bytes 294920 | tf_op jit(solution)/shard_map/ppermute | solution.py:478
  133.9 1.1 collective-permute-start.14
  135.5 14.2 %forward.4.refs_0_ = bf16[4,1024,640]{2,1,0:T(8,128)(2,1)} custom-call(s32[6]{0:T(128)} %stack.27.info, bf16[15,4,1088,128]{3,2,1,0:T(8,128)(2,1)} %get-tuple-element.50.slab_hbm, bf16[2880,640]{1,0:T(8,128)(2,1)} %own_ref.5, bf16[1440,640]{1,0:T(8,128)(2,1)} %collective-permute-done.near_ref, ...), custom_call_target="tpu_custom_call", output_to_operand_aliasing={{}: (5, {})} | custom-call | flops 7549747200 | bytes 11550720 | tf_op jit(solution)/shard_map/forward/pallas_call | solution.py:315
  149.8 1.6 choose.1
  151.4 5.2 %all-to-all-start.2 = ((bf16[16,2,3,24,128]{4,3,2,1,0:T(8,128)(2,1)}), bf16[16,2,3,24,128]{4,3,2,1,0:T(8,128)(2,1)S(1)}, u32[]{:S(2)}, u32[]{:S(2)}) async-start(bf16[16,2,3,24,128]{4,3,2,1,0:T(8,128)(2,1)} %choose.1), calls=%async_computation.2 | async-start | bytes 1179648 | tf_op jit(solution)/shard_map/all_to_all | solution.py:571
  156.7 14.3 %forward.5 = bf16[4,1024,640]{2,1,0:T(8,128)(2,1)} custom-call(s32[6]{0:T(128)} %stack.27.info, bf16[15,4,1088,128]{3,2,1,0:T(8,128)(2,1)} %get-tuple-element.50.slab_hbm, bf16[2880,640]{1,0:T(8,128)(2,1)} %own_ref.5, bf16[1440,640]{1,0:T(8,128)(2,1)} %collective-permute-done.near_ref, ...), custom_call_target="tpu_custom_call", output_to_operand_aliasing={{}: (5, {})} | custom-call | flops 7549747200 | bytes 11550720 | tf_op jit(solution)/shard_map/forward/pallas_call | solution.py:315
  171.0 1.2 all-to-all-done.2.grad_ref
  172.2 3.2 %update.1 = (f32[1,2,40,2880]{3,2,1,0:T(8,128)}, f32[1,2,40,2880]{3,2,1,0:T(8,128)}, f32[1,2,40,2880]{3,2,1,0:T(8,128)}) custom-call(s32[6]{0:T(128)S(1)} %copy-done.3, s32[16]{0:T(128)S(1)} %copy-done.5, bf16[16,2,3,24,128]{4,3,2,1,0:T(8,128)(2,1)S(1)} %all-to-all-done.2.grad_ref, f32[40,2880]{1,0:T(8,128)S(1)} %copy-done, f32[40,2880]{1,0:T(8,128)S(1)} %copy-done.1, ...), custom_call_target="tpu_custom_call" | custom-call | tf_op jit(solution)/shard_map/update/pallas_call | solution.py:441
  (40 shorter events, 2.9 us)
Async XLA Ops:
  0.6 6.0 %copy-start = (f32[40,2880]{1,0:T(8,128)S(1)}, f32[40,2880]{1,0:T(8,128)}, u32[]{:S(2)}) copy-start(f32[40,2880]{1,0:T(8,128)} %master_ref.3) | copy-start | bytes 1382404
  0.6 6.0 %copy-start.1 = (f32[40,2880]{1,0:T(8,128)S(1)}, f32[40,2880]{1,0:T(8,128)}, u32[]{:S(2)}) copy-start(f32[40,2880]{1,0:T(8,128)} %one_ref.3) | copy-start | bytes 1382404
  0.7 6.0 %copy-start.2 = (f32[40,2880]{1,0:T(8,128)S(1)}, f32[40,2880]{1,0:T(8,128)}, u32[]{:S(2)}) copy-start(f32[40,2880]{1,0:T(8,128)} %two_ref.3) | copy-start | bytes 1382404
  3.7 63.6 %collective-permute-start = (bf16[1440,640]{1,0:T(8,128)(2,1)}, bf16[1440,640]{1,0:T(8,128)(2,1)}, u32[]{:S(2)}, u32[]{:S(2)}) collective-permute-start(bf16[1440,640]{1,0:T(8,128)(2,1)} %constant_dynamic-slice_fusion.8), channel_id=1, source_target_pairs={{0,1},{1,0},{2,3},{3,2},{4,5},{5,4},{6,7},{7,6},{8,9},{9,8},{10,11... | collective-permute-start | bytes 5529608 | tf_op jit(solution)/shard_map/ppermute | solution.py:481
  7.6 59.7 %all-to-all-start = ((bf16[16,8,2880]{2,1,0:T(8,128)(2,1)}), bf16[16,8,2880]{2,1,0:T(8,128)(2,1)S(1)}, u32[]{:S(2)}, u32[]{:S(2)}) async-start(bf16[16,8,2880]{2,1,0:T(8,128)(2,1)} %bitcast.7), calls=%async_computation | async-start | bytes 1507328 | tf_op jit(solution)/shard_map/all_to_all | solution.py:519
  14.1 54.2 %copy-start.4 = (s32[16]{0:T(128)S(1)}, s32[16]{0:T(128)}, u32[]{:S(2)}) copy-start(s32[16]{0:T(128)} %partner.3) | copy-start | bytes 196
  67.3 8.2 %collective-permute-start.2 = (bf16[8,2,640,128]{3,2,1,0:T(8,128)(2,1)}, bf16[8,2,640,128]{3,2,1,0:T(8,128)(2,1)}, u32[]{:S(2)}, u32[]{:S(2)}) collective-permute-start(bf16[8,2,640,128]{3,2,1,0:T(8,128)(2,1)} %get-tuple-element.48), channel_id=1, source_target_pairs={{0,2},{2,0},{4,6},{6,4},{8,10},{10,8},{12,14},{14,12},{16,18},{18,... | collective-permute-start | bytes 7864328 | tf_op jit(solution)/shard_map/ppermute | solution.py:478
  67.8 18.3 %collective-permute-start.6 = (bf16[1440,640]{1,0:T(8,128)(2,1)}, bf16[1440,640]{1,0:T(8,128)(2,1)}, u32[]{:S(2)}, u32[]{:S(2)}) collective-permute-start(bf16[1440,640]{1,0:T(8,128)(2,1)} %collective-permute-done.near_ref), channel_id=1, source_target_pairs={{0,2},{2,0},{4,6},{6,4},{8,10},{10,8},{12,14},{14,12},{16,18},{18,... | collective-permute-start | bytes 5529608 | tf_op jit(solution)/shard_map/ppermute | solution.py:478
  67.9 15.5 %collective-permute-start.1 = (bf16[4,2,640,128]{3,2,1,0:T(8,128)(2,1)}, bf16[4,2,640,128]{3,2,1,0:T(8,128)(2,1)}, u32[]{:S(2)}, u32[]{:S(2)}) collective-permute-start(bf16[4,2,640,128]{3,2,1,0:T(8,128)(2,1)} %get-tuple-element.46), channel_id=1, source_target_pairs={{0,2},{2,0},{4,6},{6,4},{8,10},{10,8},{12,14},{14,12},{16,18},{18,... | collective-permute-start | bytes 3932168 | tf_op jit(solution)/shard_map/ppermute | solution.py:478
  69.8 46.1 %all-to-all-start.1 = ((bf16[16,8,2880]{2,1,0:T(8,128)(2,1)}), bf16[16,8,2880]{2,1,0:T(8,128)(2,1)S(1)}, u32[]{:S(2)}, u32[]{:S(2)}) async-start(bf16[16,8,2880]{2,1,0:T(8,128)(2,1)} %route.1), calls=%async_computation.1 | async-start | bytes 1507328 | tf_op jit(solution)/shard_map/all_to_all | solution.py:531
  75.5 7.9 %copy-start.6 = (bf16[4,2,640,128]{3,2,1,0:T(8,128)(2,1)S(1)}, bf16[4,2,640,128]{3,2,1,0:T(8,128)(2,1)}, u32[]{:S(2)}) copy-start(bf16[4,2,640,128]{3,2,1,0:T(8,128)(2,1)} %get-tuple-element.52) | copy-start | bytes 3932164
  80.0 32.6 %collective-permute-start.3 = (bf16[2,2,640,128]{3,2,1,0:T(8,128)(2,1)}, bf16[2,2,640,128]{3,2,1,0:T(8,128)(2,1)S(1)}, u32[]{:S(2)}, u32[]{:S(2)}) collective-permute-start(bf16[2,2,640,128]{3,2,1,0:T(8,128)(2,1)} %get-tuple-element.85), channel_id=1, source_target_pairs={{0,5},{1,4},{2,7},{3,6},{4,1},{5,0},{6,3},{7,2},{8,13},{9,12},{10,... | collective-permute-start | bytes 1966088 | tf_op jit(solution)/shard_map/ppermute | solution.py:485
  81.8 30.9 %collective-permute-start.4 = (bf16[2,2,640,128]{3,2,1,0:T(8,128)(2,1)}, bf16[2,2,640,128]{3,2,1,0:T(8,128)(2,1)S(1)}, u32[]{:S(2)}, u32[]{:S(2)}) collective-permute-start(bf16[2,2,640,128]{3,2,1,0:T(8,128)(2,1)} %get-tuple-element.86), channel_id=1, source_target_pairs={{0,1},{1,0},{2,3},{3,2},{4,5},{5,4},{6,7},{7,6},{8,9},{9,8},{10,11... | collective-permute-start | bytes 1966088 | tf_op jit(solution)/shard_map/ppermute | solution.py:481
  83.3 32.6 %collective-permute-start.5 = (bf16[2,2,640,128]{3,2,1,0:T(8,128)(2,1)}, bf16[2,2,640,128]{3,2,1,0:T(8,128)(2,1)}, u32[]{:S(2)}, u32[]{:S(2)}) collective-permute-start(bf16[2,2,640,128]{3,2,1,0:T(8,128)(2,1)} %get-tuple-element.87), channel_id=1, source_target_pairs={{0,4},{2,6},{4,0},{6,2},{8,12},{10,14},{12,8},{14,10},{16,20},{18,... | collective-permute-start | bytes 1966088 | tf_op jit(solution)/shard_map/ppermute | solution.py:478
  86.1 37.2 %collective-permute-start.9 = (bf16[1,2,640,128]{3,2,1,0:T(8,128)(2,1)}, bf16[1,2,640,128]{3,2,1,0:T(8,128)(2,1)S(1)}, u32[]{:S(2)}, u32[]{:S(2)}) collective-permute-start(bf16[1,2,640,128]{3,2,1,0:T(8,128)(2,1)} %get-tuple-element.90), channel_id=1, source_target_pairs={{0,5},{1,4},{2,7},{3,6},{4,1},{5,0},{6,3},{7,2},{8,13},{9,12},{10,... | collective-permute-start | bytes 983048 | tf_op jit(solution)/shard_map/ppermute | solution.py:485
  87.9 38.7 %collective-permute-start.10 = (bf16[1,2,640,128]{3,2,1,0:T(8,128)(2,1)}, bf16[1,2,640,128]{3,2,1,0:T(8,128)(2,1)}, u32[]{:S(2)}, u32[]{:S(2)}) collective-permute-start(bf16[1,2,640,128]{3,2,1,0:T(8,128)(2,1)} %get-tuple-element.89), channel_id=1, source_target_pairs={{0,1},{1,0},{2,3},{3,2},{4,5},{5,4},{6,7},{7,6},{8,9},{9,8},{10,11... | collective-permute-start | bytes 983048 | tf_op jit(solution)/shard_map/ppermute | solution.py:481
  112.5 0.8 copy-start.7
  112.6 17.2 %collective-permute-start.11 = (bf16[1,2,640,128]{3,2,1,0:T(8,128)(2,1)}, bf16[1,2,640,128]{3,2,1,0:T(8,128)(2,1)}, u32[]{:S(2)}, u32[]{:S(2)}) collective-permute-start(bf16[1,2,640,128]{3,2,1,0:T(8,128)(2,1)} %get-tuple-element.88), channel_id=1, source_target_pairs={{0,4},{2,6},{4,0},{6,2},{8,12},{10,14},{12,8},{14,10},{16,20},{18,... | collective-permute-start | bytes 983048 | tf_op jit(solution)/shard_map/ppermute | solution.py:478
  113.4 0.8 copy-start.8
  118.7 11.1 %collective-permute-start.12 = (bf16[2,16,24,128]{3,2,1,0:T(8,128)(2,1)}, bf16[2,16,24,128]{3,2,1,0:T(8,128)(2,1)S(1)}, u32[]{:S(2)}, u32[]{:S(2)}) collective-permute-start(bf16[2,16,24,128]{3,2,1,0:T(8,128)(2,1)} %get-tuple-element.92), channel_id=1, source_target_pairs={{0,8},{2,10},{4,12},{6,14},{8,0},{10,2},{12,4},{14,6},{16,24},{18,... | collective-permute-start | bytes 589832 | tf_op jit(solution)/shard_map/ppermute | solution.py:478
  121.1 28.6 %collective-permute-start.7 = (bf16[2,16,24,128]{3,2,1,0:T(8,128)(2,1)}, bf16[2,16,24,128]{3,2,1,0:T(8,128)(2,1)S(1)}, u32[]{:S(2)}, u32[]{:S(2)}) collective-permute-start(bf16[2,16,24,128]{3,2,1,0:T(8,128)(2,1)} %get-tuple-element.94), channel_id=1, source_target_pairs={{0,24},{2,26},{4,28},{6,30},{8,16},{10,18},{12,20},{14,22},{16,8},... | collective-permute-start | bytes 589832 | tf_op jit(solution)/shard_map/ppermute | solution.py:478
  123.3 26.4 %collective-permute-start.8 = (bf16[2,16,24,128]{3,2,1,0:T(8,128)(2,1)S(1)}, bf16[2,16,24,128]{3,2,1,0:T(8,128)(2,1)S(1)}, u32[]{:S(2)}, u32[]{:S(2)}) collective-permute-start(bf16[2,16,24,128]{3,2,1,0:T(8,128)(2,1)S(1)} %get-tuple-element.93), channel_id=1, source_target_pairs={{0,16},{2,18},{4,20},{6,22},{8,24},{10,26},{12,28},{14,30},{16,0},... | collective-permute-start | bytes 589832 | tf_op jit(solution)/shard_map/ppermute | solution.py:478
  131.1 18.7 %collective-permute-start.13 = (bf16[1,16,24,128]{3,2,1,0:T(8,128)(2,1)S(1)}, bf16[1,16,24,128]{3,2,1,0:T(8,128)(2,1)S(1)}, u32[]{:S(2)}, u32[]{:S(2)}) collective-permute-start(bf16[1,16,24,128]{3,2,1,0:T(8,128)(2,1)S(1)} %get-tuple-element.98), channel_id=1, source_target_pairs={{0,24},{2,26},{4,28},{6,30},{8,16},{10,18},{12,20},{14,22},{16,8},... | collective-permute-start | bytes 294920 | tf_op jit(solution)/shard_map/ppermute | solution.py:478
  133.9 15.8 %collective-permute-start.14 = (bf16[1,16,24,128]{3,2,1,0:T(8,128)(2,1)S(1)}, bf16[1,16,24,128]{3,2,1,0:T(8,128)(2,1)S(1)}, u32[]{:S(2)}, u32[]{:S(2)}) collective-permute-start(bf16[1,16,24,128]{3,2,1,0:T(8,128)(2,1)S(1)} %get-tuple-element.97), channel_id=1, source_target_pairs={{0,16},{2,18},{4,20},{6,22},{8,24},{10,26},{12,28},{14,30},{16,0},... | collective-permute-start | bytes 294920 | tf_op jit(solution)/shard_map/ppermute | solution.py:478
  135.0 14.8 %collective-permute-start.15 = (bf16[1,16,24,128]{3,2,1,0:T(8,128)(2,1)S(1)}, bf16[1,16,24,128]{3,2,1,0:T(8,128)(2,1)S(1)}, u32[]{:S(2)}, u32[]{:S(2)}) collective-permute-start(bf16[1,16,24,128]{3,2,1,0:T(8,128)(2,1)S(1)} %get-tuple-element.96), channel_id=1, source_target_pairs={{0,8},{2,10},{4,12},{6,14},{8,0},{10,2},{12,4},{14,6},{16,24},{18,... | collective-permute-start | bytes 294920 | tf_op jit(solution)/shard_map/ppermute | solution.py:478
  151.4 20.8 %all-to-all-start.2 = ((bf16[16,2,3,24,128]{4,3,2,1,0:T(8,128)(2,1)}), bf16[16,2,3,24,128]{4,3,2,1,0:T(8,128)(2,1)S(1)}, u32[]{:S(2)}, u32[]{:S(2)}) async-start(bf16[16,2,3,24,128]{4,3,2,1,0:T(8,128)(2,1)} %choose.1), calls=%async_computation.2 | async-start | bytes 1179648 | tf_op jit(solution)/shard_map/all_to_all | solution.py:571
  156.6 15.5 %copy-start.3 = (s32[6]{0:T(128)S(1)}, s32[6]{0:T(128)}, u32[]{:S(2)}) copy-start(s32[6]{0:T(128)} %stack.27.info) | copy-start | bytes 76
  156.6 15.5 %copy-start.5 = (s32[16]{0:T(128)S(1)}, s32[16]{0:T(128)}, u32[]{:S(2)}) copy-start(s32[16]{0:T(128)} %departing.3) | copy-start | bytes 196

commit v4 on v3

--- a/solution.py
+++ b/solution.py
@@ -13,7 +13,7 @@
 MIB = 1024 * 1024
 VMEM_LIMIT = 58 * MIB
 SMALL_LIMIT = 20 * MIB
-PARTS = 3
+PARTS = 5
 
 beta_one = 0.9
 beta_two = 0.999
@@ -120,7 +120,7 @@
         for slab in range(3 * tiles):
             slabs[slab, image, 0:width, :] = edge
             slabs[slab, image, cells + width : cells + 2 * width, :] = edge
-        lax.fori_loop(0, rows, write_row, 0, unroll=2)
+        lax.fori_loop(0, rows, write_row, 0)
         stores.append(pltpu.make_async_copy(slabs.at[:, image], slab_hbm.at[:, image], slab_sems.at[image]))
         stores[-1].start()
 

time: 176 us -> 175 us (level)
  no operation moved by 1% of the time
where the time goes in v4:
time: 175 us
  Pallas kernels  112 us (64%)
  starting transfers between devices  39.9 us (23%)
  other arithmetic  10.2 us (6%)
  waiting for transfers between devices  6.04 us (3%)
  local copies, waits for them, and re-layouts  6.03 us (3%)
    pallas_call x1, Pallas kernels, norm_grad(): pl.pallas_call(functools.partial(norm_grad_kernel, inners), in_specs=[sme...  52.6 us
    pallas_call x3, Pallas kernels, forward(): pl.pallas_call(functools.partial(forward_kernel, first, count), grid_spec...  51.9 us
    ppermute x11, starting transfers between devices, swap_rep(): return lax.ppermute(value, 'rep', [(i, i ^ bits) for i in range(reps)])  13.4 us
    convert_element_type x4, other arithmetic, add(): return total.astype(BF16)  10.2 us
    ppermute x3, starting transfers between devices, swap_shard(): return lax.ppermute(value, 'shard', [(0, 1), (1, 0)])  6 us
    all_to_all x1, starting transfers between devices, per_device(): spread = lax.all_to_all(state, 'rep', 0, 0, tiled=True)  5.91 us
    all_to_all x1, starting transfers between devices, per_device(): mates = lax.all_to_all(routed.reshape(-1, cols), 'rep', 0, 0, tiled=True)  5.74 us
    all_to_all x1, starting transfers between devices, per_device(): received = lax.all_to_all(choose(pieces, partner), 'rep', 0, 0, tiled=True)  5.2 us
  transfers between devices with their start and end apart: 19, of which 4 were waited for; matrix products, arithmetic and copies ran while one was open for 7% of the time, Pallas kernels for 61%

profile of v4, /device:TPU:0, one launch (start us, length us, event | category | flops | bytes accessed | tf_op | source)
XLA Modules:
  0.0 174.9 jit_solution(1499540855277418101)
XLA Ops:
  0.7 3.0 %constant_dynamic-slice_fusion.8 = bf16[1440,640]{1,0:T(8,128)(2,1)} fusion(bf16[2880,640]{1,0:T(8,128)(2,1)} %own_ref.5, s32[]{:T(128)S(6)} %select_n.14), kind=kLoop, calls=%fused_computation.18 | loop fusion | bytes 3686404 | tf_op jit(solution)/shard_map/dynamic_slice | solution.py:489
  3.7 3.0 %collective-permute-start = (bf16[1440,640]{1,0:T(8,128)(2,1)}, bf16[1440,640]{1,0:T(8,128)(2,1)}, u32[]{:S(2)}, u32[]{:S(2)}) collective-permute-start(bf16[1440,640]{1,0:T(8,128)(2,1)} %constant_dynamic-slice_fusion.8), channel_id=1, source_target_pairs={{0,1},{1,0},{2,3},{3,2},{4,5},{5,4},{6,7},{7,6},{8,9},{9,8},{10,11... | collective-permute-start | bytes 5529608 | tf_op jit(solution)/shard_map/ppermute | solution.py:481
  6.7 0.9 pack.1
  7.6 5.9 %all-to-all-start = ((bf16[16,8,2880]{2,1,0:T(8,128)(2,1)}), bf16[16,8,2880]{2,1,0:T(8,128)(2,1)S(1)}, u32[]{:S(2)}, u32[]{:S(2)}) async-start(bf16[16,8,2880]{2,1,0:T(8,128)(2,1)} %bitcast.7), calls=%async_computation | async-start | bytes 1507328 | tf_op jit(solution)/shard_map/all_to_all | solution.py:519
  14.1 52.6 %norm_grad.1 = (bf16[15,4,1088,128]{3,2,1,0:T(8,128)(2,1)}, bf16[8,2,640,128]{3,2,1,0:T(8,128)(2,1)}, bf16[8,2,640,128]{3,2,1,0:T(8,128)(2,1)}, bf16[4,2,640,128]{3,2,1,0:T(8,128)(2,1)}, bf16[4,2,640,128]{3,2,1,0:T(8,128)(2,1)}) custom-call(s32[96]{0:T(128)} %constant.30.clone.table, s32[6]{0:T(128)} %stack.27.info, s32[16]{0:T(128)} %departing.3, ...), custom_call_target="tpu_custom_call" | custom-call | flops 32212254720 | bytes 26214400 | tf_op jit(solution)/shard_map/norm_grad/pallas_call | solution.py:194
  67.8 1.5 route.1
  69.2 5.7 %all-to-all-start.1 = ((bf16[16,8,2880]{2,1,0:T(8,128)(2,1)}), bf16[16,8,2880]{2,1,0:T(8,128)(2,1)S(1)}, u32[]{:S(2)}, u32[]{:S(2)}) async-start(bf16[16,8,2880]{2,1,0:T(8,128)(2,1)} %route.1), calls=%async_computation.1 | async-start | bytes 1507328 | tf_op jit(solution)/shard_map/all_to_all | solution.py:531
  75.0 4.4 %add_convert_fusion.4 = (bf16[2,2,640,128]{3,2,1,0:T(8,128)(2,1)S(1)}, bf16[2,2,640,128]{3,2,1,0:T(8,128)(2,1)}, bf16[2,2,640,128]{3,2,1,0:T(8,128)(2,1)}, bf16[2,2,640,128]{3,2,1,0:T(8,128)(2,1)}) fusion(bf16[8,2,640,128]{3,2,1,0:T(8,128)(2,1)} %collective-permute-done.2, bf16[8,2,640,128]{3,2,1,0:T(8,128)(2,1)} %get-tuple-element.47), kind=kLoop, calls=%fused_computation.4 | loop fusion | flops 5242880 | bytes 7864320 | tf_op jit(solution)/shard_map/convert_element_type | solution.py:508
  79.4 1.9 %collective-permute-start.3 = (bf16[2,2,640,128]{3,2,1,0:T(8,128)(2,1)}, bf16[2,2,640,128]{3,2,1,0:T(8,128)(2,1)S(1)}, u32[]{:S(2)}, u32[]{:S(2)}) collective-permute-start(bf16[2,2,640,128]{3,2,1,0:T(8,128)(2,1)} %get-tuple-element.85), channel_id=1, source_target_pairs={{0,5},{1,4},{2,7},{3,6},{4,1},{5,0},{6,3},{7,2},{8,13},{9,12},{10,... | collective-permute-start | bytes 1966088 | tf_op jit(solution)/shard_map/ppermute | solution.py:485
  81.3 1.5 collective-permute-start.4
  82.9 2.6 %add_convert_fusion.6 = (bf16[1,2,640,128]{3,2,1,0:T(8,128)(2,1)}, bf16[1,2,640,128]{3,2,1,0:T(8,128)(2,1)}, bf16[1,2,640,128]{3,2,1,0:T(8,128)(2,1)}, bf16[1,2,640,128]{3,2,1,0:T(8,128)(2,1)S(1)}) fusion(bf16[4,2,640,128]{3,2,1,0:T(8,128)(2,1)} %collective-permute-done.1, bf16[4,2,640,128]{3,2,1,0:T(8,128)(2,1)S(1)} %copy-done.6), kind=kLoop, calls=%fused_computation.6 | loop fusion | flops 2621440 | bytes 3932160 | tf_op jit(solution)/shard_map/convert_element_type | solution.py:508
  85.5 1.9 %collective-permute-start.9 = (bf16[1,2,640,128]{3,2,1,0:T(8,128)(2,1)}, bf16[1,2,640,128]{3,2,1,0:T(8,128)(2,1)S(1)}, u32[]{:S(2)}, u32[]{:S(2)}) collective-permute-start(bf16[1,2,640,128]{3,2,1,0:T(8,128)(2,1)} %get-tuple-element.90), channel_id=1, source_target_pairs={{0,5},{1,4},{2,7},{3,6},{4,1},{5,0},{6,3},{7,2},{8,13},{9,12},{10,... | collective-permute-start | bytes 983048 | tf_op jit(solution)/shard_map/ppermute | solution.py:485
  87.4 1.5 collective-permute-start.10
  88.9 23.3 %forward.3.refs_0_ = bf16[4,1024,640]{2,1,0:T(8,128)(2,1)} custom-call(s32[6]{0:T(128)} %stack.27.info, bf16[15,4,1088,128]{3,2,1,0:T(8,128)(2,1)} %get-tuple-element.50.slab_hbm, bf16[2880,640]{1,0:T(8,128)(2,1)} %own_ref.5, bf16[1440,640]{1,0:T(8,128)(2,1)} %collective-permute-done.near_ref, bf16[1440,640]{1,0:T(8,128)(2,1)} %collective-permute-done.6.far_ref), custom_call_target="tpu_custom_call" | custom-call | flops 15099494400 | bytes 15728640 | tf_op jit(solution)/shard_map/forward/pallas_call | solution.py:315
  112.4 0.7 copy-done.7
  113.0 0.8 copy-done.8
  113.9 1.5 collective-permute-done.5
  115.4 1.9 %add_convert_fusion = bf16[2,2,640,128]{3,2,1,0:T(8,128)(2,1)S(1)} fusion(bf16[2,2,640,128]{3,2,1,0:T(8,128)(2,1)} %collective-permute-done.5, bf16[2,2,640,128]{3,2,1,0:T(8,128)(2,1)} %copy-done.8, bf16[2,2,640,128]{3,2,1,0:T(8,128)(2,1)} %copy-done.7, bf16[2,2,640,128]{3,2,1,0:T(8,128)(2,1)S(1)} %get-tuple-element.49), kind=kLoop, calls=%fused_computation | loop fusion | flops 2621440 | bytes 3276800 | tf_op jit(solution)/shard_map/convert_element_type | solution.py:508
  117.3 0.8 constant_dynamic-slice_fusion.4
  118.1 2.5 %collective-permute-start.12 = (bf16[2,16,24,128]{3,2,1,0:T(8,128)(2,1)}, bf16[2,16,24,128]{3,2,1,0:T(8,128)(2,1)S(1)}, u32[]{:S(2)}, u32[]{:S(2)}) collective-permute-start(bf16[2,16,24,128]{3,2,1,0:T(8,128)(2,1)} %get-tuple-element.92), channel_id=1, source_target_pairs={{0,8},{2,10},{4,12},{6,14},{8,0},{10,2},{12,4},{14,6},{16,24},{18,... | collective-permute-start | bytes 589832 | tf_op jit(solution)/shard_map/ppermute | solution.py:478
  120.6 1.8 %collective-permute-start.7 = (bf16[2,16,24,128]{3,2,1,0:T(8,128)(2,1)}, bf16[2,16,24,128]{3,2,1,0:T(8,128)(2,1)S(1)}, u32[]{:S(2)}, u32[]{:S(2)}) collective-permute-start(bf16[2,16,24,128]{3,2,1,0:T(8,128)(2,1)} %get-tuple-element.94), channel_id=1, source_target_pairs={{0,24},{2,26},{4,28},{6,30},{8,16},{10,18},{12,20},{14,22},{16,8},... | collective-permute-start | bytes 589832 | tf_op jit(solution)/shard_map/ppermute | solution.py:478
  122.7 3.4 %collective-permute-start.8 = (bf16[2,16,24,128]{3,2,1,0:T(8,128)(2,1)S(1)}, bf16[2,16,24,128]{3,2,1,0:T(8,128)(2,1)S(1)}, u32[]{:S(2)}, u32[]{:S(2)}) collective-permute-start(bf16[2,16,24,128]{3,2,1,0:T(8,128)(2,1)S(1)} %get-tuple-element.93), channel_id=1, source_target_pairs={{0,16},{2,18},{4,20},{6,22},{8,24},{10,26},{12,28},{14,30},{16,0},... | collective-permute-start | bytes 589832 | tf_op jit(solution)/shard_map/ppermute | solution.py:478
  126.1 3.1 %collective-permute-done.11 = bf16[1,2,640,128]{3,2,1,0:T(8,128)(2,1)} collective-permute-done((bf16[1,2,640,128]{3,2,1,0:T(8,128)(2,1)}, bf16[1,2,640,128]{3,2,1,0:T(8,128)(2,1)}, u32[]{:S(2)}, u32[]{:S(2)}) %collective-permute-start.11) | collective-permute-done | bytes 327712 | tf_op jit(solution)/shard_map/ppermute | solution.py:478
  129.2 1.3 add_convert_fusion.5
  130.5 2.8 %collective-permute-start.13 = (bf16[1,16,24,128]{3,2,1,0:T(8,128)(2,1)S(1)}, bf16[1,16,24,128]{3,2,1,0:T(8,128)(2,1)S(1)}, u32[]{:S(2)}, u32[]{:S(2)}) collective-permute-start(bf16[1,16,24,128]{3,2,1,0:T(8,128)(2,1)S(1)} %get-tuple-element.98), channel_id=1, source_target_pairs={{0,24},{2,26},{4,28},{6,30},{8,16},{10,18},{12,20},{14,22},{16,8},... | collective-permute-start | bytes 294920 | tf_op jit(solution)/shard_map/ppermute | solution.py:478
  133.4 1.1 collective-permute-start.14
  135.0 14.2 %forward.4.refs_0_ = bf16[4,1024,640]{2,1,0:T(8,128)(2,1)} custom-call(s32[6]{0:T(128)} %stack.27.info, bf16[15,4,1088,128]{3,2,1,0:T(8,128)(2,1)} %get-tuple-element.50.slab_hbm, bf16[2880,640]{1,0:T(8,128)(2,1)} %own_ref.5, bf16[1440,640]{1,0:T(8,128)(2,1)} %collective-permute-done.near_ref, ...), custom_call_target="tpu_custom_call", output_to_operand_aliasing={{}: (5, {})} | custom-call | flops 7549747200 | bytes 11550720 | tf_op jit(solution)/shard_map/forward/pallas_call | solution.py:315
  149.3 1.6 choose.1
  150.9 5.2 %all-to-all-start.2 = ((bf16[16,2,3,24,128]{4,3,2,1,0:T(8,128)(2,1)}), bf16[16,2,3,24,128]{4,3,2,1,0:T(8,128)(2,1)S(1)}, u32[]{:S(2)}, u32[]{:S(2)}) async-start(bf16[16,2,3,24,128]{4,3,2,1,0:T(8,128)(2,1)} %choose.1), calls=%async_computation.2 | async-start | bytes 1179648 | tf_op jit(solution)/shard_map/all_to_all | solution.py:571
  156.2 14.4 %forward.5 = bf16[4,1024,640]{2,1,0:T(8,128)(2,1)} custom-call(s32[6]{0:T(128)} %stack.27.info, bf16[15,4,1088,128]{3,2,1,0:T(8,128)(2,1)} %get-tuple-element.50.slab_hbm, bf16[2880,640]{1,0:T(8,128)(2,1)} %own_ref.5, bf16[1440,640]{1,0:T(8,128)(2,1)} %collective-permute-done.near_ref, ...), custom_call_target="tpu_custom_call", output_to_operand_aliasing={{}: (5, {})} | custom-call | flops 7549747200 | bytes 11550720 | tf_op jit(solution)/shard_map/forward/pallas_call | solution.py:315
  170.6 1.1 all-to-all-done.2.grad_ref
  171.7 3.2 %update.1 = (f32[1,2,40,2880]{3,2,1,0:T(8,128)}, f32[1,2,40,2880]{3,2,1,0:T(8,128)}, f32[1,2,40,2880]{3,2,1,0:T(8,128)}) custom-call(s32[6]{0:T(128)S(1)} %copy-done.3, s32[16]{0:T(128)S(1)} %copy-done.5, bf16[16,2,3,24,128]{4,3,2,1,0:T(8,128)(2,1)S(1)} %all-to-all-done.2.grad_ref, f32[40,2880]{1,0:T(8,128)S(1)} %copy-done, f32[40,2880]{1,0:T(8,128)S(1)} %copy-done.1, ...), custom_call_target="tpu_custom_call" | custom-call | tf_op jit(solution)/shard_map/update/pallas_call | solution.py:441
  (40 shorter events, 2.8 us)
Async XLA Ops:
  0.6 6.0 %copy-start = (f32[40,2880]{1,0:T(8,128)S(1)}, f32[40,2880]{1,0:T(8,128)}, u32[]{:S(2)}) copy-start(f32[40,2880]{1,0:T(8,128)} %master_ref.3) | copy-start | bytes 1382404
  0.6 6.0 %copy-start.1 = (f32[40,2880]{1,0:T(8,128)S(1)}, f32[40,2880]{1,0:T(8,128)}, u32[]{:S(2)}) copy-start(f32[40,2880]{1,0:T(8,128)} %one_ref.3) | copy-start | bytes 1382404
  0.7 6.0 %copy-start.2 = (f32[40,2880]{1,0:T(8,128)S(1)}, f32[40,2880]{1,0:T(8,128)}, u32[]{:S(2)}) copy-start(f32[40,2880]{1,0:T(8,128)} %two_ref.3) | copy-start | bytes 1382404
  3.7 63.1 %collective-permute-start = (bf16[1440,640]{1,0:T(8,128)(2,1)}, bf16[1440,640]{1,0:T(8,128)(2,1)}, u32[]{:S(2)}, u32[]{:S(2)}) collective-permute-start(bf16[1440,640]{1,0:T(8,128)(2,1)} %constant_dynamic-slice_fusion.8), channel_id=1, source_target_pairs={{0,1},{1,0},{2,3},{3,2},{4,5},{5,4},{6,7},{7,6},{8,9},{9,8},{10,11... | collective-permute-start | bytes 5529608 | tf_op jit(solution)/shard_map/ppermute | solution.py:481
  7.6 59.2 %all-to-all-start = ((bf16[16,8,2880]{2,1,0:T(8,128)(2,1)}), bf16[16,8,2880]{2,1,0:T(8,128)(2,1)S(1)}, u32[]{:S(2)}, u32[]{:S(2)}) async-start(bf16[16,8,2880]{2,1,0:T(8,128)(2,1)} %bitcast.7), calls=%async_computation | async-start | bytes 1507328 | tf_op jit(solution)/shard_map/all_to_all | solution.py:519
  14.1 53.6 %copy-start.4 = (s32[16]{0:T(128)S(1)}, s32[16]{0:T(128)}, u32[]{:S(2)}) copy-start(s32[16]{0:T(128)} %partner.3) | copy-start | bytes 196
  66.8 8.2 %collective-permute-start.2 = (bf16[8,2,640,128]{3,2,1,0:T(8,128)(2,1)}, bf16[8,2,640,128]{3,2,1,0:T(8,128)(2,1)}, u32[]{:S(2)}, u32[]{:S(2)}) collective-permute-start(bf16[8,2,640,128]{3,2,1,0:T(8,128)(2,1)} %get-tuple-element.48), channel_id=1, source_target_pairs={{0,2},{2,0},{4,6},{6,4},{8,10},{10,8},{12,14},{14,12},{16,18},{18,... | collective-permute-start | bytes 7864328 | tf_op jit(solution)/shard_map/ppermute | solution.py:478
  67.2 18.3 %collective-permute-start.6 = (bf16[1440,640]{1,0:T(8,128)(2,1)}, bf16[1440,640]{1,0:T(8,128)(2,1)}, u32[]{:S(2)}, u32[]{:S(2)}) collective-permute-start(bf16[1440,640]{1,0:T(8,128)(2,1)} %collective-permute-done.near_ref), channel_id=1, source_target_pairs={{0,2},{2,0},{4,6},{6,4},{8,10},{10,8},{12,14},{14,12},{16,18},{18,... | collective-permute-start | bytes 5529608 | tf_op jit(solution)/shard_map/ppermute | solution.py:478
  67.4 15.5 %collective-permute-start.1 = (bf16[4,2,640,128]{3,2,1,0:T(8,128)(2,1)}, bf16[4,2,640,128]{3,2,1,0:T(8,128)(2,1)}, u32[]{:S(2)}, u32[]{:S(2)}) collective-permute-start(bf16[4,2,640,128]{3,2,1,0:T(8,128)(2,1)} %get-tuple-element.46), channel_id=1, source_target_pairs={{0,2},{2,0},{4,6},{6,4},{8,10},{10,8},{12,14},{14,12},{16,18},{18,... | collective-permute-start | bytes 3932168 | tf_op jit(solution)/shard_map/ppermute | solution.py:478
  69.2 46.1 %all-to-all-start.1 = ((bf16[16,8,2880]{2,1,0:T(8,128)(2,1)}), bf16[16,8,2880]{2,1,0:T(8,128)(2,1)S(1)}, u32[]{:S(2)}, u32[]{:S(2)}) async-start(bf16[16,8,2880]{2,1,0:T(8,128)(2,1)} %route.1), calls=%async_computation.1 | async-start | bytes 1507328 | tf_op jit(solution)/shard_map/all_to_all | solution.py:531
  75.0 7.9 %copy-start.6 = (bf16[4,2,640,128]{3,2,1,0:T(8,128)(2,1)S(1)}, bf16[4,2,640,128]{3,2,1,0:T(8,128)(2,1)}, u32[]{:S(2)}) copy-start(bf16[4,2,640,128]{3,2,1,0:T(8,128)(2,1)} %get-tuple-element.52) | copy-start | bytes 3932164
  79.4 32.8 %collective-permute-start.3 = (bf16[2,2,640,128]{3,2,1,0:T(8,128)(2,1)}, bf16[2,2,640,128]{3,2,1,0:T(8,128)(2,1)S(1)}, u32[]{:S(2)}, u32[]{:S(2)}) collective-permute-start(bf16[2,2,640,128]{3,2,1,0:T(8,128)(2,1)} %get-tuple-element.85), channel_id=1, source_target_pairs={{0,5},{1,4},{2,7},{3,6},{4,1},{5,0},{6,3},{7,2},{8,13},{9,12},{10,... | collective-permute-start | bytes 1966088 | tf_op jit(solution)/shard_map/ppermute | solution.py:485
  81.3 31.1 %collective-permute-start.4 = (bf16[2,2,640,128]{3,2,1,0:T(8,128)(2,1)}, bf16[2,2,640,128]{3,2,1,0:T(8,128)(2,1)S(1)}, u32[]{:S(2)}, u32[]{:S(2)}) collective-permute-start(bf16[2,2,640,128]{3,2,1,0:T(8,128)(2,1)} %get-tuple-element.86), channel_id=1, source_target_pairs={{0,1},{1,0},{2,3},{3,2},{4,5},{5,4},{6,7},{7,6},{8,9},{9,8},{10,11... | collective-permute-start | bytes 1966088 | tf_op jit(solution)/shard_map/ppermute | solution.py:481
  82.8 32.6 %collective-permute-start.5 = (bf16[2,2,640,128]{3,2,1,0:T(8,128)(2,1)}, bf16[2,2,640,128]{3,2,1,0:T(8,128)(2,1)}, u32[]{:S(2)}, u32[]{:S(2)}) collective-permute-start(bf16[2,2,640,128]{3,2,1,0:T(8,128)(2,1)} %get-tuple-element.87), channel_id=1, source_target_pairs={{0,4},{2,6},{4,0},{6,2},{8,12},{10,14},{12,8},{14,10},{16,20},{18,... | collective-permute-start | bytes 1966088 | tf_op jit(solution)/shard_map/ppermute | solution.py:478
  85.5 37.2 %collective-permute-start.9 = (bf16[1,2,640,128]{3,2,1,0:T(8,128)(2,1)}, bf16[1,2,640,128]{3,2,1,0:T(8,128)(2,1)S(1)}, u32[]{:S(2)}, u32[]{:S(2)}) collective-permute-start(bf16[1,2,640,128]{3,2,1,0:T(8,128)(2,1)} %get-tuple-element.90), channel_id=1, source_target_pairs={{0,5},{1,4},{2,7},{3,6},{4,1},{5,0},{6,3},{7,2},{8,13},{9,12},{10,... | collective-permute-start | bytes 983048 | tf_op jit(solution)/shard_map/ppermute | solution.py:485
  87.4 38.7 %collective-permute-start.10 = (bf16[1,2,640,128]{3,2,1,0:T(8,128)(2,1)}, bf16[1,2,640,128]{3,2,1,0:T(8,128)(2,1)}, u32[]{:S(2)}, u32[]{:S(2)}) collective-permute-start(bf16[1,2,640,128]{3,2,1,0:T(8,128)(2,1)} %get-tuple-element.89), channel_id=1, source_target_pairs={{0,1},{1,0},{2,3},{3,2},{4,5},{5,4},{6,7},{7,6},{8,9},{9,8},{10,11... | collective-permute-start | bytes 983048 | tf_op jit(solution)/shard_map/ppermute | solution.py:481
  112.2 0.8 copy-start.7
  112.2 17.0 %collective-permute-start.11 = (bf16[1,2,640,128]{3,2,1,0:T(8,128)(2,1)}, bf16[1,2,640,128]{3,2,1,0:T(8,128)(2,1)}, u32[]{:S(2)}, u32[]{:S(2)}) collective-permute-start(bf16[1,2,640,128]{3,2,1,0:T(8,128)(2,1)} %get-tuple-element.88), channel_id=1, source_target_pairs={{0,4},{2,6},{4,0},{6,2},{8,12},{10,14},{12,8},{14,10},{16,20},{18,... | collective-permute-start | bytes 983048 | tf_op jit(solution)/shard_map/ppermute | solution.py:478
  113.0 0.8 copy-start.8
  118.1 11.1 %collective-permute-start.12 = (bf16[2,16,24,128]{3,2,1,0:T(8,128)(2,1)}, bf16[2,16,24,128]{3,2,1,0:T(8,128)(2,1)S(1)}, u32[]{:S(2)}, u32[]{:S(2)}) collective-permute-start(bf16[2,16,24,128]{3,2,1,0:T(8,128)(2,1)} %get-tuple-element.92), channel_id=1, source_target_pairs={{0,8},{2,10},{4,12},{6,14},{8,0},{10,2},{12,4},{14,6},{16,24},{18,... | collective-permute-start | bytes 589832 | tf_op jit(solution)/shard_map/ppermute | solution.py:478
  120.6 28.7 %collective-permute-start.7 = (bf16[2,16,24,128]{3,2,1,0:T(8,128)(2,1)}, bf16[2,16,24,128]{3,2,1,0:T(8,128)(2,1)S(1)}, u32[]{:S(2)}, u32[]{:S(2)}) collective-permute-start(bf16[2,16,24,128]{3,2,1,0:T(8,128)(2,1)} %get-tuple-element.94), channel_id=1, source_target_pairs={{0,24},{2,26},{4,28},{6,30},{8,16},{10,18},{12,20},{14,22},{16,8},... | collective-permute-start | bytes 589832 | tf_op jit(solution)/shard_map/ppermute | solution.py:478
  122.7 26.5 %collective-permute-start.8 = (bf16[2,16,24,128]{3,2,1,0:T(8,128)(2,1)S(1)}, bf16[2,16,24,128]{3,2,1,0:T(8,128)(2,1)S(1)}, u32[]{:S(2)}, u32[]{:S(2)}) collective-permute-start(bf16[2,16,24,128]{3,2,1,0:T(8,128)(2,1)S(1)} %get-tuple-element.93), channel_id=1, source_target_pairs={{0,16},{2,18},{4,20},{6,22},{8,24},{10,26},{12,28},{14,30},{16,0},... | collective-permute-start | bytes 589832 | tf_op jit(solution)/shard_map/ppermute | solution.py:478
  130.5 18.7 %collective-permute-start.13 = (bf16[1,16,24,128]{3,2,1,0:T(8,128)(2,1)S(1)}, bf16[1,16,24,128]{3,2,1,0:T(8,128)(2,1)S(1)}, u32[]{:S(2)}, u32[]{:S(2)}) collective-permute-start(bf16[1,16,24,128]{3,2,1,0:T(8,128)(2,1)S(1)} %get-tuple-element.98), channel_id=1, source_target_pairs={{0,24},{2,26},{4,28},{6,30},{8,16},{10,18},{12,20},{14,22},{16,8},... | collective-permute-start | bytes 294920 | tf_op jit(solution)/shard_map/ppermute | solution.py:478
  133.4 15.9 %collective-permute-start.14 = (bf16[1,16,24,128]{3,2,1,0:T(8,128)(2,1)S(1)}, bf16[1,16,24,128]{3,2,1,0:T(8,128)(2,1)S(1)}, u32[]{:S(2)}, u32[]{:S(2)}) collective-permute-start(bf16[1,16,24,128]{3,2,1,0:T(8,128)(2,1)S(1)} %get-tuple-element.97), channel_id=1, source_target_pairs={{0,16},{2,18},{4,20},{6,22},{8,24},{10,26},{12,28},{14,30},{16,0},... | collective-permute-start | bytes 294920 | tf_op jit(solution)/shard_map/ppermute | solution.py:478
  134.4 14.8 %collective-permute-start.15 = (bf16[1,16,24,128]{3,2,1,0:T(8,128)(2,1)S(1)}, bf16[1,16,24,128]{3,2,1,0:T(8,128)(2,1)S(1)}, u32[]{:S(2)}, u32[]{:S(2)}) collective-permute-start(bf16[1,16,24,128]{3,2,1,0:T(8,128)(2,1)S(1)} %get-tuple-element.96), channel_id=1, source_target_pairs={{0,8},{2,10},{4,12},{6,14},{8,0},{10,2},{12,4},{14,6},{16,24},{18,... | collective-permute-start | bytes 294920 | tf_op jit(solution)/shard_map/ppermute | solution.py:478
  150.9 20.8 %all-to-all-start.2 = ((bf16[16,2,3,24,128]{4,3,2,1,0:T(8,128)(2,1)}), bf16[16,2,3,24,128]{4,3,2,1,0:T(8,128)(2,1)S(1)}, u32[]{:S(2)}, u32[]{:S(2)}) async-start(bf16[16,2,3,24,128]{4,3,2,1,0:T(8,128)(2,1)} %choose.1), calls=%async_computation.2 | async-start | bytes 1179648 | tf_op jit(solution)/shard_map/all_to_all | solution.py:571
  156.2 15.5 %copy-start.3 = (s32[6]{0:T(128)S(1)}, s32[6]{0:T(128)}, u32[]{:S(2)}) copy-start(s32[6]{0:T(128)} %stack.27.info) | copy-start | bytes 76
  156.2 15.5 %copy-start.5 = (s32[16]{0:T(128)S(1)}, s32[16]{0:T(128)}, u32[]{:S(2)}) copy-start(s32[16]{0:T(128)} %departing.3) | copy-start | bytes 196
